TPU v7x, 256 devices: a whole 4x4x8 slice. The times are simulated.
256 devices in a mesh: ctx: 64 (over y_lo, z, x), dp: 4 (over y_hi, core).
Axes of the slice: x: 4, y: 4 (y_hi: 2, y_lo: 2; y = y_hi * 2 + y_lo), z: 8, core: 2. Of those that a mesh axis runs over, the one named last changes fastest.
Arguments:
- frames_fwd: int32 [16384], P('ctx'), may hold values from 0 to 1023, never falling along the last dimension, each value on 1 to 64 neighbouring positions
- query_fwd: bfloat16 [16384, 2048], P('ctx', 'dp'), may hold values from -20 to 20
- keys_fwd: bfloat16 [16384, 2048], P('ctx', 'dp'), may hold values from -20 to 20
- values_fwd: bfloat16 [16384, 2048], P('ctx', 'dp'), may hold values from -6 to 6
- frames_bwd: int32 [16384], P('ctx'), may hold values from 0 to 1023, never falling along the last dimension, each value on 1 to 64 neighbouring positions
- query_bwd: bfloat16 [16384, 2048], P('ctx', 'dp'), may hold values from -6 to 6
- keys_bwd: bfloat16 [16384, 2048], P('ctx', 'dp'), may hold values from -6 to 6
- values_bwd: bfloat16 [16384, 2048], P('ctx', 'dp'), may hold values from -6 to 6
- attn_bwd: bfloat16 [16384, 2048], P('ctx', 'dp'), may hold values from -4 to 4
- logsumexp_bwd: float32 [16, 16384], P('dp', 'ctx'), may hold values from 4 to 6.5
- cotangent: bfloat16 [16384, 2048], P('ctx', 'dp'), may hold values from -6 to 6
- out_weight: bfloat16 [2048, 2048], P('dp'), may hold values from -0.125 to 0.125
Outputs:
- attended: bfloat16 [16384, 2048], P('ctx', 'dp')
- attended_logsumexp: float32 [16, 16384], P('dp', 'ctx')
- grad_query: float32 [16384, 2048], P('ctx', 'dp')
- grad_keys: float32 [16384, 2048], P('ctx', 'dp')
- grad_values: float32 [16384, 2048], P('ctx', 'dp')
- grad_weight: bfloat16 [2048, 2048], P('dp')
Inputs may be any that keep to these rules, and one draw needn't show every extreme that they name: `frames_fwd`: frame ids never fall along the sequence; each frame spans 1 to 64 consecutive tokens and one spans exactly 64. `frames_bwd`: frame ids never fall along the sequence; each frame spans 1 to 64 consecutive tokens and one spans exactly 64.
All inputs are finite; a program needn't handle non-finite values.
Results may differ from a plain program's by a relative error of at most 0.0087.
Values may be sent and summed in bfloat16 or wider, within the bound.
No kernel may reach another device: no remote copies, remote signals or barrier semaphores. Data moves between devices by JAX's collectives and lax.ppermute only.
A program may use at most 64 MiB of HBM per device.

v0:
```python
import math

import jax
import jax.numpy as jnp
from jax import lax
from jax.sharding import PartitionSpec as P

HDIM = 128
REACH = 4


def from_behind(value, axis, steps):
    count = lax.axis_size(axis)
    first, last = (max(0, -steps), min(count, count - steps))
    return lax.ppermute(value, axis, [(source, source + steps) for source in range(first, last)])


def shifted(block, axis, distance):
    devices = range(lax.axis_size(axis))
    route = [((i - distance) % len(devices), i) for i in devices]
    return lax.ppermute(block, axis, route)


def split_heads(matrix):
    return matrix.reshape(matrix.shape[0], -1, HDIM)


def block_scores(query_heads, key_heads):
    return jnp.einsum(
        "qhd,khd->hqk", query_heads, key_heads, preferred_element_type=jnp.float32
    ) * (1.0 / math.sqrt(HDIM))


def forward_window(queries, key_block, value_block, frames):
    ctx_index = lax.axis_index("ctx")
    tokens_here = queries.shape[0]
    query_heads = split_heads(queries)
    heads_here = query_heads.shape[1]
    running_max = jnp.full((heads_here, tokens_here), -jnp.inf, jnp.float32)
    running_sum = jnp.zeros((heads_here, tokens_here), jnp.float32)
    accumulated = jnp.zeros((heads_here, tokens_here, HDIM), jnp.float32)
    own_visible = (frames[None, :] <= frames[:, None])[None]
    for cycle_step in range(REACH):
        if cycle_step > 0:
            key_block, value_block = from_behind((key_block, value_block), "ctx", 1)
            visible = ctx_index >= cycle_step
        else:
            visible = own_visible
        scores = jnp.where(visible, block_scores(query_heads, split_heads(key_block)), -jnp.inf)
        fresh_max = jnp.maximum(running_max, scores.max(-1))
        carried = jnp.exp(running_max - fresh_max)
        weights = jnp.exp(scores - fresh_max[:, :, None])
        running_sum = running_sum * carried + weights.sum(-1)
        accumulated = accumulated * carried[:, :, None] + jnp.einsum(
            "hqk,khd->hqd",
            weights.astype(jnp.bfloat16),
            split_heads(value_block),
            preferred_element_type=jnp.float32,
        )
        running_max = fresh_max
    attended = (accumulated / running_sum[:, :, None]).transpose(1, 0, 2).reshape(tokens_here, -1)
    return (attended.astype(jnp.bfloat16), running_max + jnp.log(running_sum))


def backward_window(queries, key_block, value_block, attn_rows, log_total, grad_attn, frames):
    ctx_index = lax.axis_index("ctx")
    tokens_here = queries.shape[0]
    softmax_scale = 1.0 / math.sqrt(HDIM)
    query_heads = split_heads(queries)
    heads_here = query_heads.shape[1]
    grad_heads = split_heads(grad_attn)
    row_delta = jnp.sum(
        grad_heads.astype(jnp.float32) * split_heads(attn_rows).astype(jnp.float32), -1
    ).T
    grad_query = jnp.zeros((tokens_here, heads_here, HDIM), jnp.float32)
    grad_keys = jnp.zeros((tokens_here, heads_here, HDIM), jnp.float32)
    grad_values = jnp.zeros((tokens_here, heads_here, HDIM), jnp.float32)
    own_visible = (frames[None, :] <= frames[:, None])[None]
    for cycle_step in range(REACH):
        if cycle_step > 0:
            key_block, value_block = from_behind((key_block, value_block), "ctx", 1)
            grad_keys, grad_values = (
                shifted(grad_keys.astype(jnp.bfloat16), "ctx", 1).astype(grad_keys.dtype),
                shifted(grad_values.astype(jnp.bfloat16), "ctx", 1).astype(grad_values.dtype),
            )
            visible = ctx_index >= cycle_step
        else:
            visible = own_visible
        key_heads = split_heads(key_block)
        value_heads = split_heads(value_block)
        weights = jnp.where(
            visible, jnp.exp(block_scores(query_heads, key_heads) - log_total[:, :, None]), 0.0
        )
        grad_values = grad_values + jnp.einsum(
            "hqk,qhd->khd",
            weights.astype(jnp.bfloat16),
            grad_heads,
            preferred_element_type=jnp.float32,
        )
        grad_weights = jnp.einsum(
            "qhd,khd->hqk", grad_heads, value_heads, preferred_element_type=jnp.float32
        )
        grad_scores = (weights * (grad_weights - row_delta[:, :, None])).astype(jnp.bfloat16)
        grad_query = (
            grad_query
            + jnp.einsum("hqk,khd->qhd", grad_scores, key_heads, preferred_element_type=jnp.float32)
            * softmax_scale
        )
        grad_keys = (
            grad_keys
            + jnp.einsum(
                "hqk,qhd->khd", grad_scores, query_heads, preferred_element_type=jnp.float32
            )
            * softmax_scale
        )
    return (
        grad_query.reshape(tokens_here, -1),
        grad_keys.reshape(tokens_here, -1),
        grad_values.reshape(tokens_here, -1),
    )


def body(
    frames_fwd,
    query_fwd,
    keys_fwd,
    values_fwd,
    frames_bwd,
    query_bwd,
    keys_bwd,
    values_bwd,
    attn_bwd,
    logsumexp_bwd,
    cotangent,
    out_weight,
):
    attended, log_total = forward_window(query_fwd, keys_fwd, values_fwd, frames_fwd)
    full_cols = lax.all_gather(cotangent, "dp", axis=1, tiled=True)
    grad_attn = jnp.einsum(
        "tc,rc->tr", full_cols, out_weight, preferred_element_type=jnp.float32
    ).astype(jnp.bfloat16)
    weight_term = jnp.einsum("tr,tc->rc", attn_bwd, full_cols, preferred_element_type=jnp.float32)
    grad_weight = lax.psum(weight_term, "ctx").astype(jnp.bfloat16)
    grad_query, grad_keys, grad_values = backward_window(
        query_bwd, keys_bwd, values_bwd, attn_bwd, logsumexp_bwd, grad_attn, frames_bwd
    )
    return (attended, log_total, grad_query, grad_keys, grad_values, grad_weight)


def solution(mesh):
    in_specs = (
        P("ctx"),
        P("ctx", "dp"),
        P("ctx", "dp"),
        P("ctx", "dp"),
        P("ctx"),
        P("ctx", "dp"),
        P("ctx", "dp"),
        P("ctx", "dp"),
        P("ctx", "dp"),
        P("dp", "ctx"),
        P("ctx", "dp"),
        P("dp", None),
    )
    out_specs = (
        P("ctx", "dp"),
        P("dp", "ctx"),
        P("ctx", "dp"),
        P("ctx", "dp"),
        P("ctx", "dp"),
        P("dp", None),
    )
    return jax.shard_map(body, mesh=mesh, in_specs=in_specs, out_specs=out_specs, check_vma=False)
```

profile of v0, /device:TPU:24, one launch (start us, length us, event | category | flops | bytes accessed | tf_op | source)
XLA Modules:
  0.0 528.0 jit_solution(13887138169669877200)
XLA Ops:
  8.0 1.8 copy.175
  9.8 3.4 collective-permute-start.7
  13.2 1.8 copy.149
  15.0 3.5 collective-permute-start
  19.6 3.1 collective-permute-start.6
  22.7 3.7 collective-permute-start.1
  26.5 1.8 copy.247
  29.7 1.4 fusion.15
  31.1 1.3 fusion.82
  32.3 11.2 %collective-permute-done.1 = bf16[256,512]{1,0:T(8,128)(2,1)} collective-permute-done((bf16[256,512]{1,0:T(8,128)(2,1)}, bf16[256,512]{1,0:T(8,128)(2,1)}, u32[]{:S(2)}, u32[]{:S(2)}) %collective-permute-start.1) | collective-permute-done | bytes 262176 | tf_op jit(solution)/shard_map/ppermute | solution.py:15
  43.5 1.8 copy.152
  45.3 1.9 collective-permute-start.3
  47.2 1.9 collective-permute-start.9
  49.2 1.9 collective-permute-start.8
  51.1 2.4 fusion.12
  53.4 3.4 collective-permute-start.2
  56.8 1.4 fusion.85
  58.2 2.7 collective-permute-done.3
  60.9 1.8 copy.156
  62.7 2.0 collective-permute-start.5
  64.8 1.8 collective-permute-done.9
  66.6 1.9 collective-permute-start.11
  68.5 3.7 collective-permute-done.8
  72.2 1.9 collective-permute-start.10
  74.1 2.4 fusion.8
  76.5 1.3 collective-permute-done.2
  77.8 1.9 collective-permute-start.4
  79.7 1.4 fusion.84
  81.1 17.2 %collective-permute-done.4 = bf16[256,512]{0,1:T(8,128)(2,1)S(1)} collective-permute-done((bf16[256,512]{0,1:T(8,128)(2,1)}, bf16[256,512]{0,1:T(8,128)(2,1)S(1)}, u32[]{:S(2)}, u32[]{:S(2)}) %collective-permute-start.4) | collective-permute-done | bytes 262176 | tf_op jit(solution)/shard_map/ppermute | solution.py:15
  99.7 1.8 copy.160
  101.5 1.7 fusion.25
  103.3 1.4 fusion.27
  106.8 2.3 fusion.4
  109.2 2.0 convolution_convert_fusion.1
  111.9 2.3 fusion.38
  114.2 1.6 fusion.23
  118.0 2.1 fusion.21
  122.3 1.3 fusion.22
  123.6 2.7 fusion.86
  126.2 360.1 %all-reduce.1 = bf16[512,2048]{1,0:T(8,128)(2,1)} all-reduce(f32[512,2048]{1,0:T(8,128)} %fusion.86), channel_id=1, replica_groups=mesh['ctx'=64,'dp'=4] {'ctx'}, use_global_device_ids=true, to_apply=%region_9.10 | all-reduce | flops 1048576 | bytes 6291456 | tf_op jit(solution)/shard_map/psum | solution.py:143
  486.3 1.7 fusion.20
  489.3 1.3 convolution_add_fusion.1
  490.6 2.0 fusion.32
  494.7 9.8 %collective-permute-done.13 = bf16[256,4,128]{0,2,1:T(8,128)(2,1)S(1)} collective-permute-done((bf16[256,4,128]{0,2,1:T(8,128)(2,1)S(1)}, bf16[256,4,128]{0,2,1:T(8,128)(2,1)S(1)}, u32[]{:S(2)}, u32[]{:S(2)}) %collective-permute-start.13) | collective-permute-done | bytes 262176 | tf_op jit(solution)/shard_map/ppermute | solution.py:21
  504.6 2.7 collective-permute-done.16
  509.2 2.0 copy.211
  511.2 4.0 collective-permute-done.14
  517.3 1.6 collective-permute-done.17
  (104 shorter events, 21.1 us)
Async XLA Ops:
  7.2 102.0 %copy-start = (bf16[512,2048]{1,0:T(8,128)(2,1)S(1)}, bf16[512,2048]{1,0:T(8,128)(2,1)}, u32[]{:S(2)}) copy-start(bf16[512,2048]{1,0:T(8,128)(2,1)} %param.23) | copy-start | bytes 6291460
  7.2 21.1 %copy-start.24 = (s32[256]{0:T(256)S(1)}, s32[256]{0:T(256)}, u32[]{:S(2)}) copy-start(s32[256]{0:T(256)} %param.12) | copy-start | bytes 3076
  7.2 21.2 %copy-start.25 = (s32[256]{0:T(256)S(1)}, s32[256]{0:T(256)}, u32[]{:S(2)}) copy-start(s32[256]{0:T(256)} %param.16) | copy-start | bytes 3076
  7.2 21.3 %copy-start.21 = (bf16[256,512]{1,0:T(8,128)(2,1)S(1)}, bf16[256,512]{1,0:T(8,128)(2,1)}, u32[]{:S(2)}) copy-start(bf16[256,512]{1,0:T(8,128)(2,1)} %param.17) | copy-start | bytes 786436
  7.2 21.5 %copy-start.15 = (bf16[256,512]{1,0:T(8,128)(2,1)S(1)}, bf16[256,512]{1,0:T(8,128)(2,1)}, u32[]{:S(2)}) copy-start(bf16[256,512]{1,0:T(8,128)(2,1)} %param.20) | copy-start | bytes 786436
  7.2 22.4 %copy-start.26 = (f32[4,256]{1,0:T(4,128)S(1)}, f32[4,256]{1,0:T(4,128)}, u32[]{:S(2)}) copy-start(f32[4,256]{1,0:T(4,128)} %param.21) | copy-start | bytes 12292
  7.2 101.9 %all-gather.2.cloned.1.call-start = ((), (), s32[]{:S(2)}) async-start(), calls=%async_computation | async-start | bytes 1310720 | tf_op jit(solution)/shard_map/all_gather | solution.py:138
  9.8 37.4 %collective-permute-start.7 = (bf16[256,512]{0,1:T(8,128)(2,1)}, bf16[256,512]{0,1:T(8,128)(2,1)}, u32[]{:S(2)}, u32[]{:S(2)}) collective-permute-start(bf16[256,512]{0,1:T(8,128)(2,1)} %copy.175), channel_id=1, source_target_pairs={{0,4},{4,8},{8,12},{12,16},{16,20},{20,24},{24,28},{28,32},{32,36}... | collective-permute-start | bytes 786440 | tf_op jit(solution)/shard_map/ppermute | solution.py:15
  15.0 16.1 %copy-start.10 = (bf16[256,512]{1,0:T(8,128)(2,1)S(1)}, bf16[256,512]{1,0:T(8,128)(2,1)}, u32[]{:S(2)}) copy-start(bf16[256,512]{1,0:T(8,128)(2,1)} %param.13) | copy-start | bytes 786436
  15.0 38.5 %collective-permute-start = (bf16[256,512]{0,1:T(8,128)(2,1)}, bf16[256,512]{0,1:T(8,128)(2,1)}, u32[]{:S(2)}, u32[]{:S(2)}) collective-permute-start(bf16[256,512]{0,1:T(8,128)(2,1)} %copy.149), channel_id=1, source_target_pairs={{0,4},{4,8},{8,12},{12,16},{16,20},{20,24},{24,28},{28,32},{32,36}... | collective-permute-start | bytes 786440 | tf_op jit(solution)/shard_map/ppermute | solution.py:15
  19.6 12.7 %copy-start.17 = (bf16[256,512]{0,1:T(8,128)(2,1)}, bf16[256,512]{0,1:T(8,128)(2,1)S(1)}, u32[]{:S(2)}) copy-start(bf16[256,512]{0,1:T(8,128)(2,1)S(1)} %copy.248) | copy-start | bytes 786436
  19.6 29.5 %collective-permute-start.6 = (bf16[256,512]{0,1:T(8,128)(2,1)S(1)}, bf16[256,512]{0,1:T(8,128)(2,1)}, u32[]{:S(2)}, u32[]{:S(2)}) collective-permute-start(bf16[256,512]{0,1:T(8,128)(2,1)S(1)} %copy.248), channel_id=1, source_target_pairs={{0,4},{4,8},{8,12},{12,16},{16,20},{20,24},{24,28},{28,32},{32,36}... | collective-permute-start | bytes 786440 | tf_op jit(solution)/shard_map/ppermute | solution.py:15
  22.7 20.8 %collective-permute-start.1 = (bf16[256,512]{1,0:T(8,128)(2,1)}, bf16[256,512]{1,0:T(8,128)(2,1)}, u32[]{:S(2)}, u32[]{:S(2)}) collective-permute-start(bf16[256,512]{1,0:T(8,128)(2,1)} %param.15), channel_id=1, source_target_pairs={{0,4},{4,8},{8,12},{12,16},{16,20},{20,24},{24,28},{28,32},{32,36}... | collective-permute-start | bytes 786440 | tf_op jit(solution)/shard_map/ppermute | solution.py:15
  28.7 2.4 copy-start.22
  45.3 15.7 %collective-permute-start.3 = (bf16[256,512]{1,0:T(8,128)(2,1)}, bf16[256,512]{1,0:T(8,128)(2,1)}, u32[]{:S(2)}, u32[]{:S(2)}) collective-permute-start(bf16[256,512]{1,0:T(8,128)(2,1)} %collective-permute-done.1), channel_id=1, source_target_pairs={{0,4},{4,8},{8,12},{12,16},{16,20},{20,24},{24,28},{28,32},{32,36}... | collective-permute-start | bytes 786440 | tf_op jit(solution)/shard_map/ppermute | solution.py:15
  47.2 19.3 %collective-permute-start.9 = (bf16[256,512]{0,1:T(8,128)(2,1)}, bf16[256,512]{0,1:T(8,128)(2,1)}, u32[]{:S(2)}, u32[]{:S(2)}) collective-permute-start(bf16[256,512]{0,1:T(8,128)(2,1)} %collective-permute-done.7), channel_id=1, source_target_pairs={{0,4},{4,8},{8,12},{12,16},{16,20},{20,24},{24,28},{28,32},{32,36}... | collective-permute-start | bytes 786440 | tf_op jit(solution)/shard_map/ppermute | solution.py:15
  49.2 23.0 %collective-permute-start.8 = (bf16[256,512]{0,1:T(8,128)(2,1)}, bf16[256,512]{0,1:T(8,128)(2,1)}, u32[]{:S(2)}, u32[]{:S(2)}) collective-permute-start(bf16[256,512]{0,1:T(8,128)(2,1)} %collective-permute-done.6), channel_id=1, source_target_pairs={{0,4},{4,8},{8,12},{12,16},{16,20},{20,24},{24,28},{28,32},{32,36}... | collective-permute-start | bytes 786440 | tf_op jit(solution)/shard_map/ppermute | solution.py:15
  53.4 24.4 %collective-permute-start.2 = (bf16[256,512]{0,1:T(8,128)(2,1)}, bf16[256,512]{0,1:T(8,128)(2,1)}, u32[]{:S(2)}, u32[]{:S(2)}) collective-permute-start(bf16[256,512]{0,1:T(8,128)(2,1)} %collective-permute-done), channel_id=1, source_target_pairs={{0,4},{4,8},{8,12},{12,16},{16,20},{20,24},{24,28},{28,32},{32,36}... | collective-permute-start | bytes 786440 | tf_op jit(solution)/shard_map/ppermute | solution.py:15
  62.7 35.6 %copy-start.11 = (bf16[256,512]{1,0:T(8,128)(2,1)S(1)}, bf16[256,512]{1,0:T(8,128)(2,1)}, u32[]{:S(2)}) copy-start(bf16[256,512]{1,0:T(8,128)(2,1)} %param.13) | copy-start | bytes 786436
  62.7 36.9 %collective-permute-start.5 = (bf16[256,512]{1,0:T(8,128)(2,1)}, bf16[256,512]{1,0:T(8,128)(2,1)}, u32[]{:S(2)}, u32[]{:S(2)}) collective-permute-start(bf16[256,512]{1,0:T(8,128)(2,1)} %collective-permute-done.3), channel_id=1, source_target_pairs={{0,4},{4,8},{8,12},{12,16},{16,20},{20,24},{24,28},{28,32},{32,36}... | collective-permute-start | bytes 786440 | tf_op jit(solution)/shard_map/ppermute | solution.py:15
  66.6 55.7 %collective-permute-start.11 = (bf16[256,512]{0,1:T(8,128)(2,1)}, bf16[256,512]{0,1:T(8,128)(2,1)}, u32[]{:S(2)}, u32[]{:S(2)}) collective-permute-start(bf16[256,512]{0,1:T(8,128)(2,1)} %collective-permute-done.9), channel_id=1, source_target_pairs={{0,4},{4,8},{8,12},{12,16},{16,20},{20,24},{24,28},{28,32},{32,36}... | collective-permute-start | bytes 786440 | tf_op jit(solution)/shard_map/ppermute | solution.py:15
  72.2 34.7 %collective-permute-start.10 = (bf16[256,512]{0,1:T(8,128)(2,1)}, bf16[256,512]{0,1:T(8,128)(2,1)}, u32[]{:S(2)}, u32[]{:S(2)}) collective-permute-start(bf16[256,512]{0,1:T(8,128)(2,1)} %collective-permute-done.8), channel_id=1, source_target_pairs={{0,4},{4,8},{8,12},{12,16},{16,20},{20,24},{24,28},{28,32},{32,36}... | collective-permute-start | bytes 786440 | tf_op jit(solution)/shard_map/ppermute | solution.py:15
  74.1 24.6 %copy-start.5 = (f32[4,256,256]{1,2,0:T(8,128)S(1)}, f32[4,256,256]{1,2,0:T(8,128)}, u32[]{:S(2)}) copy-start(f32[4,256,256]{1,2,0:T(8,128)} %get-tuple-element.33) | copy-start | bytes 3145732
  77.8 20.5 %collective-permute-start.4 = (bf16[256,512]{0,1:T(8,128)(2,1)}, bf16[256,512]{0,1:T(8,128)(2,1)S(1)}, u32[]{:S(2)}, u32[]{:S(2)}) collective-permute-start(bf16[256,512]{0,1:T(8,128)(2,1)} %collective-permute-done.2), channel_id=1, source_target_pairs={{0,4},{4,8},{8,12},{12,16},{16,20},{20,24},{24,28},{28,32},{32,36}... | collective-permute-start | bytes 786440 | tf_op jit(solution)/shard_map/ppermute | solution.py:15
  81.1 18.2 %copy-start.1 = (f32[4,256,256]{1,2,0:T(8,128)}, f32[4,256,256]{1,2,0:T(8,128)S(1)}, u32[]{:S(2)}) copy-start(f32[4,256,256]{1,2,0:T(8,128)S(1)} %get-tuple-element.37) | copy-start | bytes 3145732
  98.7 1.0 copy-start.8
  101.5 3.1 copy-start.2
  101.5 3.1 copy-start.19
  103.3 1.8 copy-start.9
  103.3 1.8 copy-start.23
  109.2 2.3 copy-start.12
  111.9 5.0 copy-start.6
  116.8 3.3 copy-start.7
  116.8 375.7 %collective-permute-start.12 = (bf16[256,4,128]{0,2,1:T(8,128)(2,1)}, bf16[256,4,128]{0,2,1:T(8,128)(2,1)}, u32[]{:S(2)}, u32[]{:S(2)}) collective-permute-start(bf16[256,4,128]{0,2,1:T(8,128)(2,1)} %fusion.39), channel_id=1, source_target_pairs={{252,0},{0,4},{4,8},{8,12},{12,16},{16,20},{20,24},{24,28},{28,32}... | collective-permute-start | bytes 786440 | tf_op jit(solution)/shard_map/ppermute | solution.py:21
  116.8 377.1 %collective-permute-start.15 = (bf16[256,4,128]{0,2,1:T(8,128)(2,1)}, bf16[256,4,128]{0,2,1:T(8,128)(2,1)S(1)}, u32[]{:S(2)}, u32[]{:S(2)}) collective-permute-start(bf16[256,4,128]{0,2,1:T(8,128)(2,1)} %fusion.38), channel_id=1, source_target_pairs={{252,0},{0,4},{4,8},{8,12},{12,16},{16,20},{20,24},{24,28},{28,32}... | collective-permute-start | bytes 786440 | tf_op jit(solution)/shard_map/ppermute | solution.py:21
  118.0 3.3 copy-start.18
  121.2 2.3 copy-start.16
  121.2 2.3 copy-start.20
  486.3 1.8 copy-start.14
  486.3 2.9 copy-start.3
  489.3 4.7 copy-start.4
  493.8 13.5 %copy-start.13 = (f32[256,4,128]{0,2,1:T(8,128)S(1)}, f32[256,4,128]{0,2,1:T(8,128)}, u32[]{:S(2)}) copy-start(f32[256,4,128]{0,2,1:T(8,128)} %convolution_bitcast_fusion.5) | copy-start | bytes 1572868
  493.8 10.7 %collective-permute-start.13 = (bf16[256,4,128]{0,2,1:T(8,128)(2,1)S(1)}, bf16[256,4,128]{0,2,1:T(8,128)(2,1)S(1)}, u32[]{:S(2)}, u32[]{:S(2)}) collective-permute-start(bf16[256,4,128]{0,2,1:T(8,128)(2,1)S(1)} %add_convert_fusion.3), channel_id=1, source_target_pairs={{252,0},{0,4},{4,8},{8,12},{12,16},{16,20},{20,24},{24,28},{28,32}... | collective-permute-start | bytes 786440 | tf_op jit(solution)/shard_map/ppermute | solution.py:21
  494.2 13.1 %collective-permute-start.16 = (bf16[256,4,128]{0,2,1:T(8,128)(2,1)S(1)}, bf16[256,4,128]{0,2,1:T(8,128)(2,1)S(1)}, u32[]{:S(2)}, u32[]{:S(2)}) collective-permute-start(bf16[256,4,128]{0,2,1:T(8,128)(2,1)S(1)} %add_convert_fusion.1), channel_id=1, source_target_pairs={{252,0},{0,4},{4,8},{8,12},{12,16},{16,20},{20,24},{24,28},{28,32}... | collective-permute-start | bytes 786440 | tf_op jit(solution)/shard_map/ppermute | solution.py:21
  504.6 10.7 %collective-permute-start.14 = (bf16[256,4,128]{0,2,1:T(8,128)(2,1)S(1)}, bf16[256,4,128]{0,2,1:T(8,128)(2,1)S(1)}, u32[]{:S(2)}, u32[]{:S(2)}) collective-permute-start(bf16[256,4,128]{0,2,1:T(8,128)(2,1)S(1)} %add_convert_fusion.2), channel_id=1, source_target_pairs={{252,0},{0,4},{4,8},{8,12},{12,16},{16,20},{20,24},{24,28},{28,32}... | collective-permute-start | bytes 786440 | tf_op jit(solution)/shard_map/ppermute | solution.py:21
  508.1 10.9 %collective-permute-start.17 = (bf16[256,4,128]{0,2,1:T(8,128)(2,1)}, bf16[256,4,128]{0,2,1:T(8,128)(2,1)}, u32[]{:S(2)}, u32[]{:S(2)}) collective-permute-start(bf16[256,4,128]{0,2,1:T(8,128)(2,1)} %add_convert_fusion), channel_id=1, source_target_pairs={{252,0},{0,4},{4,8},{8,12},{12,16},{16,20},{20,24},{24,28},{28,32}... | collective-permute-start | bytes 786440 | tf_op jit(solution)/shard_map/ppermute | solution.py:21
Sparse Core Ops, SparseCore 0:
  9.9 24.4 all-gather.1
where the time goes:
time: 529 us; the launch traced here: 528 us
  blocking collectives  360 us (68%)
  waiting for transfers between devices  56.7 us (11%)
  matrix products  42.1 us (8%)
  starting transfers between devices  31 us (6%)
  local copies, waits for them, and re-layouts  18.6 us (4%)
  between operations  14.6 us (3%)
    psum x1, blocking collectives, body(): grad_weight = lax.psum(weight_term, 'ctx').astype(jnp.bfloat16)  360 us
    ppermute x12, waiting for transfers between devices, from_behind(): lax.ppermute(value, axis, [(source, source + steps) for source in range(f...  37.8 us
    ppermute x12, starting transfers between devices, from_behind(): lax.ppermute(value, axis, [(source, source + steps) for source in range(f...  30.7 us
    ppermute x6, waiting for transfers between devices, shifted(): return lax.ppermute(block, axis, route)  18.2 us
    dot_general x8, matrix products, block_scores(): jnp.einsum('qhd,khd->hqk', query_heads, key_heads, preferred_element_type...  12.9 us
  transfers between devices with their start and end apart: 19, of which 10 were waited for; matrix products, arithmetic and copies ran while one was open for 12% of the time, Pallas kernels for 0%

commit v1 on v0

v1 whole, which is shorter than its diff:
```python
import math

import jax
import jax.numpy as jnp
from jax import lax
from jax.experimental import pallas as pl
from jax.experimental.pallas import tpu as pltpu
from jax.sharding import Mesh
from jax.sharding import PartitionSpec as P

HDIM = 128
TOK = 256
REACH = 4
HALO = REACH - 1
SCALE = 1.0 / math.sqrt(HDIM)
LOG2E = math.log2(math.e)
LN2 = math.log(2.0)
FAR = 1e30
EXTRA = 16
VMEM_BYTES = 48 * 1024 * 1024

f32 = jnp.float32
bf16 = jnp.bfloat16

Q_F, K_F, V_F, K_B, V_B, Q_B, EXT = (TOK * i for i in range(7))
BLOCK_ROWS = EXT + EXTRA
HALO_FROM = K_F
GRAD_ROWS = TOK + EXTRA


def nt(a, b):
    return lax.dot_general(a, b, (((1,), (1,)), ((), ())), preferred_element_type=f32)


def nn(a, b):
    return lax.dot_general(a, b, (((1,), (0,)), ((), ())), preferred_element_type=f32)


def three_terms(value):
    high = value.astype(bf16).astype(f32)
    rest = value - high
    middle = rest.astype(bf16).astype(f32)
    return [high, middle, rest - middle]


def extra_rows(rows):
    halves = []
    for row in rows:
        halves += [row[:, :HDIM], row[:, HDIM:]]
    halves += [jnp.zeros((EXTRA - len(halves), HDIM), f32)]
    return jnp.concatenate(halves, axis=0).astype(bf16)


def row_of(extra, first, count=1):
    total = None
    for i in range(first, first + count):
        row = jnp.concatenate([extra[2 * i : 2 * i + 1], extra[2 * i + 1 : 2 * i + 2]], axis=1)
        total = row if total is None else total + row
    return total


def call(kernel, out_shape, n_smem, *args):
    spaces = [pltpu.SMEM] * n_smem + [pltpu.VMEM] * (len(args) - n_smem)
    single = not isinstance(out_shape, (tuple, list))
    out_space = pl.BlockSpec(memory_space=pltpu.VMEM)
    return pl.pallas_call(
        kernel,
        out_shape=out_shape,
        in_specs=[pl.BlockSpec(memory_space=space) for space in spaces],
        out_specs=out_space if single else [out_space] * len(out_shape),
        compiler_params=pltpu.CompilerParams(vmem_limit_bytes=VMEM_BYTES),
    )(*args)


def shape(*dims, dtype=bf16):
    return jax.ShapeDtypeStruct(dims, dtype)


def pack_kernel(qf, kf, vf, kb, vb, qb, lse, ends, out):
    for head in range(4):
        lanes = slice(head * HDIM, (head + 1) * HDIM)
        for i, ref in enumerate((qf, kf, vf, kb, vb, qb)):
            out[head, i * TOK : (i + 1) * TOK, :] = ref[:, lanes]
        rows = [ends[0:1, :], ends[1:2, :]] + three_terms(lse[head : head + 1, :])
        out[head, EXT:, :] = extra_rows(rows)


def part(own, halo, index, first, rows):
    if index < HALO:
        return halo[index, first - HALO_FROM : first - HALO_FROM + rows, :]
    return own[index - HALO, first : first + rows, :]


def forward_kernel(first_row, own, halo, out):
    off = jnp.where(first_row[0] == 0, FAR, 0.0).astype(f32)
    scale2 = SCALE * LOG2E
    key_index = lax.broadcasted_iota(jnp.int32, (TOK, TOK), 0)
    keys, values = [], []
    for i in range(7):
        keys.append(part(own, halo, i, K_F, TOK))
        values.append(part(own, halo, i, V_F, TOK).T)
    for a in range(4):
        query = own[a, Q_F : Q_F + TOK, :]
        ends = row_of(own[a, EXT:, :].astype(f32), 0).astype(jnp.int32)
        scores = []
        for b in range(a, a + REACH):
            s = nt(keys[b], query) * scale2
            if b < HALO:
                s = s - off
            if b == a + HALO:
                s = jnp.where(key_index <= ends, s, -FAR)
            scores.append(s)
        top = scores[0].max(0, keepdims=True)
        for s in scores[1:]:
            top = jnp.maximum(top, s.max(0, keepdims=True))
        total = jnp.zeros((1, TOK), f32)
        summed = jnp.zeros((HDIM, TOK), f32)
        for b, s in zip(range(a, a + REACH), scores):
            weights = jnp.exp2(s - top)
            total = total + weights.sum(0, keepdims=True)
            summed = summed + nn(values[b], weights.astype(bf16))
        out[a, :TOK, :] = (summed / total).T.astype(bf16)
        out[a, TOK:, :] = extra_rows(three_terms(top * LN2 + jnp.log(total)))


def backward_kernel(first_row, own, halo, grads, grads_halo, forward_out, out):
    off = jnp.where(first_row[0] == 0, FAR, 0.0).astype(f32)
    scale2 = SCALE * LOG2E
    key_index = lax.broadcasted_iota(jnp.int32, (TOK, TOK), 0)
    out[:, 3 * TOK :, :] = forward_out[...]

    def grad_rows(index, first, rows):
        if index < HALO:
            return grads_halo[index, first : first + rows, :]
        return grads[index - HALO, first : first + rows, :]

    extra = [part(own, halo, i, EXT, EXTRA).astype(f32) for i in range(7)]
    delta = [row_of(grad_rows(i, TOK, EXTRA).astype(f32), 0, 3) for i in range(7)]
    totals = [row_of(extra[i], 2, 3) * LOG2E for i in range(7)]
    grad_query = [None] * 7
    for b in range(7):
        key = part(own, halo, b, K_B, TOK)
        value = part(own, halo, b, V_B, TOK)
        key_turned = key.T
        grad_key = grad_value = None
        for a in range(b, min(b + REACH, 7)):
            if a < HALO and b > HALO:
                continue
            query = part(own, halo, a, Q_B, TOK)
            grad = grad_rows(a, 0, TOK)
            total = totals[a] + off if (a >= HALO and b < HALO) else totals[a]
            weights = jnp.exp2(nt(key, query) * scale2 - total)
            if a == b:
                ends = row_of(extra[a], 1).astype(jnp.int32)
                weights = jnp.where(key_index <= ends, weights, 0.0)
            scores = (weights * (nt(value, grad) - delta[a])).astype(bf16)
            if b <= HALO:
                dk, dv = nn(scores, query), nn(weights.astype(bf16), grad)
                grad_key = dk if grad_key is None else grad_key + dk
                grad_value = dv if grad_value is None else grad_value + dv
            if a >= HALO:
                dq = nn(key_turned, scores)
                grad_query[a] = dq if grad_query[a] is None else grad_query[a] + dq
        if b <= HALO:
            out[b, TOK : 2 * TOK, :] = (grad_key * SCALE).astype(bf16)
            out[b, 2 * TOK : 3 * TOK, :] = grad_value.astype(bf16)
    for a in range(4):
        out[a, :TOK, :] = (grad_query[a + HALO] * SCALE).T.astype(bf16)


def unpack_kernel(packed, attended, log_total, grad_query, grad_keys, grad_values):
    for head in range(4):
        lanes = slice(head * HDIM, (head + 1) * HDIM)
        grad_query[:, lanes] = packed[head, :TOK, :].astype(f32)
        grad_keys[:, lanes] = packed[head, TOK : 2 * TOK, :].astype(f32)
        grad_values[:, lanes] = packed[head, 2 * TOK : 3 * TOK, :].astype(f32)
        attended[:, lanes] = packed[head, 3 * TOK : 4 * TOK, :]
        extra = packed[head, 4 * TOK :, :].astype(f32)
        log_total[head : head + 1, :] = row_of(extra, 0, 3)


def grad_kernel(place, c0, c1, c2, c3, o0, o1, o2, o3, weight, attn, attn_far, out):
    y_lo, y_hi, core = place[0], place[1], place[2]
    own = {(0, 0): c0, (0, 1): o0, (1, 0): c2, (1, 1): o2}
    far = {(0, 0): (c1, c3), (0, 1): (o1, o3), (1, 0): (c3, c1), (1, 1): (o3, o1)}
    width = 4 * HDIM
    half = attn[:, pl.ds(pl.multiple_of(y_lo * TOK, TOK), TOK)].T
    half_far = attn_far[...].T
    total = None
    for (hi, side), cot_ref in own.items():
        y = y_hi + hi - 2 * y_hi * hi
        c = core + side - 2 * core * side
        group = 2 * y + c
        cot = cot_ref[...]
        term = nt(cot, weight[:, pl.ds(pl.multiple_of(group * width, width), width)])
        total = term if total is None else total + term
        pair = far[hi, side]
        cot_far = jnp.where(y_lo == 1, pair[0][...], pair[1][...])
        product = (nn(half, cot) + nn(half_far, cot_far)).astype(bf16)
        for j in range(4):
            rows = pl.ds(GRAD_ROWS + j * TOK, TOK)
            out[group, rows, :] = product[:, j * HDIM : (j + 1) * HDIM]
    grad = total.astype(bf16)
    for head in range(4):
        lanes = slice(head * HDIM, (head + 1) * HDIM)
        product = grad[:, lanes].astype(f32) * attn[:, lanes].astype(f32)
        out[head, :TOK, :] = grad[:, lanes]
        out[head, TOK:GRAD_ROWS, :] = extra_rows(three_terms(product.T.sum(0, keepdims=True)))


def sum_kernel(parts, out):
    total = parts[0, GRAD_ROWS:, :].astype(f32)
    for i in range(1, 4):
        total = total + parts[i, GRAD_ROWS:, :].astype(f32)
    out[...] = total.astype(bf16)


def last_sum_kernel(parts, out):
    total = parts[0].astype(f32)
    for i in range(1, 8):
        total = total + parts[i].astype(f32)
    total = total.astype(bf16)
    for i in range(8):
        out[i] = total


def assemble_kernel(parts, out):
    for y in range(2):
        for x in range(4):
            for j in range(4):
                lanes = slice((x * 4 + j) * HDIM, (x * 4 + j + 1) * HDIM)
                out[y * TOK : (y + 1) * TOK, lanes] = parts[y * 4 + x, j * TOK : (j + 1) * TOK, :]


def across(value, axes):
    return lax.all_to_all(value, axes, 0, 0, tiled=True)


def along_y(value, distance):
    def place(y):
        return (y % 2) * 2 + (y // 2) % 2

    return lax.ppermute(value, ("yl", "yh"), [(place(y), place((y + distance) % 4)) for y in range(4)])


def next_row(value):
    return lax.ppermute(value, ("yl", "z"), [(i, (i + 1) % 16) for i in range(16)])


def other(value, axis):
    return lax.ppermute(value, axis, [(0, 1), (1, 0)])


def block_ends(frames):
    return (frames[:, None] <= frames[None, :]).astype(f32).sum(0) - 1.0


def body(
    frames_fwd,
    query_fwd,
    keys_fwd,
    values_fwd,
    frames_bwd,
    query_bwd,
    keys_bwd,
    values_bwd,
    attn_bwd,
    logsumexp_bwd,
    cotangent,
    out_weight,
):
    y_lo = lax.axis_index("yl")
    place = jnp.stack([y_lo, lax.axis_index("yh"), lax.axis_index("core")]).astype(jnp.int32)
    row = (lax.axis_index(("yl", "z"))).astype(jnp.int32).reshape(1)

    cots = [cotangent] + [along_y(cotangent, d) for d in range(1, 4)]
    attn_far = other(lax.dynamic_slice_in_dim(attn_bwd, (1 - y_lo) * TOK, TOK, 1), "yl")

    ends = jnp.stack([block_ends(frames_fwd), block_ends(frames_bwd)])
    packed = call(
        pack_kernel,
        shape(4, BLOCK_ROWS, HDIM),
        0,
        query_fwd,
        keys_fwd,
        values_fwd,
        keys_bwd,
        values_bwd,
        query_bwd,
        logsumexp_bwd,
        ends,
    )
    own = across(packed, "x")
    halo = next_row(own[1:, HALO_FROM:, :])

    others = [other(c, "core") for c in cots]
    grads_packed = call(
        grad_kernel,
        shape(4, GRAD_ROWS + 4 * TOK, HDIM),
        1,
        place,
        *cots,
        *others,
        out_weight,
        attn_bwd,
        attn_far,
    )
    grads = across(grads_packed, "x")
    grads_own = grads[:, :GRAD_ROWS, :]
    grads_halo = next_row(grads[1:, :GRAD_ROWS, :])

    summed = call(sum_kernel, shape(4 * TOK, HDIM), 0, grads)
    parts = across(summed.reshape(8, HDIM, HDIM), "z")
    chunks = call(last_sum_kernel, shape(8, HDIM, HDIM), 0, parts)
    gathered = across(chunks, "z").reshape(1, 4 * TOK, HDIM)

    forward_out = call(forward_kernel, shape(4, GRAD_ROWS, HDIM), 1, row, own, halo)
    backward_out = call(
        backward_kernel,
        shape(4, 4 * TOK + EXTRA, HDIM),
        1,
        row,
        own,
        halo,
        grads_own,
        grads_halo,
        forward_out,
    )
    back = across(backward_out, "x")
    attended, log_total, grad_query, grad_keys, grad_values = call(
        unpack_kernel,
        [
            shape(TOK, 4 * HDIM),
            shape(4, TOK, dtype=f32),
            shape(TOK, 4 * HDIM, dtype=f32),
            shape(TOK, 4 * HDIM, dtype=f32),
            shape(TOK, 4 * HDIM, dtype=f32),
        ],
        0,
        back,
    )
    whole = across(jnp.broadcast_to(gathered, (8, 4 * TOK, HDIM)), ("yl", "x"))
    grad_weight = call(assemble_kernel, shape(2 * TOK, 16 * HDIM), 0, whole)
    return (attended, log_total, grad_query, grad_keys, grad_values, grad_weight)


def solution(mesh):
    fine = Mesh(mesh.devices.reshape(2, 8, 4, 2, 2), ("yl", "z", "x", "yh", "core"))
    ctx, dp = ("yl", "z", "x"), ("yh", "core")
    in_specs = (
        P(ctx),
        P(ctx, dp),
        P(ctx, dp),
        P(ctx, dp),
        P(ctx),
        P(ctx, dp),
        P(ctx, dp),
        P(ctx, dp),
        P(ctx, dp),
        P(dp, ctx),
        P(ctx, dp),
        P(dp, None),
    )
    out_specs = (
        P(ctx, dp),
        P(dp, ctx),
        P(ctx, dp),
        P(ctx, dp),
        P(ctx, dp),
        P(dp, None),
    )
    return jax.shard_map(body, mesh=fine, in_specs=in_specs, out_specs=out_specs, check_vma=False)
```

time: 529 us -> 159 us (0.30)
  the two profiles are of different devices: /device:TPU:24 before, /device:TPU:2 now
where the time goes in v1:
time: 159 us; the launch traced here: 157 us
  waiting for transfers between devices  59.5 us (37%)
  blocking collectives  35.3 us (22%)
  starting transfers between devices  28.7 us (18%)
  Pallas kernels  17.6 us (11%)
  local copies, waits for them, and re-layouts  13 us (8%)
  other arithmetic  1.83 us (1%)
    all_to_all x4, waiting for transfers between devices, across(): return lax.all_to_all(value, axes, 0, 0, tiled=True)  35.5 us
    all_to_all x2, blocking collectives, across(): return lax.all_to_all(value, axes, 0, 0, tiled=True)  35.3 us
    all_to_all x4, starting transfers between devices, across(): return lax.all_to_all(value, axes, 0, 0, tiled=True)  20.7 us
    pallas_call x8, Pallas kernels, call(): pl.pallas_call(kernel, out_shape=out_shape, in_specs=[pl.BlockSpec(memory...  17.6 us
    ppermute x3, waiting for transfers between devices, along_y(): lax.ppermute(value, ('yl', 'yh'), [(place(y), place((y + distance) % 4))...  12.3 us
    unnamed x24, local copies, waits for them, and re-layouts  9.05 us
    ppermute x5, waiting for transfers between devices, other(): return lax.ppermute(value, axis, [(0, 1), (1, 0)])  6.04 us
    ppermute x2, waiting for transfers between devices, next_row(): lax.ppermute(value, ('yl', 'z'), [(i, (i + 1) % 16) for i in range(16)])  5.6 us
  transfers between devices with their start and end apart: 14, of which 7 were waited for; matrix products, arithmetic and copies ran while one was open for 2% of the time, Pallas kernels for 9%

profile of v1, /device:TPU:2, one launch (start us, length us, event | category | flops | bytes accessed | tf_op | source)
XLA Modules:
  0.0 156.7 jit_solution(12548682163839816430)
XLA Ops:
  0.6 0.9 convert_reduce_fusion.1
  1.5 0.9 convert_reduce_fusion
  2.4 0.0 copy-start.5
  2.4 0.9 copy-done.5
  3.4 0.9 copy-done.6
  4.3 0.9 copy-done.7
  5.3 0.9 copy-done.8
  6.2 0.9 copy-done.9
  7.2 0.9 copy-done.10
  8.1 0.7 copy-done.11
  8.8 1.4 shard_map.163
  10.2 5.9 %all-to-all-start = ((bf16[4,1552,128]{2,1,0:T(8,128)(2,1)}), bf16[4,1552,128]{2,1,0:T(8,128)(2,1)S(1)}, u32[]{:S(2)}, u32[]{:S(2)}) async-start(bf16[4,1552,128]{2,1,0:T(8,128)(2,1)} %shard_map.163), calls=%async_computation | async-start | bytes 3178496 | tf_op jit(solution)/shard_map/all_to_all | solution.py:236
  16.2 2.0 %collective-permute-start.3 = (bf16[256,512]{1,0:T(8,128)(2,1)S(1)}, bf16[256,512]{1,0:T(8,128)(2,1)S(1)}, u32[]{:S(2)}, u32[]{:S(2)}) collective-permute-start(bf16[256,512]{1,0:T(8,128)(2,1)S(1)} %copy-done.4), channel_id=1, source_target_pairs={{0,130},{128,0},{2,128},{130,2},{1,131},{129,1},{3,129},{131,3},{4... | collective-permute-start | bytes 786440 | tf_op jit(solution)/shard_map/ppermute | solution.py:243
  18.2 0.6 collective-permute-start.2
  18.8 1.0 collective-permute-start.1
  19.8 0.0 collective-permute-start.4
  19.8 9.0 %collective-permute-done.3.c3 = bf16[256,512]{1,0:T(8,128)(2,1)S(1)} collective-permute-done((bf16[256,512]{1,0:T(8,128)(2,1)S(1)}, bf16[256,512]{1,0:T(8,128)(2,1)S(1)}, u32[]{:S(2)}, u32[]{:S(2)}) %collective-permute-start.3) | collective-permute-done | bytes 262176 | tf_op jit(solution)/shard_map/ppermute | solution.py:243
  28.8 0.1 collective-permute-done.2.c2
  29.0 0.4 collective-permute-start.6
  29.4 3.2 %collective-permute-done.1.c1 = bf16[256,512]{1,0:T(8,128)(2,1)S(1)} collective-permute-done((bf16[256,512]{1,0:T(8,128)(2,1)S(1)}, bf16[256,512]{1,0:T(8,128)(2,1)S(1)}, u32[]{:S(2)}, u32[]{:S(2)}) %collective-permute-start.1) | collective-permute-done | bytes 262176 | tf_op jit(solution)/shard_map/ppermute | solution.py:243
  32.5 0.0 collective-permute-start.5
  32.6 0.7 constant_dynamic-slice_fusion
  33.2 0.1 pad_add_fusion.place
  33.3 6.0 %collective-permute-done.8.attn_far = bf16[256,256]{1,0:T(8,128)(2,1)S(1)} collective-permute-done((bf16[256,256]{1,0:T(8,128)(2,1)}, bf16[256,256]{1,0:T(8,128)(2,1)S(1)}, u32[]{:S(2)}, u32[]{:S(2)}) %collective-permute-start.8) | collective-permute-done | bytes 131104 | tf_op jit(solution)/shard_map/ppermute | solution.py:251
  39.3 0.0 collective-permute-done.4.o0
  39.4 0.0 copy-start.2
  39.4 1.6 %copy-done.2 = bf16[512,2048]{1,0:T(8,128)(2,1)S(1)} copy-done((bf16[512,2048]{1,0:T(8,128)(2,1)S(1)}, bf16[512,2048]{1,0:T(8,128)(2,1)}, u32[]{:S(2)}) %copy-start.2) | copy-done | bytes 2097176
  41.0 2.4 %shard_map.164 = bf16[4,1296,128]{2,1,0:T(8,128)(2,1)S(1)} custom-call(s32[3]{0:T(128)S(1)} %pad_add_fusion.place, bf16[256,512]{1,0:T(8,128)(2,1)S(1)} %copy-done.4, bf16[256,512]{1,0:T(8,128)(2,1)S(1)} %collective-permute-done.1.c1, bf16[256,512]{1,0:T(8,128)(2,1)S(1)} %collective-permute-done.2.c2, bf16[256,512]{1,0:T(8,128)(2,1)S(1)} %collective-permute-done.3.c3, ...), custom_call_target="tpu_custom_call" | custom-call | tf_op jit(solution)/shard_map/pallas_call | solution.py:66
  43.3 1.1 copy-done
  44.4 4.8 %all-to-all-start.1 = ((bf16[4,1296,128]{2,1,0:T(8,128)(2,1)}), bf16[4,1296,128]{2,1,0:T(8,128)(2,1)S(1)}, u32[]{:S(2)}, u32[]{:S(2)}) async-start(bf16[4,1296,128]{2,1,0:T(8,128)(2,1)} %copy-done), calls=%async_computation.1 | async-start | bytes 2654208 | tf_op jit(solution)/shard_map/all_to_all | solution.py:236
  49.2 1.0 slice.12
  50.2 1.9 %collective-permute-start = (bf16[3,1296,128]{2,1,0:T(8,128)(2,1)}, bf16[3,1296,128]{2,1,0:T(8,128)(2,1)}, u32[]{:S(2)}, u32[]{:S(2)}) collective-permute-start(bf16[3,1296,128]{2,1,0:T(8,128)(2,1)} %slice.12), channel_id=1, source_target_pairs={{0,16},{16,32},{32,48},{48,64},{64,80},{80,96},{96,112},{112,128},... | collective-permute-start | bytes 2985992 | tf_op jit(solution)/shard_map/ppermute | solution.py:247
  52.1 13.6 %all-to-all-done.1.parts = bf16[4,1296,128]{2,1,0:T(8,128)(2,1)S(1)} async-done(((bf16[4,1296,128]{2,1,0:T(8,128)(2,1)}), bf16[4,1296,128]{2,1,0:T(8,128)(2,1)S(1)}, u32[]{:S(2)}, u32[]{:S(2)}) %all-to-all-start.1) | async-done | bytes 1327136 | tf_op jit(solution)/shard_map/all_to_all | solution.py:236
  65.7 0.1 shard_map.168
  65.8 18.1 %all_to_all.30.parts = bf16[8,128,128]{2,1,0:T(8,128)(2,1)S(1)} all-to-all(bf16[8,128,128]{2,1,0:T(8,128)(2,1)S(1)} %bitcast.8), channel_id=1, replica_groups=mesh['yl'=2,'z'=8,'x'=4,'yh'=2,'core'=2] {'z'}, dimensions={0} | all-to-all | bytes 524288 | tf_op jit(solution)/shard_map/all_to_all | solution.py:236
  83.9 0.7 shard_map.169
  84.7 4.9 %all-to-all-start.4 = ((bf16[8,128,128]{2,1,0:T(8,128)(2,1)}), bf16[8,128,128]{2,1,0:T(8,128)(2,1)S(1)}, u32[]{:S(2)}, u32[]{:S(2)}) async-start(bf16[8,128,128]{2,1,0:T(8,128)(2,1)} %shard_map.169), calls=%async_computation.4 | async-start | bytes 524288 | tf_op jit(solution)/shard_map/all_to_all | solution.py:236
  89.5 0.7 slice.14
  90.2 2.0 %collective-permute-start.9 = (bf16[3,272,128]{2,1,0:T(8,128)(2,1)}, bf16[3,272,128]{2,1,0:T(8,128)(2,1)S(1)}, u32[]{:S(2)}, u32[]{:S(2)}) collective-permute-start(bf16[3,272,128]{2,1,0:T(8,128)(2,1)} %slice.14), channel_id=1, source_target_pairs={{0,16},{16,32},{32,48},{48,64},{64,80},{80,96},{96,112},{112,128},... | collective-permute-start | bytes 626696 | tf_op jit(solution)/shard_map/ppermute | solution.py:247
  92.3 3.6 %shard_map.165.forward_out = bf16[4,272,128]{2,1,0:T(8,128)(2,1)S(1)} custom-call(s32[1]{0:T(128)} %bitcast.first_row, bf16[4,1552,128]{2,1,0:T(8,128)(2,1)S(1)} %all-to-all-done.own, bf16[3,1296,128]{2,1,0:T(8,128)(2,1)} %collective-permute-done.halo), custom_call_target="tpu_custom_call" | custom-call | tf_op jit(solution)/shard_map/pallas_call | solution.py:66
  95.9 5.6 %collective-permute-done.9.grads_halo = bf16[3,272,128]{2,1,0:T(8,128)(2,1)S(1)} collective-permute-done((bf16[3,272,128]{2,1,0:T(8,128)(2,1)}, bf16[3,272,128]{2,1,0:T(8,128)(2,1)S(1)}, u32[]{:S(2)}, u32[]{:S(2)}) %collective-permute-start.9) | collective-permute-done | bytes 208928 | tf_op jit(solution)/shard_map/ppermute | solution.py:247
  101.5 6.0 %shard_map.166 = bf16[4,1040,128]{2,1,0:T(8,128)(2,1)S(1)} custom-call(s32[1]{0:T(128)} %bitcast.first_row, bf16[4,1552,128]{2,1,0:T(8,128)(2,1)S(1)} %all-to-all-done.own, bf16[3,1296,128]{2,1,0:T(8,128)(2,1)} %collective-permute-done.halo, bf16[4,272,128]{2,1,0:T(8,128)(2,1)S(1)} %slice.13.grads, ...), custom_call_target="tpu_custom_call" | custom-call | tf_op jit(solution)/shard_map/pallas_call | solution.py:66
  107.5 17.2 %all_to_all.31.packed = bf16[4,1040,128]{2,1,0:T(8,128)(2,1)} all-to-all(bf16[4,1040,128]{2,1,0:T(8,128)(2,1)S(1)} %shard_map.166), channel_id=1, replica_groups=mesh['yl'=2,'z'=8,'x'=4,'yh'=2,'core'=2] {'x'}, dimensions={0} | all-to-all | bytes 2129920 | tf_op jit(solution)/shard_map/all_to_all | solution.py:236
  124.7 1.6 %broadcast_in_dim.5 = bf16[8,1024,128]{2,1,0:T(8,128)(2,1)} broadcast(bf16[1024,128]{1,0:T(8,128)(2,1)S(1)} %bitcast.9), dimensions={1,2} | broadcast | bytes 2359296 | tf_op jit(solution)/shard_map/broadcast_in_dim | solution.py:342
  126.3 5.1 %all-to-all-start.5 = ((bf16[8,1024,128]{2,1,0:T(8,128)(2,1)}), bf16[8,1024,128]{2,1,0:T(8,128)(2,1)S(1)}, u32[]{:S(2)}, u32[]{:S(2)}) async-start(bf16[8,1024,128]{2,1,0:T(8,128)(2,1)} %broadcast_in_dim.5), calls=%async_computation.5 | async-start | bytes 4194304 | tf_op jit(solution)/shard_map/all_to_all | solution.py:236
  131.4 1.4 shard_map.167
  132.8 21.9 %all-to-all-done.5.parts = bf16[8,1024,128]{2,1,0:T(8,128)(2,1)S(1)} async-done(((bf16[8,1024,128]{2,1,0:T(8,128)(2,1)}), bf16[8,1024,128]{2,1,0:T(8,128)(2,1)S(1)}, u32[]{:S(2)}, u32[]{:S(2)}) %all-to-all-start.5) | async-done | bytes 2097184 | tf_op jit(solution)/shard_map/all_to_all | solution.py:236
  154.8 1.9 %shard_map.170 = bf16[512,2048]{1,0:T(8,128)(2,1)} custom-call(bf16[8,1024,128]{2,1,0:T(8,128)(2,1)S(1)} %all-to-all-done.5.parts), custom_call_target="tpu_custom_call" | custom-call | tf_op jit(solution)/shard_map/pallas_call | solution.py:66
  (25 shorter events, 0.1 us)
Async XLA Ops:
  2.4 1.0 copy-start.5
  3.4 0.9 copy-start.6
  4.3 0.9 copy-start.7
  5.3 0.9 copy-start.8
  6.2 0.9 copy-start.9
  7.2 0.9 copy-start.10
  8.1 0.7 copy-start.11
  10.2 5.9 %copy-start.4 = (bf16[256,512]{1,0:T(8,128)(2,1)S(1)}, bf16[256,512]{1,0:T(8,128)(2,1)}, u32[]{:S(2)}) copy-start(bf16[256,512]{1,0:T(8,128)(2,1)} %c0.1) | copy-start | bytes 786436
  10.2 22.3 %copy-start.3 = (bf16[256,512]{1,0:T(8,128)(2,1)S(1)}, bf16[256,512]{1,0:T(8,128)(2,1)}, u32[]{:S(2)}) copy-start(bf16[256,512]{1,0:T(8,128)(2,1)} %attn.1) | copy-start | bytes 786436
  10.2 34.2 %all-to-all-start = ((bf16[4,1552,128]{2,1,0:T(8,128)(2,1)}), bf16[4,1552,128]{2,1,0:T(8,128)(2,1)S(1)}, u32[]{:S(2)}, u32[]{:S(2)}) async-start(bf16[4,1552,128]{2,1,0:T(8,128)(2,1)} %shard_map.163), calls=%async_computation | async-start | bytes 3178496 | tf_op jit(solution)/shard_map/all_to_all | solution.py:236
  16.2 12.7 %collective-permute-start.3 = (bf16[256,512]{1,0:T(8,128)(2,1)S(1)}, bf16[256,512]{1,0:T(8,128)(2,1)S(1)}, u32[]{:S(2)}, u32[]{:S(2)}) collective-permute-start(bf16[256,512]{1,0:T(8,128)(2,1)S(1)} %copy-done.4), channel_id=1, source_target_pairs={{0,130},{128,0},{2,128},{130,2},{1,131},{129,1},{3,129},{131,3},{4... | collective-permute-start | bytes 786440 | tf_op jit(solution)/shard_map/ppermute | solution.py:243
  18.2 10.8 %collective-permute-start.2 = (bf16[256,512]{1,0:T(8,128)(2,1)S(1)}, bf16[256,512]{1,0:T(8,128)(2,1)S(1)}, u32[]{:S(2)}, u32[]{:S(2)}) collective-permute-start(bf16[256,512]{1,0:T(8,128)(2,1)S(1)} %copy-done.4), channel_id=1, source_target_pairs={{0,2},{128,130},{2,0},{130,128},{1,3},{129,131},{3,1},{131,129},{4... | collective-permute-start | bytes 786440 | tf_op jit(solution)/shard_map/ppermute | solution.py:243
  18.8 13.7 %collective-permute-start.1 = (bf16[256,512]{1,0:T(8,128)(2,1)S(1)}, bf16[256,512]{1,0:T(8,128)(2,1)S(1)}, u32[]{:S(2)}, u32[]{:S(2)}) collective-permute-start(bf16[256,512]{1,0:T(8,128)(2,1)S(1)} %copy-done.4), channel_id=1, source_target_pairs={{0,128},{128,2},{2,130},{130,0},{1,129},{129,3},{3,131},{131,1},{4... | collective-permute-start | bytes 786440 | tf_op jit(solution)/shard_map/ppermute | solution.py:243
  19.8 19.5 %collective-permute-start.4 = (bf16[256,512]{1,0:T(8,128)(2,1)S(1)}, bf16[256,512]{1,0:T(8,128)(2,1)S(1)}, u32[]{:S(2)}, u32[]{:S(2)}) collective-permute-start(bf16[256,512]{1,0:T(8,128)(2,1)S(1)} %copy-done.4), channel_id=1, source_target_pairs={{0,1},{1,0},{2,3},{3,2},{4,5},{5,4},{6,7},{7,6},{8,9},{9,8},{10,11... | collective-permute-start | bytes 786440 | tf_op jit(solution)/shard_map/ppermute | solution.py:251
  28.8 10.5 %collective-permute-start.7 = (bf16[256,512]{1,0:T(8,128)(2,1)S(1)}, bf16[256,512]{1,0:T(8,128)(2,1)S(1)}, u32[]{:S(2)}, u32[]{:S(2)}) collective-permute-start(bf16[256,512]{1,0:T(8,128)(2,1)S(1)} %collective-permute-done.3.c3), channel_id=1, source_target_pairs={{0,1},{1,0},{2,3},{3,2},{4,5},{5,4},{6,7},{7,6},{8,9},{9,8},{10,11... | collective-permute-start | bytes 786440 | tf_op jit(solution)/shard_map/ppermute | solution.py:251
  29.0 10.4 %collective-permute-start.6 = (bf16[256,512]{1,0:T(8,128)(2,1)S(1)}, bf16[256,512]{1,0:T(8,128)(2,1)}, u32[]{:S(2)}, u32[]{:S(2)}) collective-permute-start(bf16[256,512]{1,0:T(8,128)(2,1)S(1)} %collective-permute-done.2.c2), channel_id=1, source_target_pairs={{0,1},{1,0},{2,3},{3,2},{4,5},{5,4},{6,7},{7,6},{8,9},{9,8},{10,11... | collective-permute-start | bytes 786440 | tf_op jit(solution)/shard_map/ppermute | solution.py:251
  32.5 6.8 %collective-permute-start.5 = (bf16[256,512]{1,0:T(8,128)(2,1)S(1)}, bf16[256,512]{1,0:T(8,128)(2,1)}, u32[]{:S(2)}, u32[]{:S(2)}) collective-permute-start(bf16[256,512]{1,0:T(8,128)(2,1)S(1)} %collective-permute-done.1.c1), channel_id=1, source_target_pairs={{0,1},{1,0},{2,3},{3,2},{4,5},{5,4},{6,7},{7,6},{8,9},{9,8},{10,11... | collective-permute-start | bytes 786440 | tf_op jit(solution)/shard_map/ppermute | solution.py:251
  33.2 6.1 %collective-permute-start.8 = (bf16[256,256]{1,0:T(8,128)(2,1)}, bf16[256,256]{1,0:T(8,128)(2,1)S(1)}, u32[]{:S(2)}, u32[]{:S(2)}) collective-permute-start(bf16[256,256]{1,0:T(8,128)(2,1)} %constant_dynamic-slice_fusion), channel_id=1, source_target_pairs={{0,128},{128,0},{1,129},{129,1},{2,130},{130,2},{3,131},{131,3},{4... | collective-permute-start | bytes 393224 | tf_op jit(solution)/shard_map/ppermute | solution.py:251
  39.4 1.6 %copy-start.2 = (bf16[512,2048]{1,0:T(8,128)(2,1)S(1)}, bf16[512,2048]{1,0:T(8,128)(2,1)}, u32[]{:S(2)}) copy-start(bf16[512,2048]{1,0:T(8,128)(2,1)} %weight.1) | copy-start | bytes 6291460
  43.3 1.1 copy-start
  44.4 21.3 %all-to-all-start.1 = ((bf16[4,1296,128]{2,1,0:T(8,128)(2,1)}), bf16[4,1296,128]{2,1,0:T(8,128)(2,1)S(1)}, u32[]{:S(2)}, u32[]{:S(2)}) async-start(bf16[4,1296,128]{2,1,0:T(8,128)(2,1)} %copy-done), calls=%async_computation.1 | async-start | bytes 2654208 | tf_op jit(solution)/shard_map/all_to_all | solution.py:236
  50.2 42.1 %collective-permute-start = (bf16[3,1296,128]{2,1,0:T(8,128)(2,1)}, bf16[3,1296,128]{2,1,0:T(8,128)(2,1)}, u32[]{:S(2)}, u32[]{:S(2)}) collective-permute-start(bf16[3,1296,128]{2,1,0:T(8,128)(2,1)} %slice.12), channel_id=1, source_target_pairs={{0,16},{16,32},{32,48},{48,64},{64,80},{80,96},{96,112},{112,128},... | collective-permute-start | bytes 2985992 | tf_op jit(solution)/shard_map/ppermute | solution.py:247
  84.7 22.8 %all-to-all-start.4 = ((bf16[8,128,128]{2,1,0:T(8,128)(2,1)}), bf16[8,128,128]{2,1,0:T(8,128)(2,1)S(1)}, u32[]{:S(2)}, u32[]{:S(2)}) async-start(bf16[8,128,128]{2,1,0:T(8,128)(2,1)} %shard_map.169), calls=%async_computation.4 | async-start | bytes 524288 | tf_op jit(solution)/shard_map/all_to_all | solution.py:236
  90.2 11.2 %collective-permute-start.9 = (bf16[3,272,128]{2,1,0:T(8,128)(2,1)}, bf16[3,272,128]{2,1,0:T(8,128)(2,1)S(1)}, u32[]{:S(2)}, u32[]{:S(2)}) collective-permute-start(bf16[3,272,128]{2,1,0:T(8,128)(2,1)} %slice.14), channel_id=1, source_target_pairs={{0,16},{16,32},{32,48},{48,64},{64,80},{80,96},{96,112},{112,128},... | collective-permute-start | bytes 626696 | tf_op jit(solution)/shard_map/ppermute | solution.py:247
  126.3 5.1 %copy-start.1 = (bf16[4,1040,128]{2,1,0:T(8,128)(2,1)S(1)}, bf16[4,1040,128]{2,1,0:T(8,128)(2,1)}, u32[]{:S(2)}) copy-start(bf16[4,1040,128]{2,1,0:T(8,128)(2,1)} %all_to_all.31.packed) | copy-start | bytes 3194884
  126.3 28.5 %all-to-all-start.5 = ((bf16[8,1024,128]{2,1,0:T(8,128)(2,1)}), bf16[8,1024,128]{2,1,0:T(8,128)(2,1)S(1)}, u32[]{:S(2)}, u32[]{:S(2)}) async-start(bf16[8,1024,128]{2,1,0:T(8,128)(2,1)} %broadcast_in_dim.5), calls=%async_computation.5 | async-start | bytes 4194304 | tf_op jit(solution)/shard_map/all_to_all | solution.py:236

commit v2 on v1

v2 whole, which is shorter than its diff:
```python
import math

import jax
import jax.numpy as jnp
from jax import lax
from jax.experimental import pallas as pl
from jax.experimental.pallas import tpu as pltpu
from jax.sharding import Mesh
from jax.sharding import PartitionSpec as P

HDIM = 128
TOK = 256
REACH = 4
HALO = REACH - 1
SCALE = 1.0 / math.sqrt(HDIM)
LOG2E = math.log2(math.e)
LN2 = math.log(2.0)
FAR = 1e30
EXTRA = 16
VMEM_BYTES = 48 * 1024 * 1024

f32 = jnp.float32
bf16 = jnp.bfloat16

Q_F, K_F, V_F, K_B, V_B, Q_B, EXT = (TOK * i for i in range(7))
BLOCK_ROWS = EXT + EXTRA
HALO_FROM = K_F
GRAD_ROWS = TOK + EXTRA
BACK_ROWS = 4 * TOK + EXTRA


def nt(a, b):
    return lax.dot_general(a, b, (((1,), (1,)), ((), ())), preferred_element_type=f32)


def nn(a, b):
    return lax.dot_general(a, b, (((1,), (0,)), ((), ())), preferred_element_type=f32)


def three_terms(value):
    high = value.astype(bf16).astype(f32)
    rest = value - high
    middle = rest.astype(bf16).astype(f32)
    return [high, middle, rest - middle]


def extra_rows(rows):
    halves = []
    for row in rows:
        halves += [row[:, :HDIM], row[:, HDIM:]]
    halves += [jnp.zeros((EXTRA - len(halves), HDIM), f32)]
    return jnp.concatenate(halves, axis=0).astype(bf16)


def row_of(extra, first, count=1):
    total = None
    for i in range(first, first + count):
        row = jnp.concatenate([extra[2 * i : 2 * i + 1], extra[2 * i + 1 : 2 * i + 2]], axis=1)
        total = row if total is None else total + row
    return total


def in_hbm(value):
    return pltpu.with_memory_space_constraint(value, pltpu.HBM)


def call(kernel, out_shape, n_smem, *args, scratch=()):
    spaces = [pltpu.SMEM] * n_smem + [pltpu.VMEM] * (len(args) - n_smem)
    single = not isinstance(out_shape, (tuple, list))
    out_space = pl.BlockSpec(memory_space=pltpu.VMEM)
    return pl.pallas_call(
        kernel,
        out_shape=out_shape,
        in_specs=[pl.BlockSpec(memory_space=space) for space in spaces],
        scratch_shapes=scratch,
        out_specs=out_space if single else [out_space] * len(out_shape),
        compiler_params=pltpu.CompilerParams(vmem_limit_bytes=VMEM_BYTES),
    )(*args)


def shape(*dims, dtype=bf16):
    return jax.ShapeDtypeStruct(dims, dtype)


def block_ends(frames):
    across_lanes = jnp.broadcast_to(frames, (TOK, TOK))
    seen = jnp.where(across_lanes.T <= across_lanes, 1.0, 0.0)
    return seen.sum(0, keepdims=True) - 1.0


def pack_kernel(place, qf, kf, vf, kb, vb, qb, lse, attn, cot, frames_fwd, frames_bwd, out, to_pair):
    far_half = pl.multiple_of((1 - place[0]) * TOK, TOK)
    to_pair[:, : 4 * HDIM] = cot[...]
    to_pair[:, 4 * HDIM :] = attn[:, pl.ds(far_half, TOK)]
    ends = [block_ends(frames_fwd[...].astype(f32)), block_ends(frames_bwd[...].astype(f32))]
    for head in range(4):
        lanes = slice(head * HDIM, (head + 1) * HDIM)
        for i, ref in enumerate((qf, kf, vf, kb, vb, qb)):
            out[head, i * TOK : (i + 1) * TOK, :] = ref[:, lanes]
        rows = ends + three_terms(lse[head : head + 1, :])
        out[head, EXT:, :] = extra_rows(rows)


def part(own, halo, index, first, rows):
    if index < HALO:
        return halo[index, first - HALO_FROM : first - HALO_FROM + rows, :]
    return own[index - HALO, first : first + rows, :]


def forward_kernel(place, own, halo, out):
    off = jnp.where(place[0] == 0, FAR, 0.0).astype(f32)
    scale2 = SCALE * LOG2E
    key_index = lax.broadcasted_iota(jnp.int32, (TOK, TOK), 0)
    keys, values = [], []
    for i in range(7):
        keys.append(part(own, halo, i, K_F, TOK))
        values.append(part(own, halo, i, V_F, TOK).T)
    for a in range(4):
        query = own[a, Q_F : Q_F + TOK, :]
        ends = row_of(own[a, EXT:, :].astype(f32), 0).astype(jnp.int32)
        scores = []
        for b in range(a, a + REACH):
            s = nt(keys[b], query) * scale2
            if b < HALO:
                s = s - off
            if b == a + HALO:
                s = jnp.where(key_index <= ends, s, -FAR)
            scores.append(s)
        top = scores[0].max(0, keepdims=True)
        for s in scores[1:]:
            top = jnp.maximum(top, s.max(0, keepdims=True))
        total = jnp.zeros((1, TOK), f32)
        summed = jnp.zeros((HDIM, TOK), f32)
        for b, s in zip(range(a, a + REACH), scores):
            weights = jnp.exp2(s - top)
            total = total + weights.sum(0, keepdims=True)
            summed = summed + nn(values[b], weights.astype(bf16))
        out[a, :TOK, :] = (summed / total).T.astype(bf16)
        out[a, TOK:, :] = extra_rows(three_terms(top * LN2 + jnp.log(total)))


def backward_kernel(place, own, halo, grads, forward_out, rest, grad_kv, ahead):
    off = jnp.where(place[0] == 0, FAR, 0.0).astype(f32)
    scale2 = SCALE * LOG2E
    key_index = lax.broadcasted_iota(jnp.int32, (TOK, TOK), 0)
    rest[:, TOK:, :] = forward_out[...]

    extra = [own[i, EXT:, :].astype(f32) for i in range(4)]
    delta = [row_of(grads[i, TOK:GRAD_ROWS, :].astype(f32), 0, 3) for i in range(4)]
    totals = [row_of(extra[i], 2, 3) * LOG2E for i in range(4)]
    grad_query = [None] * 4
    for b in range(7):
        key = part(own, halo, b, K_B, TOK)
        value = part(own, halo, b, V_B, TOK)
        key_turned = key.T
        grad_key = grad_value = None
        for a in range(max(b - HALO, 0), min(b, HALO) + 1):
            query = own[a, Q_B : Q_B + TOK, :]
            grad = grads[a, :TOK, :]
            total = totals[a] + off if b < HALO else totals[a]
            weights = jnp.exp2(nt(key, query) * scale2 - total)
            if a + HALO == b:
                ends = row_of(extra[a], 1).astype(jnp.int32)
                weights = jnp.where(key_index <= ends, weights, 0.0)
            scores = (weights * (nt(value, grad) - delta[a])).astype(bf16)
            dk, dv = nn(scores, query), nn(weights.astype(bf16), grad)
            grad_key = dk if grad_key is None else grad_key + dk
            grad_value = dv if grad_value is None else grad_value + dv
            dq = nn(key_turned, scores)
            grad_query[a] = dq if grad_query[a] is None else grad_query[a] + dq
        if b <= HALO:
            grad_kv[b, :TOK, :] = grad_key * SCALE
            grad_kv[b, TOK:, :] = grad_value
        else:
            ahead[b - 4, :TOK, :] = (grad_key * SCALE).astype(bf16)
            ahead[b - 4, TOK:, :] = grad_value.astype(bf16)
    for a in range(4):
        rest[a, :TOK, :] = (grad_query[a] * SCALE).T.astype(bf16)


def finish_kernel(place, rest, grad_kv, behind, out0, out1, out2, out3, out):
    for b in range(4):
        total = grad_kv[b]
        if b < HALO:
            total = total + behind[b].astype(f32)
        out[b, : 2 * TOK, :] = total.astype(bf16)
        out[b, 2 * TOK :, :] = rest[b]
    for distance, ref in enumerate((out0, out1, out2, out3)):
        ref[...] = out[lax.rem(place[1] + distance, 4)]


def unpack_kernel(place, in0, in1, in2, in3, attended, log_total, grad_query, grad_keys, grad_values):
    for distance, ref in enumerate((in0, in1, in2, in3)):
        head = lax.rem(place[1] + 4 - distance, 4)
        lanes = pl.ds(pl.multiple_of(head * HDIM, HDIM), HDIM)
        grad_keys[:, lanes] = ref[:TOK, :].astype(f32)
        grad_values[:, lanes] = ref[TOK : 2 * TOK, :].astype(f32)
        grad_query[:, lanes] = ref[2 * TOK : 3 * TOK, :].astype(f32)
        attended[:, lanes] = ref[3 * TOK : 4 * TOK, :]
        extra = ref[4 * TOK :, :].astype(f32)
        log_total[pl.ds(head, 1), :] = row_of(extra, 0, 3)


def grad_kernel(place, c0, o0, c1, o1, c2, o2, c3, o3, weight, attn, out):
    y_lo, y_hi, core = place[0], place[1], place[2]
    width = 4 * HDIM
    half = attn[:, pl.ds(pl.multiple_of(y_lo * TOK, TOK), TOK)].T
    half_far = c1[:, width:].T
    total = None
    for hi, side, near, far in ((0, 0, c0, c1), (0, 1, o0, o1), (1, 0, c2, c3), (1, 1, o2, o3)):
        y = y_hi + hi - 2 * y_hi * hi
        c = core + side - 2 * core * side
        group = 2 * y + c
        cot = near[...]
        term = nt(cot, weight[:, pl.ds(pl.multiple_of(group * width, width), width)])
        total = term if total is None else total + term
        product = (nn(half, cot) + nn(half_far, far[:, :width])).astype(bf16)
        for j in range(4):
            rows = pl.ds(GRAD_ROWS + j * TOK, TOK)
            out[group, rows, :] = product[:, j * HDIM : (j + 1) * HDIM]
    grad = total.astype(bf16)
    for head in range(4):
        lanes = slice(head * HDIM, (head + 1) * HDIM)
        product = grad[:, lanes].astype(f32) * attn[:, lanes].astype(f32)
        out[head, :TOK, :] = grad[:, lanes]
        out[head, TOK:GRAD_ROWS, :] = extra_rows(three_terms(product.T.sum(0, keepdims=True)))


def sum_kernel(parts, out):
    total = parts[0, GRAD_ROWS:, :].astype(f32)
    for i in range(1, 4):
        total = total + parts[i, GRAD_ROWS:, :].astype(f32)
    out[...] = total.astype(bf16)


def last_sum_kernel(parts, out):
    total = parts[0].astype(f32)
    for i in range(1, 8):
        total = total + parts[i].astype(f32)
    total = total.astype(bf16)
    for i in range(8):
        out[i] = total


def assemble_kernel(place, *refs):
    out = refs[-1]
    for far in range(2):
        y = place[0] + far - 2 * place[0] * far
        rows = pl.ds(pl.multiple_of(y * TOK, TOK), TOK)
        for distance in range(4):
            x = lax.rem(place[1] + 4 - distance, 4)
            ref = refs[far * 4 + distance]
            for j in range(4):
                lanes = pl.ds(pl.multiple_of((x * 4 + j) * HDIM, HDIM), HDIM)
                out[rows, lanes] = ref[j * TOK : (j + 1) * TOK, :]


def across(value, axes):
    return lax.all_to_all(value, axes, 0, 0, tiled=True)


def diagonal(value):
    return lax.ppermute(value, ("yl", "yh"), [(0, 3), (1, 2), (2, 1), (3, 0)])


def along_x(value, distance):
    return lax.ppermute(value, "x", [(i, (i + distance) % 4) for i in range(4)])


def next_row(value):
    return lax.ppermute(value, ("yl", "z"), [(i, (i + 1) % 16) for i in range(16)])


def other(value, axis):
    return lax.ppermute(value, axis, [(0, 1), (1, 0)])


def body(
    frames_fwd,
    query_fwd,
    keys_fwd,
    values_fwd,
    frames_bwd,
    query_bwd,
    keys_bwd,
    values_bwd,
    attn_bwd,
    logsumexp_bwd,
    cotangent,
    out_weight,
):
    y_lo = lax.axis_index("yl")
    place = jnp.stack([y_lo, lax.axis_index("yh"), lax.axis_index("core")]).astype(jnp.int32)
    place_x = jnp.stack([lax.axis_index(("yl", "z")), lax.axis_index("x")]).astype(jnp.int32)

    packed, to_pair = call(
        pack_kernel,
        [pltpu.HBM((4, BLOCK_ROWS, HDIM), bf16), pltpu.HBM((TOK, 6 * HDIM), bf16)],
        1,
        place,
        *map(in_hbm, (query_fwd, keys_fwd, values_fwd, keys_bwd, values_bwd, query_bwd)),
        *map(in_hbm, (logsumexp_bwd, attn_bwd, cotangent)),
        in_hbm(frames_fwd.reshape(1, TOK)),
        in_hbm(frames_bwd.reshape(1, TOK)),
    )
    cots = [cotangent, other(to_pair, "yl"), other(cotangent, "yh"), diagonal(cotangent)]
    own = across(packed, "x")
    halo = next_row(own[1:, HALO_FROM:Q_B, :])

    pairs = [(c, other(c[:, : 4 * HDIM], "core")) for c in cots]
    grads_packed = call(
        grad_kernel,
        pltpu.HBM((4, GRAD_ROWS + 4 * TOK, HDIM), bf16),
        1,
        place,
        *sum(pairs, ()),
        in_hbm(out_weight),
        in_hbm(attn_bwd),
    )
    grads = across(grads_packed, "x")
    grads_own = grads[:, :GRAD_ROWS, :]

    summed = call(sum_kernel, shape(4 * TOK, HDIM), 0, grads)
    parts = across(summed.reshape(8, HDIM, HDIM), "z")
    forward_out = call(forward_kernel, shape(4, GRAD_ROWS, HDIM), 1, place_x, own, halo)
    parts, forward_out = lax.optimization_barrier((parts, forward_out))
    chunks = call(last_sum_kernel, pltpu.HBM((8, HDIM, HDIM), bf16), 0, parts)
    gathered = across(chunks, "z").reshape(4 * TOK, HDIM)
    rest, grad_kv, ahead = call(
        backward_kernel,
        [shape(4, TOK + GRAD_ROWS, HDIM), shape(4, 2 * TOK, HDIM, dtype=f32), pltpu.HBM((HALO, 2 * TOK, HDIM), bf16)],
        1,
        place_x,
        own,
        halo,
        grads_own,
        forward_out,
    )
    behind = next_row(ahead)
    gathered, ahead = lax.optimization_barrier((gathered, ahead))
    row_parts = [gathered] + [along_x(gathered, d) for d in range(1, 4)]
    far_parts = [other(part, "yl") for part in row_parts]
    behind, row_parts, far_parts[0] = lax.optimization_barrier((behind, row_parts, far_parts[0]))
    outs = call(
        finish_kernel,
        [pltpu.HBM((BACK_ROWS, HDIM), bf16)] * 4,
        1,
        place_x,
        rest,
        grad_kv,
        behind,
        scratch=[pltpu.VMEM((4, BACK_ROWS, HDIM), bf16)],
    )
    back = [outs[0]] + [along_x(outs[d], d) for d in range(1, 4)]
    attended, log_total, grad_query, grad_keys, grad_values = call(
        unpack_kernel,
        [
            shape(TOK, 4 * HDIM),
            shape(4, TOK, dtype=f32),
            shape(TOK, 4 * HDIM, dtype=f32),
            shape(TOK, 4 * HDIM, dtype=f32),
            shape(TOK, 4 * HDIM, dtype=f32),
        ],
        1,
        place_x,
        *back,
    )
    place_xy = jnp.stack([y_lo, lax.axis_index("x")]).astype(jnp.int32)
    grad_weight = call(assemble_kernel, shape(2 * TOK, 16 * HDIM), 1, place_xy, *row_parts, *far_parts)
    return (attended, log_total, grad_query, grad_keys, grad_values, grad_weight)


def solution(mesh):
    fine = Mesh(mesh.devices.reshape(2, 8, 4, 2, 2), ("yl", "z", "x", "yh", "core"))
    ctx, dp = ("yl", "z", "x"), ("yh", "core")
    in_specs = (
        P(ctx),
        P(ctx, dp),
        P(ctx, dp),
        P(ctx, dp),
        P(ctx),
        P(ctx, dp),
        P(ctx, dp),
        P(ctx, dp),
        P(ctx, dp),
        P(dp, ctx),
        P(ctx, dp),
        P(dp, None),
    )
    out_specs = (
        P(ctx, dp),
        P(dp, ctx),
        P(ctx, dp),
        P(ctx, dp),
        P(ctx, dp),
        P(dp, None),
    )
    return jax.shard_map(body, mesh=fine, in_specs=in_specs, out_specs=out_specs, check_vma=False)
```

time: 159 us -> 127 us (0.80)
  blocking collectives: 35.3 us -> 0 us
  starting transfers between devices: 28.7 us -> 41.4 us
  local copies, waits for them, and re-layouts: 13 us -> 2.82 us
  Pallas kernels: 17.6 us -> 24.4 us
  waiting for transfers between devices: 59.5 us -> 56.5 us
  other arithmetic: 1.83 us -> 0.23 us
    all_to_all x2 -> x0, blocking collectives: 35.3 us -> none  [across(): return lax.all_to_all(value, axes, 0, 0, tiled=True)]
    ppermute x5 -> x10, waiting for transfers between devices: 6.04 us -> 25.8 us  [other(): return lax.ppermute(value, axis, [(0, 1), (1, 0)])]
    all_to_all x4, waiting for transfers between devices: 35.5 us -> 25 us  [across(): return lax.all_to_all(value, axes, 0, 0, tiled=True)]
    ppermute x5 -> x10, starting transfers between devices: 0.41 us -> 7.97 us  [other(): return lax.ppermute(value, axis, [(0, 1), (1, 0)])]
    unnamed x24 -> x10, local copies, waits for them, and re-layouts: 9.05 us -> 1.86 us
    pallas_call x8 -> x9, Pallas kernels: 17.6 us -> 24.4 us  [call(): pl.pallas_call(kernel, out_shape=out_shape, in_specs=[pl.BlockSpec(memory...]
    ppermute x3 -> x7, waiting for transfers between devices: 12.3 us -> 5.72 us  [the longest x6 5.71 us: along_x(): return lax.ppermute(value, 'x', [(i, (i + distance) % 4) for i in range(4)])]
    ppermute x2, waiting for transfers between devices: 5.6 us -> 0.01 us  [next_row(): lax.ppermute(value, ('yl', 'z'), [(i, (i + 1) % 16) for i in range(16)])]
  transfers between devices with their start and end apart: 14 -> 23, of which waited for: 7 -> 11; matrix products, arithmetic and copies ran while one was open for 2% -> 1% of each run, Pallas kernels for 9% -> 15%
where the time goes in v2:
time: 127 us; the launch traced here: 126 us
  waiting for transfers between devices  56.5 us (44%)
  starting transfers between devices  41.4 us (33%)
  Pallas kernels  24.4 us (19%)
  local copies, waits for them, and re-layouts  2.82 us (2%)
    ppermute x10, waiting for transfers between devices, other(): return lax.ppermute(value, axis, [(0, 1), (1, 0)])  25.8 us
    all_to_all x4, waiting for transfers between devices, across(): return lax.all_to_all(value, axes, 0, 0, tiled=True)  25 us
    pallas_call x9, Pallas kernels, call(): pl.pallas_call(kernel, out_shape=out_shape, in_specs=[pl.BlockSpec(memory...  24.4 us
    all_to_all x4, starting transfers between devices, across(): return lax.all_to_all(value, axes, 0, 0, tiled=True)  22.8 us
    ppermute x10, starting transfers between devices, other(): return lax.ppermute(value, axis, [(0, 1), (1, 0)])  7.97 us
    ppermute x6, starting transfers between devices, along_x(): return lax.ppermute(value, 'x', [(i, (i + distance) % 4) for i in range(4)])  7.23 us
    ppermute x6, waiting for transfers between devices, along_x(): return lax.ppermute(value, 'x', [(i, (i + distance) % 4) for i in range(4)])  5.71 us
  transfers between devices with their start and end apart: 23, of which 11 were waited for; matrix products, arithmetic and copies ran while one was open for 1% of the time, Pallas kernels for 15%

profile of v2, /device:TPU:2, one launch (start us, length us, event | category | flops | bytes accessed | tf_op | source)
XLA Modules:
  0.0 126.1 jit_solution(2988491541963929163)
XLA Ops:
  0.6 0.1 pad_add_fusion.1.place
  0.7 3.2 %shard_map.163 = (bf16[4,1552,128]{2,1,0:T(8,128)(2,1)}, bf16[256,768]{1,0:T(8,128)(2,1)}) custom-call(s32[3]{0:T(128)S(1)} %pad_add_fusion.1.place, bf16[256,512]{1,0:T(8,128)(2,1)} %qf.1, bf16[256,512]{1,0:T(8,128)(2,1)} %kf.1, bf16[256,512]{1,0:T(8,128)(2,1)} %vf.1, bf16[256,512]{1,0:T(8,128)(2,1)} %kb.1, bf16[256,512]{1,0:T(8,128)(2,1)} %vb.1, ...), custom_call_target="tpu_custom_call" | custom-call | tf_op jit(solution)/shard_map/pallas_call | solution.py:71
  3.9 5.9 %all-to-all-start = ((bf16[4,1552,128]{2,1,0:T(8,128)(2,1)}), bf16[4,1552,128]{2,1,0:T(8,128)(2,1)S(1)}, u32[]{:S(2)}, u32[]{:S(2)}) async-start(bf16[4,1552,128]{2,1,0:T(8,128)(2,1)} %get-tuple-element.29), calls=%async_computation | async-start | bytes 3178496 | tf_op jit(solution)/shard_map/all_to_all | solution.py:259
  9.8 0.6 collective-permute-start.2
  10.4 2.9 %collective-permute-start.4 = (bf16[256,512]{1,0:T(8,128)(2,1)S(1)}, bf16[256,512]{1,0:T(8,128)(2,1)S(1)}, u32[]{:S(2)}, u32[]{:S(2)}) collective-permute-start(bf16[256,512]{1,0:T(8,128)(2,1)S(1)} %copy-done), channel_id=1, source_target_pairs={{0,2},{2,0},{1,3},{3,1},{4,6},{6,4},{5,7},{7,5},{8,10},{10,8},{9,1... | collective-permute-start | bytes 786440 | tf_op jit(solution)/shard_map/ppermute | solution.py:275
  13.3 1.2 collective-permute-start.6
  14.5 12.7 %collective-permute-done.4.c2 = bf16[256,512]{1,0:T(8,128)(2,1)S(1)} collective-permute-done((bf16[256,512]{1,0:T(8,128)(2,1)S(1)}, bf16[256,512]{1,0:T(8,128)(2,1)S(1)}, u32[]{:S(2)}, u32[]{:S(2)}) %collective-permute-start.4) | collective-permute-done | bytes 262176 | tf_op jit(solution)/shard_map/ppermute | solution.py:275
  27.2 0.0 collective-permute-start.5
  27.2 0.0 collective-permute-done.6.c3
  27.2 0.5 collective-permute-start.7
  27.8 0.1 collective-permute-start.3
  27.9 0.9 collective-permute-done.5.o2
  28.8 0.4 collective-permute-done.7.o3
  29.1 0.4 collective-permute-done.3.o1
  29.5 4.0 %shard_map.164 = bf16[4,1296,128]{2,1,0:T(8,128)(2,1)} custom-call(s32[3]{0:T(128)S(1)} %pad_add_fusion.1.place, bf16[256,512]{1,0:T(8,128)(2,1)S(1)} %copy-done, bf16[256,512]{1,0:T(8,128)(2,1)S(1)} %collective-permute-done.1.o0, bf16[256,768]{1,0:T(8,128)(2,1)S(1)} %collective-permute-done.2.c1, bf16[256,512]{1,0:T(8,128)(2,1)S(1)} %collective-permute-done.3.o1, ...), custom_call_target="tpu_custom_call" | custom-call | tf_op jit(solution)/shard_map/pallas_call | solution.py:71
  33.5 4.8 %all-to-all-start.1 = ((bf16[4,1296,128]{2,1,0:T(8,128)(2,1)}), bf16[4,1296,128]{2,1,0:T(8,128)(2,1)S(1)}, u32[]{:S(2)}, u32[]{:S(2)}) async-start(bf16[4,1296,128]{2,1,0:T(8,128)(2,1)} %shard_map.164), calls=%async_computation.1 | async-start | bytes 2654208 | tf_op jit(solution)/shard_map/all_to_all | solution.py:259
  38.3 0.9 slice.12
  39.2 1.9 %collective-permute-start = (bf16[3,1024,128]{2,1,0:T(8,128)(2,1)}, bf16[3,1024,128]{2,1,0:T(8,128)(2,1)}, u32[]{:S(2)}, u32[]{:S(2)}) collective-permute-start(bf16[3,1024,128]{2,1,0:T(8,128)(2,1)} %slice.12), channel_id=1, source_target_pairs={{0,16},{16,32},{32,48},{48,64},{64,80},{80,96},{96,112},{112,128},... | collective-permute-start | bytes 2359304 | tf_op jit(solution)/shard_map/ppermute | solution.py:271
  41.2 14.1 %all-to-all-done.1.parts = bf16[4,1296,128]{2,1,0:T(8,128)(2,1)S(1)} async-done(((bf16[4,1296,128]{2,1,0:T(8,128)(2,1)}), bf16[4,1296,128]{2,1,0:T(8,128)(2,1)S(1)}, u32[]{:S(2)}, u32[]{:S(2)}) %all-to-all-start.1) | async-done | bytes 1327136 | tf_op jit(solution)/shard_map/all_to_all | solution.py:259
  55.2 0.8 shard_map.165
  56.1 8.5 %all-to-all-start.2 = ((bf16[8,128,128]{2,1,0:T(8,128)(2,1)}), bf16[8,128,128]{2,1,0:T(8,128)(2,1)S(1)}, u32[]{:S(2)}, u32[]{:S(2)}) async-start(bf16[8,128,128]{2,1,0:T(8,128)(2,1)} %bitcast.7), calls=%async_computation.2 | async-start | bytes 524288 | tf_op jit(solution)/shard_map/all_to_all | solution.py:259
  64.5 0.1 pad_add_fusion.place
  64.6 3.5 %shard_map.166.forward_out = bf16[4,272,128]{2,1,0:T(8,128)(2,1)S(1)} custom-call(s32[2]{0:T(128)S(1)} %pad_add_fusion.place, bf16[4,1552,128]{2,1,0:T(8,128)(2,1)S(1)} %all-to-all-done.own, bf16[3,1024,128]{2,1,0:T(8,128)(2,1)} %collective-permute-done.halo), custom_call_target="tpu_custom_call" | custom-call | tf_op jit(solution)/shard_map/pallas_call | solution.py:71
  68.1 7.5 %all-to-all-done.2.parts = bf16[8,128,128]{2,1,0:T(8,128)(2,1)S(1)} async-done(((bf16[8,128,128]{2,1,0:T(8,128)(2,1)}), bf16[8,128,128]{2,1,0:T(8,128)(2,1)S(1)}, u32[]{:S(2)}, u32[]{:S(2)}) %all-to-all-start.2) | async-done | bytes 262176 | tf_op jit(solution)/shard_map/all_to_all | solution.py:259
  75.7 0.7 shard_map.168
  76.4 3.6 %all-to-all-start.3 = ((bf16[8,128,128]{2,1,0:T(8,128)(2,1)}), bf16[8,128,128]{2,1,0:T(8,128)(2,1)S(1)}, u32[]{:S(2)}, u32[]{:S(2)}) async-start(bf16[8,128,128]{2,1,0:T(8,128)(2,1)} %shard_map.168), calls=%async_computation.3 | async-start | bytes 524288 | tf_op jit(solution)/shard_map/all_to_all | solution.py:259
  80.0 6.1 %shard_map.167 = (bf16[4,528,128]{2,1,0:T(8,128)(2,1)S(1)}, f32[4,512,128]{2,1,0:T(8,128)S(1)}, bf16[3,512,128]{2,1,0:T(8,128)(2,1)}) custom-call(s32[2]{0:T(128)S(1)} %pad_add_fusion.place, bf16[4,1552,128]{2,1,0:T(8,128)(2,1)S(1)} %all-to-all-done.own, bf16[3,1024,128]{2,1,0:T(8,128)(2,1)} %collective-permute-done.halo, ...), custom_call_target="tpu_custom_call" | custom-call | tf_op jit(solution)/shard_map/pallas_call | solution.py:71
  86.1 0.8 copy-done.1
  86.9 3.4 %all-to-all-done.3 = bf16[8,128,128]{2,1,0:T(8,128)(2,1)S(1)} async-done(((bf16[8,128,128]{2,1,0:T(8,128)(2,1)}), bf16[8,128,128]{2,1,0:T(8,128)(2,1)S(1)}, u32[]{:S(2)}, u32[]{:S(2)}) %all-to-all-start.3) | async-done | bytes 262176 | tf_op jit(solution)/shard_map/all_to_all | solution.py:259
  90.3 1.4 %collective-permute-start.11 = (bf16[1024,128]{1,0:T(8,128)(2,1)S(1)}, bf16[1024,128]{1,0:T(8,128)(2,1)S(1)}, u32[]{:S(2)}, u32[]{:S(2)}) collective-permute-start(bf16[1024,128]{1,0:T(8,128)(2,1)S(1)} %bitcast.9), channel_id=1, source_target_pairs={{0,12},{4,0},{8,4},{12,8},{1,13},{5,1},{9,5},{13,9},{2,14},{6,2},{... | collective-permute-start | bytes 786440 | tf_op jit(solution)/shard_map/ppermute | solution.py:267
  91.7 0.3 collective-permute-start.8
  92.0 0.1 collective-permute-start.12
  92.1 0.3 collective-permute-start.10
  92.4 2.3 %collective-permute-start.9 = (bf16[1024,128]{1,0:T(8,128)(2,1)S(1)}, bf16[1024,128]{1,0:T(8,128)(2,1)S(1)}, u32[]{:S(2)}, u32[]{:S(2)}) collective-permute-start(bf16[1024,128]{1,0:T(8,128)(2,1)S(1)} %bitcast.12), channel_id=1, source_target_pairs={{0,4},{4,8},{8,12},{12,0},{1,5},{5,9},{9,13},{13,1},{2,6},{6,10},{... | collective-permute-start | bytes 786440 | tf_op jit(solution)/shard_map/ppermute | solution.py:267
  94.8 5.7 %collective-permute-done.11.refs_3_ = bf16[1024,128]{1,0:T(8,128)(2,1)S(1)} collective-permute-done((bf16[1024,128]{1,0:T(8,128)(2,1)S(1)}, bf16[1024,128]{1,0:T(8,128)(2,1)S(1)}, u32[]{:S(2)}, u32[]{:S(2)}) %collective-permute-start.11) | collective-permute-done | bytes 262176 | tf_op jit(solution)/shard_map/ppermute | solution.py:267
  100.5 1.7 %collective-permute-start.18 = (bf16[1024,128]{1,0:T(8,128)(2,1)S(1)}, bf16[1024,128]{1,0:T(8,128)(2,1)S(1)}, u32[]{:S(2)}, u32[]{:S(2)}) collective-permute-start(bf16[1024,128]{1,0:T(8,128)(2,1)S(1)} %collective-permute-done.11.refs_3_), channel_id=1, source_target_pairs={{0,128},{128,0},{1,129},{129,1},{2,130},{130,2},{3,131},{131,3},{4... | collective-permute-start | bytes 786440 | tf_op jit(solution)/shard_map/ppermute | solution.py:275
  102.2 4.4 %collective-permute-done.12.refs_4_ = bf16[1024,128]{1,0:T(8,128)(2,1)S(1)} collective-permute-done((bf16[1024,128]{1,0:T(8,128)(2,1)S(1)}, bf16[1024,128]{1,0:T(8,128)(2,1)S(1)}, u32[]{:S(2)}, u32[]{:S(2)}) %collective-permute-start.12) | collective-permute-done | bytes 262176 | tf_op jit(solution)/shard_map/ppermute | solution.py:275
  106.6 1.0 copy-done.2
  107.6 1.7 %shard_map.169 = (bf16[1040,128]{1,0:T(8,128)(2,1)}, bf16[1040,128]{1,0:T(8,128)(2,1)}, bf16[1040,128]{1,0:T(8,128)(2,1)}, bf16[1040,128]{1,0:T(8,128)(2,1)}) custom-call(s32[2]{0:T(128)S(1)} %pad_add_fusion.place, bf16[4,528,128]{2,1,0:T(8,128)(2,1)S(1)} %copy-done.2, f32[4,512,128]{2,1,0:T(8,128)S(1)} %get-tuple-element.33.grad_kv, ...), custom_call_target="tpu_custom_call" | custom-call | tf_op jit(solution)/shard_map/pallas_call | solution.py:71
  109.3 0.9 collective-permute-start.13
  110.2 2.4 %collective-permute-start.14 = (bf16[1040,128]{1,0:T(8,128)(2,1)}, bf16[1040,128]{1,0:T(8,128)(2,1)S(1)}, u32[]{:S(2)}, u32[]{:S(2)}) collective-permute-start(bf16[1040,128]{1,0:T(8,128)(2,1)} %get-tuple-element.40), channel_id=1, source_target_pairs={{0,8},{4,12},{8,0},{12,4},{1,9},{5,13},{9,1},{13,5},{2,10},{6,14},... | collective-permute-start | bytes 798728 | tf_op jit(solution)/shard_map/ppermute | solution.py:267
  112.5 0.1 collective-permute-start.17
  112.7 1.9 %collective-permute-start.16 = (bf16[1024,128]{1,0:T(8,128)(2,1)S(1)}, bf16[1024,128]{1,0:T(8,128)(2,1)S(1)}, u32[]{:S(2)}, u32[]{:S(2)}) collective-permute-start(bf16[1024,128]{1,0:T(8,128)(2,1)S(1)} %collective-permute-done.9.refs_1_), channel_id=1, source_target_pairs={{0,128},{128,0},{1,129},{129,1},{2,130},{130,2},{3,131},{131,3},{4... | collective-permute-start | bytes 786440 | tf_op jit(solution)/shard_map/ppermute | solution.py:275
  114.5 0.1 pad_add_fusion.2.place
  114.6 4.3 %collective-permute-done.17.refs_6_ = bf16[1024,128]{1,0:T(8,128)(2,1)S(1)} collective-permute-done((bf16[1024,128]{1,0:T(8,128)(2,1)S(1)}, bf16[1024,128]{1,0:T(8,128)(2,1)S(1)}, u32[]{:S(2)}, u32[]{:S(2)}) %collective-permute-start.17) | collective-permute-done | bytes 262176 | tf_op jit(solution)/shard_map/ppermute | solution.py:275
  118.9 2.8 %collective-permute-done.16.refs_5_ = bf16[1024,128]{1,0:T(8,128)(2,1)S(1)} collective-permute-done((bf16[1024,128]{1,0:T(8,128)(2,1)S(1)}, bf16[1024,128]{1,0:T(8,128)(2,1)S(1)}, u32[]{:S(2)}, u32[]{:S(2)}) %collective-permute-start.16) | collective-permute-done | bytes 262176 | tf_op jit(solution)/shard_map/ppermute | solution.py:275
  121.7 2.5 %shard_map.171 = bf16[512,2048]{1,0:T(8,128)(2,1)} custom-call(s32[2]{0:T(128)S(1)} %pad_add_fusion.2.place, bf16[1024,128]{1,0:T(8,128)(2,1)S(1)} %bitcast.13, bf16[1024,128]{1,0:T(8,128)(2,1)S(1)} %collective-permute-done.9.refs_1_, bf16[1024,128]{1,0:T(8,128)(2,1)S(1)} %collective-permute-done.10.refs_2_, ...), custom_call_target="tpu_custom_call" | custom-call | tf_op jit(solution)/shard_map/pallas_call | solution.py:71
  124.2 1.9 %shard_map.170 = (bf16[256,512]{1,0:T(8,128)(2,1)}, f32[4,256]{1,0:T(4,128)}, f32[256,512]{1,0:T(8,128)}, f32[256,512]{1,0:T(8,128)}, f32[256,512]{1,0:T(8,128)}) custom-call(s32[2]{0:T(128)S(1)} %pad_add_fusion.place, bf16[1040,128]{1,0:T(8,128)(2,1)S(1)} %copy-done.3, bf16[1040,128]{1,0:T(8,128)(2,1)S(1)} %collective-permute-done.13.in1, ...), custom_call_target="tpu_custom_call" | custom-call | tf_op jit(solution)/shard_map/pallas_call | solution.py:71
  (23 shorter events, 0.1 us)
Async XLA Ops:
  3.9 6.0 %copy-start.4 = (bf16[256,768]{1,0:T(8,128)(2,1)S(1)}, bf16[256,768]{1,0:T(8,128)(2,1)}, u32[]{:S(2)}) copy-start(bf16[256,768]{1,0:T(8,128)(2,1)} %get-tuple-element.30) | copy-start | bytes 1179652
  3.9 6.6 %copy-start = (bf16[256,512]{1,0:T(8,128)(2,1)S(1)}, bf16[256,512]{1,0:T(8,128)(2,1)}, u32[]{:S(2)}) copy-start(bf16[256,512]{1,0:T(8,128)(2,1)} %c0.1) | copy-start | bytes 786436
  3.9 29.6 %all-to-all-start = ((bf16[4,1552,128]{2,1,0:T(8,128)(2,1)}), bf16[4,1552,128]{2,1,0:T(8,128)(2,1)S(1)}, u32[]{:S(2)}, u32[]{:S(2)}) async-start(bf16[4,1552,128]{2,1,0:T(8,128)(2,1)} %get-tuple-element.29), calls=%async_computation | async-start | bytes 3178496 | tf_op jit(solution)/shard_map/all_to_all | solution.py:259
  9.8 17.9 %collective-permute-start.2 = (bf16[256,768]{1,0:T(8,128)(2,1)S(1)}, bf16[256,768]{1,0:T(8,128)(2,1)S(1)}, u32[]{:S(2)}, u32[]{:S(2)}) collective-permute-start(bf16[256,768]{1,0:T(8,128)(2,1)S(1)} %copy-done.4), channel_id=1, source_target_pairs={{0,128},{128,0},{1,129},{129,1},{2,130},{130,2},{3,131},{131,3},{4... | collective-permute-start | bytes 1179656 | tf_op jit(solution)/shard_map/ppermute | solution.py:275
  10.4 16.8 %collective-permute-start.4 = (bf16[256,512]{1,0:T(8,128)(2,1)S(1)}, bf16[256,512]{1,0:T(8,128)(2,1)S(1)}, u32[]{:S(2)}, u32[]{:S(2)}) collective-permute-start(bf16[256,512]{1,0:T(8,128)(2,1)S(1)} %copy-done), channel_id=1, source_target_pairs={{0,2},{2,0},{1,3},{3,1},{4,6},{6,4},{5,7},{7,5},{8,10},{10,8},{9,1... | collective-permute-start | bytes 786440 | tf_op jit(solution)/shard_map/ppermute | solution.py:275
  13.3 13.9 %collective-permute-start.6 = (bf16[256,512]{1,0:T(8,128)(2,1)S(1)}, bf16[256,512]{1,0:T(8,128)(2,1)S(1)}, u32[]{:S(2)}, u32[]{:S(2)}) collective-permute-start(bf16[256,512]{1,0:T(8,128)(2,1)S(1)} %copy-done), channel_id=1, source_target_pairs={{0,130},{2,128},{128,2},{130,0},{1,131},{3,129},{129,3},{131,1},{4... | collective-permute-start | bytes 786440 | tf_op jit(solution)/shard_map/ppermute | solution.py:263
  14.5 13.3 %collective-permute-start.1 = (bf16[256,512]{1,0:T(8,128)(2,1)S(1)}, bf16[256,512]{1,0:T(8,128)(2,1)S(1)}, u32[]{:S(2)}, u32[]{:S(2)}) collective-permute-start(bf16[256,512]{1,0:T(8,128)(2,1)S(1)} %copy-done), channel_id=1, source_target_pairs={{0,1},{1,0},{2,3},{3,2},{4,5},{5,4},{6,7},{7,6},{8,9},{9,8},{10,11... | collective-permute-start | bytes 786440 | tf_op jit(solution)/shard_map/ppermute | solution.py:275
  27.2 1.5 %collective-permute-start.5 = (bf16[256,512]{1,0:T(8,128)(2,1)S(1)}, bf16[256,512]{1,0:T(8,128)(2,1)S(1)}, u32[]{:S(2)}, u32[]{:S(2)}) collective-permute-start(bf16[256,512]{1,0:T(8,128)(2,1)S(1)} %collective-permute-done.4.c2), channel_id=1, source_target_pairs={{0,1},{1,0},{2,3},{3,2},{4,5},{5,4},{6,7},{7,6},{8,9},{9,8},{10,11... | collective-permute-start | bytes 786440 | tf_op jit(solution)/shard_map/ppermute | solution.py:275
  27.2 1.9 %collective-permute-start.7 = (bf16[256,512]{1,0:T(8,128)(2,1)S(1)}, bf16[256,512]{1,0:T(8,128)(2,1)S(1)}, u32[]{:S(2)}, u32[]{:S(2)}) collective-permute-start(bf16[256,512]{1,0:T(8,128)(2,1)S(1)} %collective-permute-done.6.c3), channel_id=1, source_target_pairs={{0,1},{1,0},{2,3},{3,2},{4,5},{5,4},{6,7},{7,6},{8,9},{9,8},{10,11... | collective-permute-start | bytes 786440 | tf_op jit(solution)/shard_map/ppermute | solution.py:275
  27.8 1.7 %collective-permute-start.3 = (bf16[256,512]{1,0:T(8,128)(2,1)S(1)}, bf16[256,512]{1,0:T(8,128)(2,1)S(1)}, u32[]{:S(2)}, u32[]{:S(2)}) collective-permute-start(bf16[256,512]{1,0:T(8,128)(2,1)S(1)} %slice.13), channel_id=1, source_target_pairs={{0,1},{1,0},{2,3},{3,2},{4,5},{5,4},{6,7},{7,6},{8,9},{9,8},{10,11... | collective-permute-start | bytes 786440 | tf_op jit(solution)/shard_map/ppermute | solution.py:275
  33.5 21.7 %all-to-all-start.1 = ((bf16[4,1296,128]{2,1,0:T(8,128)(2,1)}), bf16[4,1296,128]{2,1,0:T(8,128)(2,1)S(1)}, u32[]{:S(2)}, u32[]{:S(2)}) async-start(bf16[4,1296,128]{2,1,0:T(8,128)(2,1)} %shard_map.164), calls=%async_computation.1 | async-start | bytes 2654208 | tf_op jit(solution)/shard_map/all_to_all | solution.py:259
  39.2 25.4 %collective-permute-start = (bf16[3,1024,128]{2,1,0:T(8,128)(2,1)}, bf16[3,1024,128]{2,1,0:T(8,128)(2,1)}, u32[]{:S(2)}, u32[]{:S(2)}) collective-permute-start(bf16[3,1024,128]{2,1,0:T(8,128)(2,1)} %slice.12), channel_id=1, source_target_pairs={{0,16},{16,32},{32,48},{48,64},{64,80},{80,96},{96,112},{112,128},... | collective-permute-start | bytes 2359304 | tf_op jit(solution)/shard_map/ppermute | solution.py:271
  56.1 19.6 %all-to-all-start.2 = ((bf16[8,128,128]{2,1,0:T(8,128)(2,1)}), bf16[8,128,128]{2,1,0:T(8,128)(2,1)S(1)}, u32[]{:S(2)}, u32[]{:S(2)}) async-start(bf16[8,128,128]{2,1,0:T(8,128)(2,1)} %bitcast.7), calls=%async_computation.2 | async-start | bytes 524288 | tf_op jit(solution)/shard_map/all_to_all | solution.py:259
  76.4 13.9 %all-to-all-start.3 = ((bf16[8,128,128]{2,1,0:T(8,128)(2,1)}), bf16[8,128,128]{2,1,0:T(8,128)(2,1)S(1)}, u32[]{:S(2)}, u32[]{:S(2)}) async-start(bf16[8,128,128]{2,1,0:T(8,128)(2,1)} %shard_map.168), calls=%async_computation.3 | async-start | bytes 524288 | tf_op jit(solution)/shard_map/all_to_all | solution.py:259
  86.1 0.8 copy-start.1
  90.3 10.1 %collective-permute-start.11 = (bf16[1024,128]{1,0:T(8,128)(2,1)S(1)}, bf16[1024,128]{1,0:T(8,128)(2,1)S(1)}, u32[]{:S(2)}, u32[]{:S(2)}) collective-permute-start(bf16[1024,128]{1,0:T(8,128)(2,1)S(1)} %bitcast.9), channel_id=1, source_target_pairs={{0,12},{4,0},{8,4},{12,8},{1,13},{5,1},{9,5},{13,9},{2,14},{6,2},{... | collective-permute-start | bytes 786440 | tf_op jit(solution)/shard_map/ppermute | solution.py:267
  91.7 10.5 %collective-permute-start.8 = (bf16[3,512,128]{2,1,0:T(8,128)(2,1)}, bf16[3,512,128]{2,1,0:T(8,128)(2,1)S(1)}, u32[]{:S(2)}, u32[]{:S(2)}) collective-permute-start(bf16[3,512,128]{2,1,0:T(8,128)(2,1)} %get-tuple-element.34), channel_id=1, source_target_pairs={{0,16},{16,32},{32,48},{48,64},{64,80},{80,96},{96,112},{112,128},... | collective-permute-start | bytes 1179656 | tf_op jit(solution)/shard_map/ppermute | solution.py:271
  92.0 14.5 %collective-permute-start.12 = (bf16[1024,128]{1,0:T(8,128)(2,1)S(1)}, bf16[1024,128]{1,0:T(8,128)(2,1)S(1)}, u32[]{:S(2)}, u32[]{:S(2)}) collective-permute-start(bf16[1024,128]{1,0:T(8,128)(2,1)S(1)} %bitcast.10), channel_id=1, source_target_pairs={{0,128},{128,0},{1,129},{129,1},{2,130},{130,2},{3,131},{131,3},{4... | collective-permute-start | bytes 786440 | tf_op jit(solution)/shard_map/ppermute | solution.py:275
  92.1 14.4 %collective-permute-start.10 = (bf16[1024,128]{1,0:T(8,128)(2,1)S(1)}, bf16[1024,128]{1,0:T(8,128)(2,1)S(1)}, u32[]{:S(2)}, u32[]{:S(2)}) collective-permute-start(bf16[1024,128]{1,0:T(8,128)(2,1)S(1)} %bitcast.11), channel_id=1, source_target_pairs={{0,8},{4,12},{8,0},{12,4},{1,9},{5,13},{9,1},{13,5},{2,10},{6,14},... | collective-permute-start | bytes 786440 | tf_op jit(solution)/shard_map/ppermute | solution.py:267
  92.4 14.1 %collective-permute-start.9 = (bf16[1024,128]{1,0:T(8,128)(2,1)S(1)}, bf16[1024,128]{1,0:T(8,128)(2,1)S(1)}, u32[]{:S(2)}, u32[]{:S(2)}) collective-permute-start(bf16[1024,128]{1,0:T(8,128)(2,1)S(1)} %bitcast.12), channel_id=1, source_target_pairs={{0,4},{4,8},{8,12},{12,0},{1,5},{5,9},{9,13},{13,1},{2,6},{6,10},{... | collective-permute-start | bytes 786440 | tf_op jit(solution)/shard_map/ppermute | solution.py:267
  100.5 12.2 %collective-permute-start.18 = (bf16[1024,128]{1,0:T(8,128)(2,1)S(1)}, bf16[1024,128]{1,0:T(8,128)(2,1)S(1)}, u32[]{:S(2)}, u32[]{:S(2)}) collective-permute-start(bf16[1024,128]{1,0:T(8,128)(2,1)S(1)} %collective-permute-done.11.refs_3_), channel_id=1, source_target_pairs={{0,128},{128,0},{1,129},{129,1},{2,130},{130,2},{3,131},{131,3},{4... | collective-permute-start | bytes 786440 | tf_op jit(solution)/shard_map/ppermute | solution.py:275
  106.5 1.1 copy-start.2
  109.3 14.9 %collective-permute-start.13 = (bf16[1040,128]{1,0:T(8,128)(2,1)}, bf16[1040,128]{1,0:T(8,128)(2,1)S(1)}, u32[]{:S(2)}, u32[]{:S(2)}) collective-permute-start(bf16[1040,128]{1,0:T(8,128)(2,1)} %get-tuple-element.39), channel_id=1, source_target_pairs={{0,4},{4,8},{8,12},{12,0},{1,5},{5,9},{9,13},{13,1},{2,6},{6,10},{... | collective-permute-start | bytes 798728 | tf_op jit(solution)/shard_map/ppermute | solution.py:267
  110.2 14.0 %collective-permute-start.14 = (bf16[1040,128]{1,0:T(8,128)(2,1)}, bf16[1040,128]{1,0:T(8,128)(2,1)S(1)}, u32[]{:S(2)}, u32[]{:S(2)}) collective-permute-start(bf16[1040,128]{1,0:T(8,128)(2,1)} %get-tuple-element.40), channel_id=1, source_target_pairs={{0,8},{4,12},{8,0},{12,4},{1,9},{5,13},{9,1},{13,5},{2,10},{6,14},... | collective-permute-start | bytes 798728 | tf_op jit(solution)/shard_map/ppermute | solution.py:267
  112.5 11.6 %collective-permute-start.15 = (bf16[1040,128]{1,0:T(8,128)(2,1)}, bf16[1040,128]{1,0:T(8,128)(2,1)S(1)}, u32[]{:S(2)}, u32[]{:S(2)}) collective-permute-start(bf16[1040,128]{1,0:T(8,128)(2,1)} %get-tuple-element.41), channel_id=1, source_target_pairs={{0,12},{4,0},{8,4},{12,8},{1,13},{5,1},{9,5},{13,9},{2,14},{6,2},{... | collective-permute-start | bytes 798728 | tf_op jit(solution)/shard_map/ppermute | solution.py:267
  112.5 6.4 %collective-permute-start.17 = (bf16[1024,128]{1,0:T(8,128)(2,1)S(1)}, bf16[1024,128]{1,0:T(8,128)(2,1)S(1)}, u32[]{:S(2)}, u32[]{:S(2)}) collective-permute-start(bf16[1024,128]{1,0:T(8,128)(2,1)S(1)} %collective-permute-done.10.refs_2_), channel_id=1, source_target_pairs={{0,128},{128,0},{1,129},{129,1},{2,130},{130,2},{3,131},{131,3},{4... | collective-permute-start | bytes 786440 | tf_op jit(solution)/shard_map/ppermute | solution.py:275
  112.7 9.0 %collective-permute-start.16 = (bf16[1024,128]{1,0:T(8,128)(2,1)S(1)}, bf16[1024,128]{1,0:T(8,128)(2,1)S(1)}, u32[]{:S(2)}, u32[]{:S(2)}) collective-permute-start(bf16[1024,128]{1,0:T(8,128)(2,1)S(1)} %collective-permute-done.9.refs_1_), channel_id=1, source_target_pairs={{0,128},{128,0},{1,129},{129,1},{2,130},{130,2},{3,131},{131,3},{4... | collective-permute-start | bytes 786440 | tf_op jit(solution)/shard_map/ppermute | solution.py:275
  114.6 9.5 %copy-start.3 = (bf16[1040,128]{1,0:T(8,128)(2,1)S(1)}, bf16[1040,128]{1,0:T(8,128)(2,1)}, u32[]{:S(2)}) copy-start(bf16[1040,128]{1,0:T(8,128)(2,1)} %get-tuple-element.38.in0) | copy-start | bytes 798724

commit v3 on v2

--- a/solution.py
+++ b/solution.py
@@ -64,10 +64,12 @@
     return pltpu.with_memory_space_constraint(value, pltpu.HBM)
 
 
-def call(kernel, out_shape, n_smem, *args, scratch=()):
+def call(kernel, out_shape, n_smem, *args, scratch=(), raw_in=(), raw_out=False):
     spaces = [pltpu.SMEM] * n_smem + [pltpu.VMEM] * (len(args) - n_smem)
+    for i in raw_in:
+        spaces[i] = pltpu.HBM
     single = not isinstance(out_shape, (tuple, list))
-    out_space = pl.BlockSpec(memory_space=pltpu.VMEM)
+    out_space = pl.BlockSpec(memory_space=pltpu.HBM if raw_out else pltpu.VMEM)
     return pl.pallas_call(
         kernel,
         out_shape=out_shape,
@@ -88,17 +90,26 @@
     return seen.sum(0, keepdims=True) - 1.0
 
 
-def pack_kernel(place, qf, kf, vf, kb, vb, qb, lse, attn, cot, frames_fwd, frames_bwd, out, to_pair):
+def pack_kernel(
+    place, qf, kf, vf, kb, vb, qb, lse, attn, cot, frames_fwd, frames_bwd, out, to_pair, packed, paired, sems
+):
     far_half = pl.multiple_of((1 - place[0]) * TOK, TOK)
-    to_pair[:, : 4 * HDIM] = cot[...]
-    to_pair[:, 4 * HDIM :] = attn[:, pl.ds(far_half, TOK)]
+    paired[:, : 4 * HDIM] = cot[...]
+    paired[:, 4 * HDIM :] = attn[:, pl.ds(far_half, TOK)]
+    copies = [pltpu.make_async_copy(paired, to_pair, sems.at[4])]
+    copies[0].start()
     ends = [block_ends(frames_fwd[...].astype(f32)), block_ends(frames_bwd[...].astype(f32))]
     for head in range(4):
         lanes = slice(head * HDIM, (head + 1) * HDIM)
         for i, ref in enumerate((qf, kf, vf, kb, vb, qb)):
-            out[head, i * TOK : (i + 1) * TOK, :] = ref[:, lanes]
+            packed[head, i * TOK : (i + 1) * TOK, :] = ref[:, lanes]
         rows = ends + three_terms(lse[head : head + 1, :])
-        out[head, EXT:, :] = extra_rows(rows)
+        packed[head, EXT:, :] = extra_rows(rows)
+        copy = pltpu.make_async_copy(packed.at[head], out.at[head], sems.at[head])
+        copy.start()
+        copies.append(copy)
+    for copy in copies:
+        copy.wait()
 
 
 def part(own, halo, index, first, rows):
@@ -139,11 +150,13 @@
         out[a, TOK:, :] = extra_rows(three_terms(top * LN2 + jnp.log(total)))
 
 
-def backward_kernel(place, own, halo, grads, forward_out, rest, grad_kv, ahead):
+def backward_kernel(place, own, halo, g0, g1, g2, g3, forward_out, rest, grad_kv, ahead, grads):
     off = jnp.where(place[0] == 0, FAR, 0.0).astype(f32)
     scale2 = SCALE * LOG2E
     key_index = lax.broadcasted_iota(jnp.int32, (TOK, TOK), 0)
     rest[:, TOK:, :] = forward_out[...]
+    for distance, ref in enumerate((g0, g1, g2, g3)):
+        grads[lax.rem(place[1] + 4 - distance, 4)] = ref[...]
 
     extra = [own[i, EXT:, :].astype(f32) for i in range(4)]
     delta = [row_of(grads[i, TOK:GRAD_ROWS, :].astype(f32), 0, 3) for i in range(4)]
@@ -201,7 +214,7 @@
         log_total[pl.ds(head, 1), :] = row_of(extra, 0, 3)
 
 
-def grad_kernel(place, c0, o0, c1, o1, c2, o2, c3, o3, weight, attn, out):
+def grad_kernel(place, c0, o0, c1, o1, c2, o2, c3, o3, weight, attn, g0, g1, g2, g3, out, grads):
     y_lo, y_hi, core = place[0], place[1], place[2]
     width = 4 * HDIM
     half = attn[:, pl.ds(pl.multiple_of(y_lo * TOK, TOK), TOK)].T
@@ -211,25 +224,26 @@
         y = y_hi + hi - 2 * y_hi * hi
         c = core + side - 2 * core * side
         group = 2 * y + c
-        cot = near[...]
+        cot = near[:, :width]
         term = nt(cot, weight[:, pl.ds(pl.multiple_of(group * width, width), width)])
         total = term if total is None else total + term
         product = (nn(half, cot) + nn(half_far, far[:, :width])).astype(bf16)
         for j in range(4):
-            rows = pl.ds(GRAD_ROWS + j * TOK, TOK)
-            out[group, rows, :] = product[:, j * HDIM : (j + 1) * HDIM]
+            out[group, j * TOK : (j + 1) * TOK, :] = product[:, j * HDIM : (j + 1) * HDIM]
     grad = total.astype(bf16)
     for head in range(4):
         lanes = slice(head * HDIM, (head + 1) * HDIM)
         product = grad[:, lanes].astype(f32) * attn[:, lanes].astype(f32)
-        out[head, :TOK, :] = grad[:, lanes]
-        out[head, TOK:GRAD_ROWS, :] = extra_rows(three_terms(product.T.sum(0, keepdims=True)))
+        grads[head, :TOK, :] = grad[:, lanes]
+        grads[head, TOK:GRAD_ROWS, :] = extra_rows(three_terms(product.T.sum(0, keepdims=True)))
+    for distance, ref in enumerate((g0, g1, g2, g3)):
+        ref[...] = grads[lax.rem(place[3] + distance, 4)]
 
 
 def sum_kernel(parts, out):
-    total = parts[0, GRAD_ROWS:, :].astype(f32)
+    total = parts[0].astype(f32)
     for i in range(1, 4):
-        total = total + parts[i, GRAD_ROWS:, :].astype(f32)
+        total = total + parts[i].astype(f32)
     out[...] = total.astype(bf16)
 
 
@@ -243,16 +257,25 @@
 
 
 def assemble_kernel(place, *refs):
-    out = refs[-1]
+    parts, (out, whole, sems) = refs[:8], refs[8:]
+    copies = []
+    strip = TOK // 4
     for far in range(2):
         y = place[0] + far - 2 * place[0] * far
-        rows = pl.ds(pl.multiple_of(y * TOK, TOK), TOK)
-        for distance in range(4):
-            x = lax.rem(place[1] + 4 - distance, 4)
-            ref = refs[far * 4 + distance]
-            for j in range(4):
-                lanes = pl.ds(pl.multiple_of((x * 4 + j) * HDIM, HDIM), HDIM)
-                out[rows, lanes] = ref[j * TOK : (j + 1) * TOK, :]
+        for piece in range(4):
+            rows = pl.ds(pl.multiple_of(y * TOK + piece * strip, strip), strip)
+            for distance in range(4):
+                x = lax.rem(place[1] + 4 - distance, 4)
+                ref = parts[far * 4 + distance]
+                for j in range(4):
+                    lanes = pl.ds(pl.multiple_of((x * 4 + j) * HDIM, HDIM), HDIM)
+                    first = j * TOK + piece * strip
+                    whole[rows, lanes] = ref[first : first + strip, :]
+            copy = pltpu.make_async_copy(whole.at[rows], out.at[rows], sems.at[len(copies)])
+            copy.start()
+            copies.append(copy)
+    for copy in copies:
+        copy.wait()
 
 
 def across(value, axes):
@@ -290,7 +313,7 @@
     out_weight,
 ):
     y_lo = lax.axis_index("yl")
-    place = jnp.stack([y_lo, lax.axis_index("yh"), lax.axis_index("core")]).astype(jnp.int32)
+    place = jnp.stack([y_lo] + [lax.axis_index(axis) for axis in ("yh", "core", "x")]).astype(jnp.int32)
     place_x = jnp.stack([lax.axis_index(("yl", "z")), lax.axis_index("x")]).astype(jnp.int32)
 
     packed, to_pair = call(
@@ -302,39 +325,51 @@
         *map(in_hbm, (logsumexp_bwd, attn_bwd, cotangent)),
         in_hbm(frames_fwd.reshape(1, TOK)),
         in_hbm(frames_bwd.reshape(1, TOK)),
+        scratch=[
+            pltpu.VMEM((4, BLOCK_ROWS, HDIM), bf16),
+            pltpu.VMEM((TOK, 6 * HDIM), bf16),
+            pltpu.SemaphoreType.DMA((5,)),
+        ],
+        raw_out=True,
     )
     cots = [cotangent, other(to_pair, "yl"), other(cotangent, "yh"), diagonal(cotangent)]
     own = across(packed, "x")
     halo = next_row(own[1:, HALO_FROM:Q_B, :])
 
-    pairs = [(c, other(c[:, : 4 * HDIM], "core")) for c in cots]
-    grads_packed = call(
+    pairs = [(c, other(c, "core")) for c in cots]
+    *grads, product = call(
         grad_kernel,
-        pltpu.HBM((4, GRAD_ROWS + 4 * TOK, HDIM), bf16),
+        [pltpu.HBM((GRAD_ROWS, HDIM), bf16)] * 4 + [pltpu.HBM((4, 4 * TOK, HDIM), bf16)],
         1,
         place,
-        *sum(pairs, ()),
+        in_hbm(cotangent),
+        *sum(pairs, ())[1:],
         in_hbm(out_weight),
         in_hbm(attn_bwd),
-    )
-    grads = across(grads_packed, "x")
-    grads_own = grads[:, :GRAD_ROWS, :]
-
-    summed = call(sum_kernel, shape(4 * TOK, HDIM), 0, grads)
+        scratch=[pltpu.VMEM((4, GRAD_ROWS, HDIM), bf16)],
+    )
+    products = across(product, "x")
+    summed = call(sum_kernel, shape(4 * TOK, HDIM), 0, products)
+    grads = [grads[0]] + [along_x(grads[d], d) for d in range(1, 4)]
     parts = across(summed.reshape(8, HDIM, HDIM), "z")
     forward_out = call(forward_kernel, shape(4, GRAD_ROWS, HDIM), 1, place_x, own, halo)
-    parts, forward_out = lax.optimization_barrier((parts, forward_out))
+    parts, forward_out, grads = lax.optimization_barrier((parts, forward_out, grads))
     chunks = call(last_sum_kernel, pltpu.HBM((8, HDIM, HDIM), bf16), 0, parts)
     gathered = across(chunks, "z").reshape(4 * TOK, HDIM)
     rest, grad_kv, ahead = call(
         backward_kernel,
-        [shape(4, TOK + GRAD_ROWS, HDIM), shape(4, 2 * TOK, HDIM, dtype=f32), pltpu.HBM((HALO, 2 * TOK, HDIM), bf16)],
+        [
+            pltpu.HBM((4, TOK + GRAD_ROWS, HDIM), bf16),
+            pltpu.HBM((4, 2 * TOK, HDIM), f32),
+            pltpu.HBM((HALO, 2 * TOK, HDIM), bf16),
+        ],
         1,
         place_x,
         own,
         halo,
-        grads_own,
+        *map(in_hbm, grads),
         forward_out,
+        scratch=[pltpu.VMEM((4, GRAD_ROWS, HDIM), bf16)],
     )
     behind = next_row(ahead)
     gathered, ahead = lax.optimization_barrier((gathered, ahead))
@@ -346,8 +381,8 @@
         [pltpu.HBM((BACK_ROWS, HDIM), bf16)] * 4,
         1,
         place_x,
-        rest,
-        grad_kv,
+        in_hbm(rest),
+        in_hbm(grad_kv),
         behind,
         scratch=[pltpu.VMEM((4, BACK_ROWS, HDIM), bf16)],
     )
@@ -366,7 +401,16 @@
         *back,
     )
     place_xy = jnp.stack([y_lo, lax.axis_index("x")]).astype(jnp.int32)
-    grad_weight = call(assemble_kernel, shape(2 * TOK, 16 * HDIM), 1, place_xy, *row_parts, *far_parts)
+    grad_weight = call(
+        assemble_kernel,
+        shape(2 * TOK, 16 * HDIM),
+        1,
+        place_xy,
+        *row_parts,
+        *far_parts,
+        scratch=[pltpu.VMEM((2 * TOK, 16 * HDIM), bf16), pltpu.SemaphoreType.DMA((8,))],
+        raw_out=True,
+    )
     return (attended, log_total, grad_query, grad_keys, grad_values, grad_weight)
 
 

time: 127 us -> 124 us (0.976)
  waiting for transfers between devices: 56.5 us -> 50.1 us
  starting transfers between devices: 41.4 us -> 46.9 us
    all_to_all x4, waiting for transfers between devices: 25 us -> 18.7 us  [across(): return lax.all_to_all(value, axes, 0, 0, tiled=True)]
    ppermute x6 -> x9, starting transfers between devices: 7.23 us -> 12.7 us  [along_x(): return lax.ppermute(value, 'x', [(i, (i + distance) % 4) for i in range(4)])]
    ppermute x2, waiting for transfers between devices: 0.01 us -> 2.89 us  [next_row(): lax.ppermute(value, ('yl', 'z'), [(i, (i + 1) % 16) for i in range(16)])]
    ppermute x6 -> x9, waiting for transfers between devices: 5.71 us -> 3.21 us  [along_x(): return lax.ppermute(value, 'x', [(i, (i + distance) % 4) for i in range(4)])]
  transfers between devices with their start and end apart: 23 -> 26, of which waited for: 11 -> 13; matrix products, arithmetic and copies ran while one was open for 1% -> 1% of each run, Pallas kernels for 15% -> 15%
where the time goes in v3:
time: 124 us; the launch traced here: 123 us
  waiting for transfers between devices  50.1 us (40%)
  starting transfers between devices  46.9 us (38%)
  Pallas kernels  23.6 us (19%)
  local copies, waits for them, and re-layouts  1.66 us (1%)
    ppermute x10, waiting for transfers between devices, other(): return lax.ppermute(value, axis, [(0, 1), (1, 0)])  25.2 us
    pallas_call x9, Pallas kernels, call(): pl.pallas_call(kernel, out_shape=out_shape, in_specs=[pl.BlockSpec(memory...  23.6 us
    all_to_all x4, starting transfers between devices, across(): return lax.all_to_all(value, axes, 0, 0, tiled=True)  23.2 us
    all_to_all x4, waiting for transfers between devices, across(): return lax.all_to_all(value, axes, 0, 0, tiled=True)  18.7 us
    ppermute x9, starting transfers between devices, along_x(): return lax.ppermute(value, 'x', [(i, (i + distance) % 4) for i in range(4)])  12.7 us
    ppermute x10, starting transfers between devices, other(): return lax.ppermute(value, axis, [(0, 1), (1, 0)])  7.46 us
    ppermute x9, waiting for transfers between devices, along_x(): return lax.ppermute(value, 'x', [(i, (i + distance) % 4) for i in range(4)])  3.21 us
    ppermute x2, waiting for transfers between devices, next_row(): lax.ppermute(value, ('yl', 'z'), [(i, (i + 1) % 16) for i in range(16)])  2.89 us
  transfers between devices with their start and end apart: 26, of which 13 were waited for; matrix products, arithmetic and copies ran while one was open for 1% of the time, Pallas kernels for 15%

profile of v3, /device:TPU:2, one launch (start us, length us, event | category | flops | bytes accessed | tf_op | source)
XLA Modules:
  0.0 123.2 jit_solution(4074319484423968809)
XLA Ops:
  0.6 0.1 pad_add_fusion.1.place
  0.7 3.0 %shard_map.163 = (bf16[4,1552,128]{2,1,0:T(8,128)(2,1)}, bf16[256,768]{1,0:T(8,128)(2,1)}) custom-call(s32[4]{0:T(128)S(1)} %pad_add_fusion.1.place, bf16[256,512]{1,0:T(8,128)(2,1)} %qf.1, bf16[256,512]{1,0:T(8,128)(2,1)} %kf.1, bf16[256,512]{1,0:T(8,128)(2,1)} %vf.1, bf16[256,512]{1,0:T(8,128)(2,1)} %kb.1, bf16[256,512]{1,0:T(8,128)(2,1)} %vb.1, ...), custom_call_target="tpu_custom_call" | custom-call | tf_op jit(solution)/shard_map/pallas_call | solution.py:73
  3.7 5.9 %all-to-all-start = ((bf16[4,1552,128]{2,1,0:T(8,128)(2,1)}), bf16[4,1552,128]{2,1,0:T(8,128)(2,1)S(1)}, u32[]{:S(2)}, u32[]{:S(2)}) async-start(bf16[4,1552,128]{2,1,0:T(8,128)(2,1)} %get-tuple-element.38), calls=%async_computation | async-start | bytes 3178496 | tf_op jit(solution)/shard_map/all_to_all | solution.py:282
  9.7 0.6 collective-permute-start.2
  10.3 2.9 %collective-permute-start.4 = (bf16[256,512]{1,0:T(8,128)(2,1)S(1)}, bf16[256,512]{1,0:T(8,128)(2,1)S(1)}, u32[]{:S(2)}, u32[]{:S(2)}) collective-permute-start(bf16[256,512]{1,0:T(8,128)(2,1)S(1)} %copy-done.2), channel_id=1, source_target_pairs={{0,2},{2,0},{1,3},{3,1},{4,6},{6,4},{5,7},{7,5},{8,10},{10,8},{9,1... | collective-permute-start | bytes 786440 | tf_op jit(solution)/shard_map/ppermute | solution.py:298
  13.2 1.2 collective-permute-start.6
  14.4 7.4 %collective-permute-done.2.c1 = bf16[256,768]{1,0:T(8,128)(2,1)S(1)} collective-permute-done((bf16[256,768]{1,0:T(8,128)(2,1)S(1)}, bf16[256,768]{1,0:T(8,128)(2,1)S(1)}, u32[]{:S(2)}, u32[]{:S(2)}) %collective-permute-start.2) | collective-permute-done | bytes 393248 | tf_op jit(solution)/shard_map/ppermute | solution.py:298
  21.7 0.5 collective-permute-start.1
  22.2 4.8 %collective-permute-done.4.c2 = bf16[256,512]{1,0:T(8,128)(2,1)S(1)} collective-permute-done((bf16[256,512]{1,0:T(8,128)(2,1)S(1)}, bf16[256,512]{1,0:T(8,128)(2,1)S(1)}, u32[]{:S(2)}, u32[]{:S(2)}) %collective-permute-start.4) | collective-permute-done | bytes 262176 | tf_op jit(solution)/shard_map/ppermute | solution.py:298
  27.0 0.5 collective-permute-start.7
  27.6 1.0 collective-permute-done.5.o2
  28.6 0.4 collective-permute-done.7.o3
  29.0 4.2 %shard_map.164 = (bf16[272,128]{1,0:T(8,128)(2,1)}, bf16[272,128]{1,0:T(8,128)(2,1)}, bf16[272,128]{1,0:T(8,128)(2,1)}, bf16[272,128]{1,0:T(8,128)(2,1)}, bf16[4,1024,128]{2,1,0:T(8,128)(2,1)}) custom-call(s32[4]{0:T(128)S(1)} %pad_add_fusion.1.place, bf16[256,512]{1,0:T(8,128)(2,1)} %c0.1, bf16[256,512]{1,0:T(8,128)(2,1)S(1)} %collective-permute-done.1.o0, ...), custom_call_target="tpu_custom_call" | custom-call | tf_op jit(solution)/shard_map/pallas_call | solution.py:73
  33.1 4.8 %all-to-all-start.1 = ((bf16[4,1024,128]{2,1,0:T(8,128)(2,1)}), bf16[4,1024,128]{2,1,0:T(8,128)(2,1)S(1)}, u32[]{:S(2)}, u32[]{:S(2)}) async-start(bf16[4,1024,128]{2,1,0:T(8,128)(2,1)} %get-tuple-element.40), calls=%async_computation.1 | async-start | bytes 2097152 | tf_op jit(solution)/shard_map/all_to_all | solution.py:282
  37.9 0.9 slice.4
  38.8 1.9 %collective-permute-start = (bf16[3,1024,128]{2,1,0:T(8,128)(2,1)}, bf16[3,1024,128]{2,1,0:T(8,128)(2,1)S(1)}, u32[]{:S(2)}, u32[]{:S(2)}) collective-permute-start(bf16[3,1024,128]{2,1,0:T(8,128)(2,1)} %slice.4), channel_id=1, source_target_pairs={{0,16},{16,32},{32,48},{48,64},{64,80},{80,96},{96,112},{112,128},... | collective-permute-start | bytes 2359304 | tf_op jit(solution)/shard_map/ppermute | solution.py:294
  40.8 11.1 %all-to-all-done.1.parts = bf16[4,1024,128]{2,1,0:T(8,128)(2,1)S(1)} async-done(((bf16[4,1024,128]{2,1,0:T(8,128)(2,1)}), bf16[4,1024,128]{2,1,0:T(8,128)(2,1)S(1)}, u32[]{:S(2)}, u32[]{:S(2)}) %all-to-all-start.1) | async-done | bytes 1048608 | tf_op jit(solution)/shard_map/all_to_all | solution.py:282
  51.8 0.1 shard_map.165
  52.0 0.7 copy-done
  52.7 8.5 %all-to-all-start.2 = ((bf16[8,128,128]{2,1,0:T(8,128)(2,1)}), bf16[8,128,128]{2,1,0:T(8,128)(2,1)S(1)}, u32[]{:S(2)}, u32[]{:S(2)}) async-start(bf16[8,128,128]{2,1,0:T(8,128)(2,1)} %bitcast.14), calls=%async_computation.2 | async-start | bytes 524288 | tf_op jit(solution)/shard_map/all_to_all | solution.py:282
  61.2 3.5 %collective-permute-start.9 = (bf16[272,128]{1,0:T(8,128)(2,1)}, bf16[272,128]{1,0:T(8,128)(2,1)S(1)}, u32[]{:S(2)}, u32[]{:S(2)}) collective-permute-start(bf16[272,128]{1,0:T(8,128)(2,1)} %get-tuple-element.43), channel_id=1, source_target_pairs={{0,8},{4,12},{8,0},{12,4},{1,9},{5,13},{9,1},{13,5},{2,10},{6,14},... | collective-permute-start | bytes 208904 | tf_op jit(solution)/shard_map/ppermute | solution.py:290
  64.7 0.6 collective-permute-start.10
  65.2 0.1 pad_add_fusion.place
  65.3 2.9 %shard_map.166.forward_out = bf16[4,272,128]{2,1,0:T(8,128)(2,1)S(1)} custom-call(s32[2]{0:T(128)S(1)} %pad_add_fusion.place, bf16[4,1552,128]{2,1,0:T(8,128)(2,1)S(1)} %all-to-all-done.own, bf16[3,1024,128]{2,1,0:T(8,128)(2,1)S(1)} %collective-permute-done.halo), custom_call_target="tpu_custom_call" | custom-call | tf_op jit(solution)/shard_map/pallas_call | solution.py:73
  68.3 0.7 collective-permute-done.10.g3
  69.0 3.2 %all-to-all-done.2.parts = bf16[8,128,128]{2,1,0:T(8,128)(2,1)S(1)} async-done(((bf16[8,128,128]{2,1,0:T(8,128)(2,1)}), bf16[8,128,128]{2,1,0:T(8,128)(2,1)S(1)}, u32[]{:S(2)}, u32[]{:S(2)}) %all-to-all-start.2) | async-done | bytes 262176 | tf_op jit(solution)/shard_map/all_to_all | solution.py:282
  72.2 0.7 shard_map.168
  72.9 4.0 %all-to-all-start.3 = ((bf16[8,128,128]{2,1,0:T(8,128)(2,1)}), bf16[8,128,128]{2,1,0:T(8,128)(2,1)S(1)}, u32[]{:S(2)}, u32[]{:S(2)}) async-start(bf16[8,128,128]{2,1,0:T(8,128)(2,1)} %shard_map.168), calls=%async_computation.3 | async-start | bytes 524288 | tf_op jit(solution)/shard_map/all_to_all | solution.py:282
  77.0 6.1 %shard_map.167 = (bf16[4,528,128]{2,1,0:T(8,128)(2,1)}, f32[4,512,128]{2,1,0:T(8,128)}, bf16[3,512,128]{2,1,0:T(8,128)(2,1)}) custom-call(s32[2]{0:T(128)S(1)} %pad_add_fusion.place, bf16[4,1552,128]{2,1,0:T(8,128)(2,1)S(1)} %all-to-all-done.own, bf16[3,1024,128]{2,1,0:T(8,128)(2,1)S(1)} %collective-permute-done.halo, ...), custom_call_target="tpu_custom_call" | custom-call | tf_op jit(solution)/shard_map/pallas_call | solution.py:73
  83.1 4.5 %all-to-all-done.3 = bf16[8,128,128]{2,1,0:T(8,128)(2,1)S(1)} async-done(((bf16[8,128,128]{2,1,0:T(8,128)(2,1)}), bf16[8,128,128]{2,1,0:T(8,128)(2,1)S(1)}, u32[]{:S(2)}, u32[]{:S(2)}) %all-to-all-start.3) | async-done | bytes 262176 | tf_op jit(solution)/shard_map/all_to_all | solution.py:282
  87.6 0.8 collective-permute-start.14
  88.4 0.4 collective-permute-start.11
  88.8 0.1 collective-permute-start.15
  88.9 1.5 %collective-permute-start.13 = (bf16[1024,128]{1,0:T(8,128)(2,1)S(1)}, bf16[1024,128]{1,0:T(8,128)(2,1)S(1)}, u32[]{:S(2)}, u32[]{:S(2)}) collective-permute-start(bf16[1024,128]{1,0:T(8,128)(2,1)S(1)} %bitcast.11), channel_id=1, source_target_pairs={{0,8},{4,12},{8,0},{12,4},{1,9},{5,13},{9,1},{13,5},{2,10},{6,14},... | collective-permute-start | bytes 786440 | tf_op jit(solution)/shard_map/ppermute | solution.py:290
  90.4 2.0 %collective-permute-start.12 = (bf16[1024,128]{1,0:T(8,128)(2,1)S(1)}, bf16[1024,128]{1,0:T(8,128)(2,1)S(1)}, u32[]{:S(2)}, u32[]{:S(2)}) collective-permute-start(bf16[1024,128]{1,0:T(8,128)(2,1)S(1)} %bitcast.12), channel_id=1, source_target_pairs={{0,4},{4,8},{8,12},{12,0},{1,5},{5,9},{9,13},{13,1},{2,6},{6,10},{... | collective-permute-start | bytes 786440 | tf_op jit(solution)/shard_map/ppermute | solution.py:290
  92.4 2.5 %collective-permute-done.14.refs_3_ = bf16[1024,128]{1,0:T(8,128)(2,1)S(1)} collective-permute-done((bf16[1024,128]{1,0:T(8,128)(2,1)S(1)}, bf16[1024,128]{1,0:T(8,128)(2,1)S(1)}, u32[]{:S(2)}, u32[]{:S(2)}) %collective-permute-start.14) | collective-permute-done | bytes 262176 | tf_op jit(solution)/shard_map/ppermute | solution.py:290
  95.0 0.8 collective-permute-start.21
  95.7 2.9 %collective-permute-done.11.behind = bf16[3,512,128]{2,1,0:T(8,128)(2,1)S(1)} collective-permute-done((bf16[3,512,128]{2,1,0:T(8,128)(2,1)}, bf16[3,512,128]{2,1,0:T(8,128)(2,1)S(1)}, u32[]{:S(2)}, u32[]{:S(2)}) %collective-permute-start.11) | collective-permute-done | bytes 393248 | tf_op jit(solution)/shard_map/ppermute | solution.py:294
  98.6 4.6 %collective-permute-done.15.refs_4_ = bf16[1024,128]{1,0:T(8,128)(2,1)S(1)} collective-permute-done((bf16[1024,128]{1,0:T(8,128)(2,1)S(1)}, bf16[1024,128]{1,0:T(8,128)(2,1)S(1)}, u32[]{:S(2)}, u32[]{:S(2)}) %collective-permute-start.15) | collective-permute-done | bytes 262176 | tf_op jit(solution)/shard_map/ppermute | solution.py:298
  103.2 2.5 %shard_map.169 = (bf16[1040,128]{1,0:T(8,128)(2,1)}, bf16[1040,128]{1,0:T(8,128)(2,1)}, bf16[1040,128]{1,0:T(8,128)(2,1)}, bf16[1040,128]{1,0:T(8,128)(2,1)}) custom-call(s32[2]{0:T(128)S(1)} %pad_add_fusion.place, bf16[4,528,128]{2,1,0:T(8,128)(2,1)} %get-tuple-element.50.rest, f32[4,512,128]{2,1,0:T(8,128)} %get-tuple-element.51.grad_kv, ...), custom_call_target="tpu_custom_call" | custom-call | tf_op jit(solution)/shard_map/pallas_call | solution.py:73
  105.7 0.8 collective-permute-start.16
  106.5 3.4 %collective-permute-start.17 = (bf16[1040,128]{1,0:T(8,128)(2,1)}, bf16[1040,128]{1,0:T(8,128)(2,1)S(1)}, u32[]{:S(2)}, u32[]{:S(2)}) collective-permute-start(bf16[1040,128]{1,0:T(8,128)(2,1)} %get-tuple-element.58), channel_id=1, source_target_pairs={{0,8},{4,12},{8,0},{12,4},{1,9},{5,13},{9,1},{13,5},{2,10},{6,14},... | collective-permute-start | bytes 798728 | tf_op jit(solution)/shard_map/ppermute | solution.py:290
  110.0 0.4 collective-permute-start.20
  110.4 1.6 %collective-permute-start.19 = (bf16[1024,128]{1,0:T(8,128)(2,1)S(1)}, bf16[1024,128]{1,0:T(8,128)(2,1)S(1)}, u32[]{:S(2)}, u32[]{:S(2)}) collective-permute-start(bf16[1024,128]{1,0:T(8,128)(2,1)S(1)} %collective-permute-done.12.refs_1_), channel_id=1, source_target_pairs={{0,128},{128,0},{1,129},{129,1},{2,130},{130,2},{3,131},{131,3},{4... | collective-permute-start | bytes 786440 | tf_op jit(solution)/shard_map/ppermute | solution.py:298
  112.1 4.3 %collective-permute-done.20.refs_6_ = bf16[1024,128]{1,0:T(8,128)(2,1)S(1)} collective-permute-done((bf16[1024,128]{1,0:T(8,128)(2,1)S(1)}, bf16[1024,128]{1,0:T(8,128)(2,1)S(1)}, u32[]{:S(2)}, u32[]{:S(2)}) %collective-permute-start.20) | collective-permute-done | bytes 262176 | tf_op jit(solution)/shard_map/ppermute | solution.py:298
  116.4 2.8 %collective-permute-done.19.refs_5_ = bf16[1024,128]{1,0:T(8,128)(2,1)S(1)} collective-permute-done((bf16[1024,128]{1,0:T(8,128)(2,1)S(1)}, bf16[1024,128]{1,0:T(8,128)(2,1)S(1)}, u32[]{:S(2)}, u32[]{:S(2)}) %collective-permute-start.19) | collective-permute-done | bytes 262176 | tf_op jit(solution)/shard_map/ppermute | solution.py:298
  119.2 2.0 %shard_map.171 = bf16[512,2048]{1,0:T(8,128)(2,1)} custom-call(s32[2]{0:T(128)S(1)} %pad_add_fusion.2.place, bf16[1024,128]{1,0:T(8,128)(2,1)S(1)} %bitcast.13, bf16[1024,128]{1,0:T(8,128)(2,1)S(1)} %collective-permute-done.12.refs_1_, bf16[1024,128]{1,0:T(8,128)(2,1)S(1)} %collective-permute-done.13.refs_2_, ...), custom_call_target="tpu_custom_call" | custom-call | tf_op jit(solution)/shard_map/pallas_call | solution.py:73
  121.2 1.9 %shard_map.170 = (bf16[256,512]{1,0:T(8,128)(2,1)}, f32[4,256]{1,0:T(4,128)}, f32[256,512]{1,0:T(8,128)}, f32[256,512]{1,0:T(8,128)}, f32[256,512]{1,0:T(8,128)}) custom-call(s32[2]{0:T(128)S(1)} %pad_add_fusion.place, bf16[1040,128]{1,0:T(8,128)(2,1)S(1)} %copy-done.1, bf16[1040,128]{1,0:T(8,128)(2,1)S(1)} %collective-permute-done.16.in1, ...), custom_call_target="tpu_custom_call" | custom-call | tf_op jit(solution)/shard_map/pallas_call | solution.py:73
  (33 shorter events, 0.2 us)
Async XLA Ops:
  3.7 6.0 %copy-start.6 = (bf16[256,768]{1,0:T(8,128)(2,1)S(1)}, bf16[256,768]{1,0:T(8,128)(2,1)}, u32[]{:S(2)}) copy-start(bf16[256,768]{1,0:T(8,128)(2,1)} %get-tuple-element.39) | copy-start | bytes 1179652
  3.7 6.6 %copy-start.2 = (bf16[256,512]{1,0:T(8,128)(2,1)S(1)}, bf16[256,512]{1,0:T(8,128)(2,1)}, u32[]{:S(2)}) copy-start(bf16[256,512]{1,0:T(8,128)(2,1)} %c0.1) | copy-start | bytes 786436
  3.7 29.4 %all-to-all-start = ((bf16[4,1552,128]{2,1,0:T(8,128)(2,1)}), bf16[4,1552,128]{2,1,0:T(8,128)(2,1)S(1)}, u32[]{:S(2)}, u32[]{:S(2)}) async-start(bf16[4,1552,128]{2,1,0:T(8,128)(2,1)} %get-tuple-element.38), calls=%async_computation | async-start | bytes 3178496 | tf_op jit(solution)/shard_map/all_to_all | solution.py:282
  9.7 12.1 %collective-permute-start.2 = (bf16[256,768]{1,0:T(8,128)(2,1)S(1)}, bf16[256,768]{1,0:T(8,128)(2,1)S(1)}, u32[]{:S(2)}, u32[]{:S(2)}) collective-permute-start(bf16[256,768]{1,0:T(8,128)(2,1)S(1)} %copy-done.6), channel_id=1, source_target_pairs={{0,128},{128,0},{1,129},{129,1},{2,130},{130,2},{3,131},{131,3},{4... | collective-permute-start | bytes 1179656 | tf_op jit(solution)/shard_map/ppermute | solution.py:298
  10.3 16.8 %collective-permute-start.4 = (bf16[256,512]{1,0:T(8,128)(2,1)S(1)}, bf16[256,512]{1,0:T(8,128)(2,1)S(1)}, u32[]{:S(2)}, u32[]{:S(2)}) collective-permute-start(bf16[256,512]{1,0:T(8,128)(2,1)S(1)} %copy-done.2), channel_id=1, source_target_pairs={{0,2},{2,0},{1,3},{3,1},{4,6},{6,4},{5,7},{7,5},{8,10},{10,8},{9,1... | collective-permute-start | bytes 786440 | tf_op jit(solution)/shard_map/ppermute | solution.py:298
  13.2 13.9 %collective-permute-start.6 = (bf16[256,512]{1,0:T(8,128)(2,1)S(1)}, bf16[256,512]{1,0:T(8,128)(2,1)S(1)}, u32[]{:S(2)}, u32[]{:S(2)}) collective-permute-start(bf16[256,512]{1,0:T(8,128)(2,1)S(1)} %copy-done.2), channel_id=1, source_target_pairs={{0,130},{2,128},{128,2},{130,0},{1,131},{3,129},{129,3},{131,1},{4... | collective-permute-start | bytes 786440 | tf_op jit(solution)/shard_map/ppermute | solution.py:286
  21.7 7.2 %collective-permute-start.3 = (bf16[256,768]{1,0:T(8,128)(2,1)S(1)}, bf16[256,768]{1,0:T(8,128)(2,1)S(1)}, u32[]{:S(2)}, u32[]{:S(2)}) collective-permute-start(bf16[256,768]{1,0:T(8,128)(2,1)S(1)} %collective-permute-done.2.c1), channel_id=1, source_target_pairs={{0,1},{1,0},{2,3},{3,2},{4,5},{5,4},{6,7},{7,6},{8,9},{9,8},{10,11... | collective-permute-start | bytes 1179656 | tf_op jit(solution)/shard_map/ppermute | solution.py:298
  21.7 5.8 %collective-permute-start.1 = (bf16[256,512]{1,0:T(8,128)(2,1)S(1)}, bf16[256,512]{1,0:T(8,128)(2,1)S(1)}, u32[]{:S(2)}, u32[]{:S(2)}) collective-permute-start(bf16[256,512]{1,0:T(8,128)(2,1)S(1)} %copy-done.2), channel_id=1, source_target_pairs={{0,1},{1,0},{2,3},{3,2},{4,5},{5,4},{6,7},{7,6},{8,9},{9,8},{10,11... | collective-permute-start | bytes 786440 | tf_op jit(solution)/shard_map/ppermute | solution.py:298
  27.0 1.5 %collective-permute-start.5 = (bf16[256,512]{1,0:T(8,128)(2,1)S(1)}, bf16[256,512]{1,0:T(8,128)(2,1)S(1)}, u32[]{:S(2)}, u32[]{:S(2)}) collective-permute-start(bf16[256,512]{1,0:T(8,128)(2,1)S(1)} %collective-permute-done.4.c2), channel_id=1, source_target_pairs={{0,1},{1,0},{2,3},{3,2},{4,5},{5,4},{6,7},{7,6},{8,9},{9,8},{10,11... | collective-permute-start | bytes 786440 | tf_op jit(solution)/shard_map/ppermute | solution.py:298
  27.0 1.9 %collective-permute-start.7 = (bf16[256,512]{1,0:T(8,128)(2,1)S(1)}, bf16[256,512]{1,0:T(8,128)(2,1)S(1)}, u32[]{:S(2)}, u32[]{:S(2)}) collective-permute-start(bf16[256,512]{1,0:T(8,128)(2,1)S(1)} %collective-permute-done.6.c3), channel_id=1, source_target_pairs={{0,1},{1,0},{2,3},{3,2},{4,5},{5,4},{6,7},{7,6},{8,9},{9,8},{10,11... | collective-permute-start | bytes 786440 | tf_op jit(solution)/shard_map/ppermute | solution.py:298
  33.1 18.7 %all-to-all-start.1 = ((bf16[4,1024,128]{2,1,0:T(8,128)(2,1)}), bf16[4,1024,128]{2,1,0:T(8,128)(2,1)S(1)}, u32[]{:S(2)}, u32[]{:S(2)}) async-start(bf16[4,1024,128]{2,1,0:T(8,128)(2,1)} %get-tuple-element.40), calls=%async_computation.1 | async-start | bytes 2097152 | tf_op jit(solution)/shard_map/all_to_all | solution.py:282
  37.9 26.8 %copy-start.7 = (bf16[272,128]{1,0:T(8,128)(2,1)S(1)}, bf16[272,128]{1,0:T(8,128)(2,1)}, u32[]{:S(2)}) copy-start(bf16[272,128]{1,0:T(8,128)(2,1)} %get-tuple-element.44) | copy-start | bytes 208900
  38.8 26.5 %collective-permute-start = (bf16[3,1024,128]{2,1,0:T(8,128)(2,1)}, bf16[3,1024,128]{2,1,0:T(8,128)(2,1)S(1)}, u32[]{:S(2)}, u32[]{:S(2)}) collective-permute-start(bf16[3,1024,128]{2,1,0:T(8,128)(2,1)} %slice.4), channel_id=1, source_target_pairs={{0,16},{16,32},{32,48},{48,64},{64,80},{80,96},{96,112},{112,128},... | collective-permute-start | bytes 2359304 | tf_op jit(solution)/shard_map/ppermute | solution.py:294
  52.0 0.7 copy-start
  52.7 19.5 %all-to-all-start.2 = ((bf16[8,128,128]{2,1,0:T(8,128)(2,1)}), bf16[8,128,128]{2,1,0:T(8,128)(2,1)S(1)}, u32[]{:S(2)}, u32[]{:S(2)}) async-start(bf16[8,128,128]{2,1,0:T(8,128)(2,1)} %bitcast.14), calls=%async_computation.2 | async-start | bytes 524288 | tf_op jit(solution)/shard_map/all_to_all | solution.py:282
  61.2 7.1 %collective-permute-start.8 = (bf16[272,128]{1,0:T(8,128)(2,1)}, bf16[272,128]{1,0:T(8,128)(2,1)S(1)}, u32[]{:S(2)}, u32[]{:S(2)}) collective-permute-start(bf16[272,128]{1,0:T(8,128)(2,1)} %get-tuple-element.42), channel_id=1, source_target_pairs={{0,4},{4,8},{8,12},{12,0},{1,5},{5,9},{9,13},{13,1},{2,6},{6,10},{... | collective-permute-start | bytes 208904 | tf_op jit(solution)/shard_map/ppermute | solution.py:290
  61.2 7.1 %collective-permute-start.9 = (bf16[272,128]{1,0:T(8,128)(2,1)}, bf16[272,128]{1,0:T(8,128)(2,1)S(1)}, u32[]{:S(2)}, u32[]{:S(2)}) collective-permute-start(bf16[272,128]{1,0:T(8,128)(2,1)} %get-tuple-element.43), channel_id=1, source_target_pairs={{0,8},{4,12},{8,0},{12,4},{1,9},{5,13},{9,1},{13,5},{2,10},{6,14},... | collective-permute-start | bytes 208904 | tf_op jit(solution)/shard_map/ppermute | solution.py:290
  64.7 4.3 %collective-permute-start.10 = (bf16[272,128]{1,0:T(8,128)(2,1)S(1)}, bf16[272,128]{1,0:T(8,128)(2,1)S(1)}, u32[]{:S(2)}, u32[]{:S(2)}) collective-permute-start(bf16[272,128]{1,0:T(8,128)(2,1)S(1)} %copy-done.7), channel_id=1, source_target_pairs={{0,12},{4,0},{8,4},{12,8},{1,13},{5,1},{9,5},{13,9},{2,14},{6,2},{... | collective-permute-start | bytes 208904 | tf_op jit(solution)/shard_map/ppermute | solution.py:290
  68.3 8.7 %copy-start.3 = (bf16[272,128]{1,0:T(8,128)(2,1)}, bf16[272,128]{1,0:T(8,128)(2,1)S(1)}, u32[]{:S(2)}) copy-start(bf16[272,128]{1,0:T(8,128)(2,1)S(1)} %collective-permute-done.8.g1) | copy-start | bytes 208900
  68.3 8.7 %copy-start.4 = (bf16[272,128]{1,0:T(8,128)(2,1)}, bf16[272,128]{1,0:T(8,128)(2,1)S(1)}, u32[]{:S(2)}) copy-start(bf16[272,128]{1,0:T(8,128)(2,1)S(1)} %collective-permute-done.9.g2) | copy-start | bytes 208900
  69.0 8.0 %copy-start.5 = (bf16[272,128]{1,0:T(8,128)(2,1)}, bf16[272,128]{1,0:T(8,128)(2,1)S(1)}, u32[]{:S(2)}) copy-start(bf16[272,128]{1,0:T(8,128)(2,1)S(1)} %collective-permute-done.10.g3) | copy-start | bytes 208900
  72.9 14.6 %all-to-all-start.3 = ((bf16[8,128,128]{2,1,0:T(8,128)(2,1)}), bf16[8,128,128]{2,1,0:T(8,128)(2,1)S(1)}, u32[]{:S(2)}, u32[]{:S(2)}) async-start(bf16[8,128,128]{2,1,0:T(8,128)(2,1)} %shard_map.168), calls=%async_computation.3 | async-start | bytes 524288 | tf_op jit(solution)/shard_map/all_to_all | solution.py:282
  87.6 7.4 %collective-permute-start.14 = (bf16[1024,128]{1,0:T(8,128)(2,1)S(1)}, bf16[1024,128]{1,0:T(8,128)(2,1)S(1)}, u32[]{:S(2)}, u32[]{:S(2)}) collective-permute-start(bf16[1024,128]{1,0:T(8,128)(2,1)S(1)} %bitcast.9), channel_id=1, source_target_pairs={{0,12},{4,0},{8,4},{12,8},{1,13},{5,1},{9,5},{13,9},{2,14},{6,2},{... | collective-permute-start | bytes 786440 | tf_op jit(solution)/shard_map/ppermute | solution.py:290
  88.4 10.2 %collective-permute-start.11 = (bf16[3,512,128]{2,1,0:T(8,128)(2,1)}, bf16[3,512,128]{2,1,0:T(8,128)(2,1)S(1)}, u32[]{:S(2)}, u32[]{:S(2)}) collective-permute-start(bf16[3,512,128]{2,1,0:T(8,128)(2,1)} %get-tuple-element.52), channel_id=1, source_target_pairs={{0,16},{16,32},{32,48},{48,64},{64,80},{80,96},{96,112},{112,128},... | collective-permute-start | bytes 1179656 | tf_op jit(solution)/shard_map/ppermute | solution.py:294
  88.8 14.4 %collective-permute-start.15 = (bf16[1024,128]{1,0:T(8,128)(2,1)S(1)}, bf16[1024,128]{1,0:T(8,128)(2,1)S(1)}, u32[]{:S(2)}, u32[]{:S(2)}) collective-permute-start(bf16[1024,128]{1,0:T(8,128)(2,1)S(1)} %bitcast.10), channel_id=1, source_target_pairs={{0,128},{128,0},{1,129},{129,1},{2,130},{130,2},{3,131},{131,3},{4... | collective-permute-start | bytes 786440 | tf_op jit(solution)/shard_map/ppermute | solution.py:298
  88.9 14.3 %collective-permute-start.13 = (bf16[1024,128]{1,0:T(8,128)(2,1)S(1)}, bf16[1024,128]{1,0:T(8,128)(2,1)S(1)}, u32[]{:S(2)}, u32[]{:S(2)}) collective-permute-start(bf16[1024,128]{1,0:T(8,128)(2,1)S(1)} %bitcast.11), channel_id=1, source_target_pairs={{0,8},{4,12},{8,0},{12,4},{1,9},{5,13},{9,1},{13,5},{2,10},{6,14},... | collective-permute-start | bytes 786440 | tf_op jit(solution)/shard_map/ppermute | solution.py:290
  90.4 12.8 %collective-permute-start.12 = (bf16[1024,128]{1,0:T(8,128)(2,1)S(1)}, bf16[1024,128]{1,0:T(8,128)(2,1)S(1)}, u32[]{:S(2)}, u32[]{:S(2)}) collective-permute-start(bf16[1024,128]{1,0:T(8,128)(2,1)S(1)} %bitcast.12), channel_id=1, source_target_pairs={{0,4},{4,8},{8,12},{12,0},{1,5},{5,9},{9,13},{13,1},{2,6},{6,10},{... | collective-permute-start | bytes 786440 | tf_op jit(solution)/shard_map/ppermute | solution.py:290
  95.0 15.4 %collective-permute-start.21 = (bf16[1024,128]{1,0:T(8,128)(2,1)S(1)}, bf16[1024,128]{1,0:T(8,128)(2,1)S(1)}, u32[]{:S(2)}, u32[]{:S(2)}) collective-permute-start(bf16[1024,128]{1,0:T(8,128)(2,1)S(1)} %collective-permute-done.14.refs_3_), channel_id=1, source_target_pairs={{0,128},{128,0},{1,129},{129,1},{2,130},{130,2},{3,131},{131,3},{4... | collective-permute-start | bytes 786440 | tf_op jit(solution)/shard_map/ppermute | solution.py:298
  105.7 15.5 %collective-permute-start.16 = (bf16[1040,128]{1,0:T(8,128)(2,1)}, bf16[1040,128]{1,0:T(8,128)(2,1)S(1)}, u32[]{:S(2)}, u32[]{:S(2)}) collective-permute-start(bf16[1040,128]{1,0:T(8,128)(2,1)} %get-tuple-element.57), channel_id=1, source_target_pairs={{0,4},{4,8},{8,12},{12,0},{1,5},{5,9},{9,13},{13,1},{2,6},{6,10},{... | collective-permute-start | bytes 798728 | tf_op jit(solution)/shard_map/ppermute | solution.py:290
  106.5 14.7 %collective-permute-start.17 = (bf16[1040,128]{1,0:T(8,128)(2,1)}, bf16[1040,128]{1,0:T(8,128)(2,1)S(1)}, u32[]{:S(2)}, u32[]{:S(2)}) collective-permute-start(bf16[1040,128]{1,0:T(8,128)(2,1)} %get-tuple-element.58), channel_id=1, source_target_pairs={{0,8},{4,12},{8,0},{12,4},{1,9},{5,13},{9,1},{13,5},{2,10},{6,14},... | collective-permute-start | bytes 798728 | tf_op jit(solution)/shard_map/ppermute | solution.py:290
  110.0 11.2 %collective-permute-start.18 = (bf16[1040,128]{1,0:T(8,128)(2,1)}, bf16[1040,128]{1,0:T(8,128)(2,1)S(1)}, u32[]{:S(2)}, u32[]{:S(2)}) collective-permute-start(bf16[1040,128]{1,0:T(8,128)(2,1)} %get-tuple-element.59), channel_id=1, source_target_pairs={{0,12},{4,0},{8,4},{12,8},{1,13},{5,1},{9,5},{13,9},{2,14},{6,2},{... | collective-permute-start | bytes 798728 | tf_op jit(solution)/shard_map/ppermute | solution.py:290
  110.0 6.4 %collective-permute-start.20 = (bf16[1024,128]{1,0:T(8,128)(2,1)S(1)}, bf16[1024,128]{1,0:T(8,128)(2,1)S(1)}, u32[]{:S(2)}, u32[]{:S(2)}) collective-permute-start(bf16[1024,128]{1,0:T(8,128)(2,1)S(1)} %collective-permute-done.13.refs_2_), channel_id=1, source_target_pairs={{0,128},{128,0},{1,129},{129,1},{2,130},{130,2},{3,131},{131,3},{4... | collective-permute-start | bytes 786440 | tf_op jit(solution)/shard_map/ppermute | solution.py:298
  110.4 8.8 %collective-permute-start.19 = (bf16[1024,128]{1,0:T(8,128)(2,1)S(1)}, bf16[1024,128]{1,0:T(8,128)(2,1)S(1)}, u32[]{:S(2)}, u32[]{:S(2)}) collective-permute-start(bf16[1024,128]{1,0:T(8,128)(2,1)S(1)} %collective-permute-done.12.refs_1_), channel_id=1, source_target_pairs={{0,128},{128,0},{1,129},{129,1},{2,130},{130,2},{3,131},{131,3},{4... | collective-permute-start | bytes 786440 | tf_op jit(solution)/shard_map/ppermute | solution.py:298
  112.1 9.1 %copy-start.1 = (bf16[1040,128]{1,0:T(8,128)(2,1)S(1)}, bf16[1040,128]{1,0:T(8,128)(2,1)}, u32[]{:S(2)}) copy-start(bf16[1040,128]{1,0:T(8,128)(2,1)} %get-tuple-element.56.in0) | copy-start | bytes 798724

commit v4 on v3

--- a/solution.py
+++ b/solution.py
@@ -202,18 +202,6 @@
         ref[...] = out[lax.rem(place[1] + distance, 4)]
 
 
-def unpack_kernel(place, in0, in1, in2, in3, attended, log_total, grad_query, grad_keys, grad_values):
-    for distance, ref in enumerate((in0, in1, in2, in3)):
-        head = lax.rem(place[1] + 4 - distance, 4)
-        lanes = pl.ds(pl.multiple_of(head * HDIM, HDIM), HDIM)
-        grad_keys[:, lanes] = ref[:TOK, :].astype(f32)
-        grad_values[:, lanes] = ref[TOK : 2 * TOK, :].astype(f32)
-        grad_query[:, lanes] = ref[2 * TOK : 3 * TOK, :].astype(f32)
-        attended[:, lanes] = ref[3 * TOK : 4 * TOK, :]
-        extra = ref[4 * TOK :, :].astype(f32)
-        log_total[pl.ds(head, 1), :] = row_of(extra, 0, 3)
-
-
 def grad_kernel(place, c0, o0, c1, o1, c2, o2, c3, o3, weight, attn, g0, g1, g2, g3, out, grads):
     y_lo, y_hi, core = place[0], place[1], place[2]
     width = 4 * HDIM
@@ -256,24 +244,49 @@
         out[i] = total
 
 
-def assemble_kernel(place, *refs):
-    parts, (out, whole, sems) = refs[:8], refs[8:]
+def last_kernel(place, *refs):
+    back, near_parts, far_parts = refs[:4], refs[4:8], refs[8:13]
+    attended, log_total, grad_query, grad_keys, grad_values, out = refs[13:19]
+    held, held_attended, held_total, whole, sems = refs[19:]
+
+    def part_rows(far, distance, rows):
+        if not far:
+            return near_parts[distance][rows, :]
+        if distance:
+            return far_parts[distance + 1][rows, :]
+        return jnp.where(place[3] == 1, far_parts[0][rows, :], far_parts[1][rows, :])
+
     copies = []
+
+    def send(source, target):
+        copies.append(pltpu.make_async_copy(source, target, sems.at[len(copies)]))
+        copies[-1].start()
+
+    for i, target in enumerate((grad_keys, grad_values, grad_query)):
+        for distance, ref in enumerate(back):
+            head = lax.rem(place[1] + 4 - distance, 4)
+            lanes = pl.ds(pl.multiple_of(head * HDIM, HDIM), HDIM)
+            held[i, :, lanes] = ref[i * TOK : (i + 1) * TOK, :].astype(f32)
+        send(held.at[i], target)
+    for distance, ref in enumerate(back):
+        head = lax.rem(place[1] + 4 - distance, 4)
+        lanes = pl.ds(pl.multiple_of(head * HDIM, HDIM), HDIM)
+        held_attended[:, lanes] = ref[3 * TOK : 4 * TOK, :]
+        held_total[pl.ds(head, 1), :] = row_of(ref[4 * TOK :, :].astype(f32), 0, 3)
+    send(held_attended, attended)
+    send(held_total, log_total)
     strip = TOK // 4
     for far in range(2):
-        y = place[0] + far - 2 * place[0] * far
+        y = place[2] + far - 2 * place[2] * far
         for piece in range(4):
             rows = pl.ds(pl.multiple_of(y * TOK + piece * strip, strip), strip)
             for distance in range(4):
                 x = lax.rem(place[1] + 4 - distance, 4)
-                ref = parts[far * 4 + distance]
                 for j in range(4):
                     lanes = pl.ds(pl.multiple_of((x * 4 + j) * HDIM, HDIM), HDIM)
                     first = j * TOK + piece * strip
-                    whole[rows, lanes] = ref[first : first + strip, :]
-            copy = pltpu.make_async_copy(whole.at[rows], out.at[rows], sems.at[len(copies)])
-            copy.start()
-            copies.append(copy)
+                    whole[rows, lanes] = part_rows(far, distance, slice(first, first + strip))
+            send(whole.at[rows], out.at[rows])
     for copy in copies:
         copy.wait()
 
@@ -288,6 +301,15 @@
 
 def along_x(value, distance):
     return lax.ppermute(value, "x", [(i, (i + distance) % 4) for i in range(4)])
+
+
+def across_y(value, parities=(0, 1)):
+    pairs = [(y * 8 + z, (1 - y) * 8 + z) for y in range(2) for z in range(8) if z % 2 in parities]
+    return lax.ppermute(value, ("yl", "z"), pairs)
+
+
+def beside(value, parity):
+    return lax.ppermute(value, "z", [(z, z ^ 1) for z in range(8) if z % 2 == parity])
 
 
 def next_row(value):
@@ -314,7 +336,9 @@
 ):
     y_lo = lax.axis_index("yl")
     place = jnp.stack([y_lo] + [lax.axis_index(axis) for axis in ("yh", "core", "x")]).astype(jnp.int32)
-    place_x = jnp.stack([lax.axis_index(("yl", "z")), lax.axis_index("x")]).astype(jnp.int32)
+    place_x = jnp.stack(
+        [lax.axis_index(("yl", "z")), lax.axis_index("x"), y_lo, lax.rem(lax.axis_index("z"), 2)]
+    ).astype(jnp.int32)
 
     packed, to_pair = call(
         pack_kernel,
@@ -349,7 +373,7 @@
         scratch=[pltpu.VMEM((4, GRAD_ROWS, HDIM), bf16)],
     )
     products = across(product, "x")
-    summed = call(sum_kernel, shape(4 * TOK, HDIM), 0, products)
+    summed = call(sum_kernel, pltpu.HBM((4 * TOK, HDIM), bf16), 0, products)
     grads = [grads[0]] + [along_x(grads[d], d) for d in range(1, 4)]
     parts = across(summed.reshape(8, HDIM, HDIM), "z")
     forward_out = call(forward_kernel, shape(4, GRAD_ROWS, HDIM), 1, place_x, own, halo)
@@ -374,8 +398,9 @@
     behind = next_row(ahead)
     gathered, ahead = lax.optimization_barrier((gathered, ahead))
     row_parts = [gathered] + [along_x(gathered, d) for d in range(1, 4)]
-    far_parts = [other(part, "yl") for part in row_parts]
-    behind, row_parts, far_parts[0] = lax.optimization_barrier((behind, row_parts, far_parts[0]))
+    crossed = across_y(row_parts[0], (1,))
+    far_parts = [crossed, beside(crossed, 1)] + [across_y(part) for part in row_parts[1:]]
+    behind, row_parts[3] = lax.optimization_barrier((behind, row_parts[3]))
     outs = call(
         finish_kernel,
         [pltpu.HBM((BACK_ROWS, HDIM), bf16)] * 4,
@@ -387,31 +412,34 @@
         scratch=[pltpu.VMEM((4, BACK_ROWS, HDIM), bf16)],
     )
     back = [outs[0]] + [along_x(outs[d], d) for d in range(1, 4)]
-    attended, log_total, grad_query, grad_keys, grad_values = call(
-        unpack_kernel,
-        [
-            shape(TOK, 4 * HDIM),
-            shape(4, TOK, dtype=f32),
-            shape(TOK, 4 * HDIM, dtype=f32),
-            shape(TOK, 4 * HDIM, dtype=f32),
-            shape(TOK, 4 * HDIM, dtype=f32),
-        ],
-        1,
-        place_x,
-        *back,
-    )
-    place_xy = jnp.stack([y_lo, lax.axis_index("x")]).astype(jnp.int32)
-    grad_weight = call(
-        assemble_kernel,
-        shape(2 * TOK, 16 * HDIM),
-        1,
-        place_xy,
-        *row_parts,
-        *far_parts,
-        scratch=[pltpu.VMEM((2 * TOK, 16 * HDIM), bf16), pltpu.SemaphoreType.DMA((8,))],
-        raw_out=True,
-    )
-    return (attended, log_total, grad_query, grad_keys, grad_values, grad_weight)
+    block = (TOK, 4 * HDIM)
+    return tuple(
+        call(
+            last_kernel,
+            [
+                shape(*block),
+                shape(4, TOK, dtype=f32),
+                shape(*block, dtype=f32),
+                shape(*block, dtype=f32),
+                shape(*block, dtype=f32),
+                shape(2 * TOK, 16 * HDIM),
+            ],
+            1,
+            place_x,
+            in_hbm(back[0]),
+            *back[1:],
+            *row_parts,
+            *far_parts,
+            scratch=[
+                pltpu.VMEM((3, *block), f32),
+                pltpu.VMEM(block, bf16),
+                pltpu.VMEM((4, TOK), f32),
+                pltpu.VMEM((2 * TOK, 16 * HDIM), bf16),
+                pltpu.SemaphoreType.DMA((13,)),
+            ],
+            raw_out=True,
+        )
+    )
 
 
 def solution(mesh):

time: 124 us -> 120 us (0.968)
  waiting for transfers between devices: 50.1 us -> 44.6 us
  starting transfers between devices: 46.9 us -> 49.5 us
    ppermute x10 -> x6, waiting for transfers between devices: 25.2 us -> 13.6 us  [other(): return lax.ppermute(value, axis, [(0, 1), (1, 0)])]
    ppermute x0 -> x5, waiting for transfers between devices: none -> 7.16 us  [the longest x4 7.16 us: across_y(): return lax.ppermute(value, ('yl', 'z'), pairs)]
    ppermute x0 -> x5, starting transfers between devices: none -> 4.66 us  [the longest x4 3.38 us: across_y(): return lax.ppermute(value, ('yl', 'z'), pairs)]
    ppermute x10 -> x6, starting transfers between devices: 7.46 us -> 4.52 us  [other(): return lax.ppermute(value, axis, [(0, 1), (1, 0)])]
    ppermute x2, starting transfers between devices: 2.27 us -> 3.56 us  [next_row(): lax.ppermute(value, ('yl', 'z'), [(i, (i + 1) % 16) for i in range(16)])]
    pallas_call x9 -> x8, Pallas kernels: 23.6 us -> 23.4 us  [call(): pl.pallas_call(kernel, out_shape=out_shape, in_specs=[pl.BlockSpec(memory...]
  transfers between devices with their start and end apart: 26 -> 27, of which waited for: 13 -> 12; matrix products, arithmetic and copies ran while one was open for 1% -> 1% of each run, Pallas kernels for 15% -> 14%
where the time goes in v4:
time: 120 us
  starting transfers between devices  49.5 us (41%)
  waiting for transfers between devices  44.6 us (37%)
  Pallas kernels  23.4 us (20%)
    pallas_call x8, Pallas kernels, call(): pl.pallas_call(kernel, out_shape=out_shape, in_specs=[pl.BlockSpec(memory...  23.4 us
    all_to_all x4, starting transfers between devices, across(): return lax.all_to_all(value, axes, 0, 0, tiled=True)  23.2 us
    all_to_all x4, waiting for transfers between devices, across(): return lax.all_to_all(value, axes, 0, 0, tiled=True)  18.6 us
    ppermute x6, waiting for transfers between devices, other(): return lax.ppermute(value, axis, [(0, 1), (1, 0)])  13.6 us
    ppermute x9, starting transfers between devices, along_x(): return lax.ppermute(value, 'x', [(i, (i + distance) % 4) for i in range(4)])  12.4 us
    ppermute x4, waiting for transfers between devices, across_y(): return lax.ppermute(value, ('yl', 'z'), pairs)  7.16 us
    ppermute x6, starting transfers between devices, other(): return lax.ppermute(value, axis, [(0, 1), (1, 0)])  4.52 us
    ppermute x2, starting transfers between devices, next_row(): lax.ppermute(value, ('yl', 'z'), [(i, (i + 1) % 16) for i in range(16)])  3.56 us
  transfers between devices with their start and end apart: 27, of which 12 were waited for; matrix products, arithmetic and copies ran while one was open for 1% of the time, Pallas kernels for 14%

profile of v4, /device:TPU:2, one launch (start us, length us, event | category | flops | bytes accessed | tf_op | source)
XLA Modules:
  0.0 119.5 jit_solution(2976339013716646788)
XLA Ops:
  0.6 0.1 pad_add_fusion.1.place
  0.7 3.0 %shard_map.163 = (bf16[4,1552,128]{2,1,0:T(8,128)(2,1)}, bf16[256,768]{1,0:T(8,128)(2,1)}) custom-call(s32[4]{0:T(128)S(1)} %pad_add_fusion.1.place, bf16[256,512]{1,0:T(8,128)(2,1)} %qf.1, bf16[256,512]{1,0:T(8,128)(2,1)} %kf.1, bf16[256,512]{1,0:T(8,128)(2,1)} %vf.1, bf16[256,512]{1,0:T(8,128)(2,1)} %kb.1, bf16[256,512]{1,0:T(8,128)(2,1)} %vb.1, ...), custom_call_target="tpu_custom_call" | custom-call | tf_op jit(solution)/shard_map/pallas_call | solution.py:73
  3.7 0.0 copy-start.4
  3.7 5.9 %all-to-all-start = ((bf16[4,1552,128]{2,1,0:T(8,128)(2,1)}), bf16[4,1552,128]{2,1,0:T(8,128)(2,1)S(1)}, u32[]{:S(2)}, u32[]{:S(2)}) async-start(bf16[4,1552,128]{2,1,0:T(8,128)(2,1)} %get-tuple-element.29), calls=%async_computation | async-start | bytes 3178496 | tf_op jit(solution)/shard_map/all_to_all | solution.py:295
  9.7 0.6 collective-permute-start.2
  10.3 2.9 %collective-permute-start.4 = (bf16[256,512]{1,0:T(8,128)(2,1)S(1)}, bf16[256,512]{1,0:T(8,128)(2,1)S(1)}, u32[]{:S(2)}, u32[]{:S(2)}) collective-permute-start(bf16[256,512]{1,0:T(8,128)(2,1)S(1)} %copy-done), channel_id=1, source_target_pairs={{0,2},{2,0},{1,3},{3,1},{4,6},{6,4},{5,7},{7,5},{8,10},{10,8},{9,1... | collective-permute-start | bytes 786440 | tf_op jit(solution)/shard_map/ppermute | solution.py:320
  13.2 1.2 %collective-permute-start.6 = (bf16[256,512]{1,0:T(8,128)(2,1)S(1)}, bf16[256,512]{1,0:T(8,128)(2,1)S(1)}, u32[]{:S(2)}, u32[]{:S(2)}) collective-permute-start(bf16[256,512]{1,0:T(8,128)(2,1)S(1)} %copy-done), channel_id=1, source_target_pairs={{0,130},{2,128},{128,2},{130,0},{1,131},{3,129},{129,3},{131,1},{4... | collective-permute-start | bytes 786440 | tf_op jit(solution)/shard_map/ppermute | solution.py:299
  14.4 7.4 %collective-permute-done.2.c1 = bf16[256,768]{1,0:T(8,128)(2,1)S(1)} collective-permute-done((bf16[256,768]{1,0:T(8,128)(2,1)S(1)}, bf16[256,768]{1,0:T(8,128)(2,1)S(1)}, u32[]{:S(2)}, u32[]{:S(2)}) %collective-permute-start.2) | collective-permute-done | bytes 393248 | tf_op jit(solution)/shard_map/ppermute | solution.py:320
  21.7 0.5 collective-permute-start.1
  22.2 4.8 %collective-permute-done.4.c2 = bf16[256,512]{1,0:T(8,128)(2,1)S(1)} collective-permute-done((bf16[256,512]{1,0:T(8,128)(2,1)S(1)}, bf16[256,512]{1,0:T(8,128)(2,1)S(1)}, u32[]{:S(2)}, u32[]{:S(2)}) %collective-permute-start.4) | collective-permute-done | bytes 262176 | tf_op jit(solution)/shard_map/ppermute | solution.py:320
  27.0 0.5 collective-permute-start.7
  27.6 1.0 collective-permute-done.5.o2
  28.6 0.4 collective-permute-done.7.o3
  29.0 4.2 %shard_map.164 = (bf16[272,128]{1,0:T(8,128)(2,1)}, bf16[272,128]{1,0:T(8,128)(2,1)}, bf16[272,128]{1,0:T(8,128)(2,1)}, bf16[272,128]{1,0:T(8,128)(2,1)}, bf16[4,1024,128]{2,1,0:T(8,128)(2,1)}) custom-call(s32[4]{0:T(128)S(1)} %pad_add_fusion.1.place, bf16[256,512]{1,0:T(8,128)(2,1)} %c0.1, bf16[256,512]{1,0:T(8,128)(2,1)S(1)} %collective-permute-done.1.o0, ...), custom_call_target="tpu_custom_call" | custom-call | tf_op jit(solution)/shard_map/pallas_call | solution.py:73
  33.1 4.8 %all-to-all-start.1 = ((bf16[4,1024,128]{2,1,0:T(8,128)(2,1)}), bf16[4,1024,128]{2,1,0:T(8,128)(2,1)S(1)}, u32[]{:S(2)}, u32[]{:S(2)}) async-start(bf16[4,1024,128]{2,1,0:T(8,128)(2,1)} %get-tuple-element.31), calls=%async_computation.1 | async-start | bytes 2097152 | tf_op jit(solution)/shard_map/all_to_all | solution.py:295
  37.9 0.9 slice.4
  38.8 1.9 %collective-permute-start = (bf16[3,1024,128]{2,1,0:T(8,128)(2,1)}, bf16[3,1024,128]{2,1,0:T(8,128)(2,1)S(1)}, u32[]{:S(2)}, u32[]{:S(2)}) collective-permute-start(bf16[3,1024,128]{2,1,0:T(8,128)(2,1)} %slice.4), channel_id=1, source_target_pairs={{0,16},{16,32},{32,48},{48,64},{64,80},{80,96},{96,112},{112,128},... | collective-permute-start | bytes 2359304 | tf_op jit(solution)/shard_map/ppermute | solution.py:316
  40.7 11.1 %all-to-all-done.1.parts = bf16[4,1024,128]{2,1,0:T(8,128)(2,1)S(1)} async-done(((bf16[4,1024,128]{2,1,0:T(8,128)(2,1)}), bf16[4,1024,128]{2,1,0:T(8,128)(2,1)S(1)}, u32[]{:S(2)}, u32[]{:S(2)}) %all-to-all-start.1) | async-done | bytes 1048608 | tf_op jit(solution)/shard_map/all_to_all | solution.py:295
  51.8 0.8 shard_map.165
  52.7 8.5 %all-to-all-start.2 = ((bf16[8,128,128]{2,1,0:T(8,128)(2,1)}), bf16[8,128,128]{2,1,0:T(8,128)(2,1)S(1)}, u32[]{:S(2)}, u32[]{:S(2)}) async-start(bf16[8,128,128]{2,1,0:T(8,128)(2,1)} %bitcast.15), calls=%async_computation.2 | async-start | bytes 524288 | tf_op jit(solution)/shard_map/all_to_all | solution.py:295
  61.1 3.5 %collective-permute-start.9 = (bf16[272,128]{1,0:T(8,128)(2,1)}, bf16[272,128]{1,0:T(8,128)(2,1)S(1)}, u32[]{:S(2)}, u32[]{:S(2)}) collective-permute-start(bf16[272,128]{1,0:T(8,128)(2,1)} %get-tuple-element.34), channel_id=1, source_target_pairs={{0,8},{4,12},{8,0},{12,4},{1,9},{5,13},{9,1},{13,5},{2,10},{6,14},... | collective-permute-start | bytes 208904 | tf_op jit(solution)/shard_map/ppermute | solution.py:303
  64.7 0.6 collective-permute-start.10
  65.2 0.1 pad_add_fusion.place
  65.3 2.9 %shard_map.166.forward_out = bf16[4,272,128]{2,1,0:T(8,128)(2,1)S(1)} custom-call(s32[4]{0:T(128)S(1)} %pad_add_fusion.place, bf16[4,1552,128]{2,1,0:T(8,128)(2,1)S(1)} %all-to-all-done.own, bf16[3,1024,128]{2,1,0:T(8,128)(2,1)S(1)} %collective-permute-done.halo), custom_call_target="tpu_custom_call" | custom-call | tf_op jit(solution)/shard_map/pallas_call | solution.py:73
  68.3 0.7 collective-permute-done.10.g3
  69.0 3.2 %all-to-all-done.2.parts = bf16[8,128,128]{2,1,0:T(8,128)(2,1)S(1)} async-done(((bf16[8,128,128]{2,1,0:T(8,128)(2,1)}), bf16[8,128,128]{2,1,0:T(8,128)(2,1)S(1)}, u32[]{:S(2)}, u32[]{:S(2)}) %all-to-all-start.2) | async-done | bytes 262176 | tf_op jit(solution)/shard_map/all_to_all | solution.py:295
  72.2 0.7 shard_map.168
  72.9 4.0 %all-to-all-start.3 = ((bf16[8,128,128]{2,1,0:T(8,128)(2,1)}), bf16[8,128,128]{2,1,0:T(8,128)(2,1)S(1)}, u32[]{:S(2)}, u32[]{:S(2)}) async-start(bf16[8,128,128]{2,1,0:T(8,128)(2,1)} %shard_map.168), calls=%async_computation.3 | async-start | bytes 524288 | tf_op jit(solution)/shard_map/all_to_all | solution.py:295
  77.0 6.1 %shard_map.167 = (bf16[4,528,128]{2,1,0:T(8,128)(2,1)}, f32[4,512,128]{2,1,0:T(8,128)}, bf16[3,512,128]{2,1,0:T(8,128)(2,1)}) custom-call(s32[4]{0:T(128)S(1)} %pad_add_fusion.place, bf16[4,1552,128]{2,1,0:T(8,128)(2,1)S(1)} %all-to-all-done.own, bf16[3,1024,128]{2,1,0:T(8,128)(2,1)S(1)} %collective-permute-done.halo, ...), custom_call_target="tpu_custom_call" | custom-call | tf_op jit(solution)/shard_map/pallas_call | solution.py:73
  83.1 4.3 %all-to-all-done.3 = bf16[8,128,128]{2,1,0:T(8,128)(2,1)S(1)} async-done(((bf16[8,128,128]{2,1,0:T(8,128)(2,1)}), bf16[8,128,128]{2,1,0:T(8,128)(2,1)S(1)}, u32[]{:S(2)}, u32[]{:S(2)}) %all-to-all-start.3) | async-done | bytes 262176 | tf_op jit(solution)/shard_map/all_to_all | solution.py:295
  87.4 0.7 collective-permute-start.18
  88.1 2.0 %collective-permute-start.17 = (bf16[1024,128]{1,0:T(8,128)(2,1)S(1)}, bf16[1024,128]{1,0:T(8,128)(2,1)S(1)}, u32[]{:S(2)}, u32[]{:S(2)}) collective-permute-start(bf16[1024,128]{1,0:T(8,128)(2,1)S(1)} %bitcast.11), channel_id=1, source_target_pairs={{0,8},{4,12},{8,0},{12,4},{1,9},{5,13},{9,1},{13,5},{2,10},{6,14},... | collective-permute-start | bytes 786440 | tf_op jit(solution)/shard_map/ppermute | solution.py:303
  90.1 1.6 %collective-permute-start.11 = (bf16[3,512,128]{2,1,0:T(8,128)(2,1)}, bf16[3,512,128]{2,1,0:T(8,128)(2,1)S(1)}, u32[]{:S(2)}, u32[]{:S(2)}) collective-permute-start(bf16[3,512,128]{2,1,0:T(8,128)(2,1)} %get-tuple-element.43), channel_id=1, source_target_pairs={{0,16},{16,32},{32,48},{48,64},{64,80},{80,96},{96,112},{112,128},... | collective-permute-start | bytes 1179656 | tf_op jit(solution)/shard_map/ppermute | solution.py:316
  91.8 1.2 collective-permute-start.12
  93.0 0.8 collective-permute-start.16
  93.8 1.3 %collective-permute-start.19 = (bf16[1024,128]{1,0:T(8,128)(2,1)S(1)}, bf16[1024,128]{1,0:T(8,128)(2,1)S(1)}, u32[]{:S(2)}, u32[]{:S(2)}) collective-permute-start(bf16[1024,128]{1,0:T(8,128)(2,1)S(1)} %collective-permute-done.18.refs_8_), channel_id=1, source_target_pairs={{16,0},{48,32},{80,64},{112,96},{17,1},{49,33},{81,65},{113,97},{1... | collective-permute-start | bytes 786440 | tf_op jit(solution)/shard_map/ppermute | solution.py:312
  95.1 1.4 %collective-permute-done.17.refs_6_ = bf16[1024,128]{1,0:T(8,128)(2,1)S(1)} collective-permute-done((bf16[1024,128]{1,0:T(8,128)(2,1)S(1)}, bf16[1024,128]{1,0:T(8,128)(2,1)S(1)}, u32[]{:S(2)}, u32[]{:S(2)}) %collective-permute-start.17) | collective-permute-done | bytes 262176 | tf_op jit(solution)/shard_map/ppermute | solution.py:303
  96.5 0.7 collective-permute-start.21
  97.2 3.1 %collective-permute-done.11.behind = bf16[3,512,128]{2,1,0:T(8,128)(2,1)S(1)} collective-permute-done((bf16[3,512,128]{2,1,0:T(8,128)(2,1)}, bf16[3,512,128]{2,1,0:T(8,128)(2,1)S(1)}, u32[]{:S(2)}, u32[]{:S(2)}) %collective-permute-start.11) | collective-permute-done | bytes 393248 | tf_op jit(solution)/shard_map/ppermute | solution.py:316
  100.3 2.5 %shard_map.169 = (bf16[1040,128]{1,0:T(8,128)(2,1)}, bf16[1040,128]{1,0:T(8,128)(2,1)}, bf16[1040,128]{1,0:T(8,128)(2,1)}, bf16[1040,128]{1,0:T(8,128)(2,1)}) custom-call(s32[4]{0:T(128)S(1)} %pad_add_fusion.place, bf16[4,528,128]{2,1,0:T(8,128)(2,1)} %get-tuple-element.41.rest, f32[4,512,128]{2,1,0:T(8,128)} %get-tuple-element.42.grad_kv, ...), custom_call_target="tpu_custom_call" | custom-call | tf_op jit(solution)/shard_map/pallas_call | solution.py:73
  102.9 0.5 collective-permute-start.13
  103.3 2.5 %collective-permute-start.14 = (bf16[1040,128]{1,0:T(8,128)(2,1)}, bf16[1040,128]{1,0:T(8,128)(2,1)S(1)}, u32[]{:S(2)}, u32[]{:S(2)}) collective-permute-start(bf16[1040,128]{1,0:T(8,128)(2,1)} %get-tuple-element.49), channel_id=1, source_target_pairs={{0,8},{4,12},{8,0},{12,4},{1,9},{5,13},{9,1},{13,5},{2,10},{6,14},... | collective-permute-start | bytes 798728 | tf_op jit(solution)/shard_map/ppermute | solution.py:303
  105.8 1.2 %collective-permute-start.15 = (bf16[1040,128]{1,0:T(8,128)(2,1)}, bf16[1040,128]{1,0:T(8,128)(2,1)S(1)}, u32[]{:S(2)}, u32[]{:S(2)}) collective-permute-start(bf16[1040,128]{1,0:T(8,128)(2,1)} %get-tuple-element.50), channel_id=1, source_target_pairs={{0,12},{4,0},{8,4},{12,8},{1,13},{5,1},{9,5},{13,9},{2,14},{6,2},{... | collective-permute-start | bytes 798728 | tf_op jit(solution)/shard_map/ppermute | solution.py:303
  107.1 0.8 collective-permute-start.20
  107.9 1.2 collective-permute-start.22
  109.1 4.3 %collective-permute-done.20.refs_10_ = bf16[1024,128]{1,0:T(8,128)(2,1)S(1)} collective-permute-done((bf16[1024,128]{1,0:T(8,128)(2,1)S(1)}, bf16[1024,128]{1,0:T(8,128)(2,1)S(1)}, u32[]{:S(2)}, u32[]{:S(2)}) %collective-permute-start.20) | collective-permute-done | bytes 262176 | tf_op jit(solution)/shard_map/ppermute | solution.py:308
  113.4 2.8 %collective-permute-done.22.refs_12_ = bf16[1024,128]{1,0:T(8,128)(2,1)S(1)} collective-permute-done((bf16[1024,128]{1,0:T(8,128)(2,1)S(1)}, bf16[1024,128]{1,0:T(8,128)(2,1)S(1)}, u32[]{:S(2)}, u32[]{:S(2)}) %collective-permute-start.22) | collective-permute-done | bytes 262176 | tf_op jit(solution)/shard_map/ppermute | solution.py:308
  116.3 3.1 %shard_map.170 = (bf16[256,512]{1,0:T(8,128)(2,1)}, f32[4,256]{1,0:T(4,128)}, f32[256,512]{1,0:T(8,128)}, f32[256,512]{1,0:T(8,128)}, f32[256,512]{1,0:T(8,128)}, /*index=5*/bf16[512,2048]{1,0:T(8,128)(2,1)}) custom-call(s32[4]{0:T(128)S(1)} %pad_add_fusion.place, bf16[1040,128]{1,0:T(8,128)(2,1)} %get-tuple-element.47.refs_0_, ...), custom_call_target="tpu_custom_call" | custom-call | tf_op jit(solution)/shard_map/pallas_call | solution.py:73
  (29 shorter events, 0.1 us)
Async XLA Ops:
  3.7 6.0 %copy-start.4 = (bf16[256,768]{1,0:T(8,128)(2,1)S(1)}, bf16[256,768]{1,0:T(8,128)(2,1)}, u32[]{:S(2)}) copy-start(bf16[256,768]{1,0:T(8,128)(2,1)} %get-tuple-element.30) | copy-start | bytes 1179652
  3.7 6.6 %copy-start = (bf16[256,512]{1,0:T(8,128)(2,1)S(1)}, bf16[256,512]{1,0:T(8,128)(2,1)}, u32[]{:S(2)}) copy-start(bf16[256,512]{1,0:T(8,128)(2,1)} %c0.1) | copy-start | bytes 786436
  3.7 29.4 %all-to-all-start = ((bf16[4,1552,128]{2,1,0:T(8,128)(2,1)}), bf16[4,1552,128]{2,1,0:T(8,128)(2,1)S(1)}, u32[]{:S(2)}, u32[]{:S(2)}) async-start(bf16[4,1552,128]{2,1,0:T(8,128)(2,1)} %get-tuple-element.29), calls=%async_computation | async-start | bytes 3178496 | tf_op jit(solution)/shard_map/all_to_all | solution.py:295
  9.7 12.1 %collective-permute-start.2 = (bf16[256,768]{1,0:T(8,128)(2,1)S(1)}, bf16[256,768]{1,0:T(8,128)(2,1)S(1)}, u32[]{:S(2)}, u32[]{:S(2)}) collective-permute-start(bf16[256,768]{1,0:T(8,128)(2,1)S(1)} %copy-done.4), channel_id=1, source_target_pairs={{0,128},{128,0},{1,129},{129,1},{2,130},{130,2},{3,131},{131,3},{4... | collective-permute-start | bytes 1179656 | tf_op jit(solution)/shard_map/ppermute | solution.py:320
  10.3 16.8 %collective-permute-start.4 = (bf16[256,512]{1,0:T(8,128)(2,1)S(1)}, bf16[256,512]{1,0:T(8,128)(2,1)S(1)}, u32[]{:S(2)}, u32[]{:S(2)}) collective-permute-start(bf16[256,512]{1,0:T(8,128)(2,1)S(1)} %copy-done), channel_id=1, source_target_pairs={{0,2},{2,0},{1,3},{3,1},{4,6},{6,4},{5,7},{7,5},{8,10},{10,8},{9,1... | collective-permute-start | bytes 786440 | tf_op jit(solution)/shard_map/ppermute | solution.py:320
  13.2 13.9 %collective-permute-start.6 = (bf16[256,512]{1,0:T(8,128)(2,1)S(1)}, bf16[256,512]{1,0:T(8,128)(2,1)S(1)}, u32[]{:S(2)}, u32[]{:S(2)}) collective-permute-start(bf16[256,512]{1,0:T(8,128)(2,1)S(1)} %copy-done), channel_id=1, source_target_pairs={{0,130},{2,128},{128,2},{130,0},{1,131},{3,129},{129,3},{131,1},{4... | collective-permute-start | bytes 786440 | tf_op jit(solution)/shard_map/ppermute | solution.py:299
  21.7 7.2 %collective-permute-start.3 = (bf16[256,768]{1,0:T(8,128)(2,1)S(1)}, bf16[256,768]{1,0:T(8,128)(2,1)S(1)}, u32[]{:S(2)}, u32[]{:S(2)}) collective-permute-start(bf16[256,768]{1,0:T(8,128)(2,1)S(1)} %collective-permute-done.2.c1), channel_id=1, source_target_pairs={{0,1},{1,0},{2,3},{3,2},{4,5},{5,4},{6,7},{7,6},{8,9},{9,8},{10,11... | collective-permute-start | bytes 1179656 | tf_op jit(solution)/shard_map/ppermute | solution.py:320
  21.7 5.8 %collective-permute-start.1 = (bf16[256,512]{1,0:T(8,128)(2,1)S(1)}, bf16[256,512]{1,0:T(8,128)(2,1)S(1)}, u32[]{:S(2)}, u32[]{:S(2)}) collective-permute-start(bf16[256,512]{1,0:T(8,128)(2,1)S(1)} %copy-done), channel_id=1, source_target_pairs={{0,1},{1,0},{2,3},{3,2},{4,5},{5,4},{6,7},{7,6},{8,9},{9,8},{10,11... | collective-permute-start | bytes 786440 | tf_op jit(solution)/shard_map/ppermute | solution.py:320
  27.0 1.5 %collective-permute-start.5 = (bf16[256,512]{1,0:T(8,128)(2,1)S(1)}, bf16[256,512]{1,0:T(8,128)(2,1)S(1)}, u32[]{:S(2)}, u32[]{:S(2)}) collective-permute-start(bf16[256,512]{1,0:T(8,128)(2,1)S(1)} %collective-permute-done.4.c2), channel_id=1, source_target_pairs={{0,1},{1,0},{2,3},{3,2},{4,5},{5,4},{6,7},{7,6},{8,9},{9,8},{10,11... | collective-permute-start | bytes 786440 | tf_op jit(solution)/shard_map/ppermute | solution.py:320
  27.0 1.9 %collective-permute-start.7 = (bf16[256,512]{1,0:T(8,128)(2,1)S(1)}, bf16[256,512]{1,0:T(8,128)(2,1)S(1)}, u32[]{:S(2)}, u32[]{:S(2)}) collective-permute-start(bf16[256,512]{1,0:T(8,128)(2,1)S(1)} %collective-permute-done.6.c3), channel_id=1, source_target_pairs={{0,1},{1,0},{2,3},{3,2},{4,5},{5,4},{6,7},{7,6},{8,9},{9,8},{10,11... | collective-permute-start | bytes 786440 | tf_op jit(solution)/shard_map/ppermute | solution.py:320
  33.1 18.7 %all-to-all-start.1 = ((bf16[4,1024,128]{2,1,0:T(8,128)(2,1)}), bf16[4,1024,128]{2,1,0:T(8,128)(2,1)S(1)}, u32[]{:S(2)}, u32[]{:S(2)}) async-start(bf16[4,1024,128]{2,1,0:T(8,128)(2,1)} %get-tuple-element.31), calls=%async_computation.1 | async-start | bytes 2097152 | tf_op jit(solution)/shard_map/all_to_all | solution.py:295
  37.9 26.8 %copy-start.5 = (bf16[272,128]{1,0:T(8,128)(2,1)S(1)}, bf16[272,128]{1,0:T(8,128)(2,1)}, u32[]{:S(2)}) copy-start(bf16[272,128]{1,0:T(8,128)(2,1)} %get-tuple-element.35) | copy-start | bytes 208900
  38.8 26.5 %collective-permute-start = (bf16[3,1024,128]{2,1,0:T(8,128)(2,1)}, bf16[3,1024,128]{2,1,0:T(8,128)(2,1)S(1)}, u32[]{:S(2)}, u32[]{:S(2)}) collective-permute-start(bf16[3,1024,128]{2,1,0:T(8,128)(2,1)} %slice.4), channel_id=1, source_target_pairs={{0,16},{16,32},{32,48},{48,64},{64,80},{80,96},{96,112},{112,128},... | collective-permute-start | bytes 2359304 | tf_op jit(solution)/shard_map/ppermute | solution.py:316
  52.7 19.5 %all-to-all-start.2 = ((bf16[8,128,128]{2,1,0:T(8,128)(2,1)}), bf16[8,128,128]{2,1,0:T(8,128)(2,1)S(1)}, u32[]{:S(2)}, u32[]{:S(2)}) async-start(bf16[8,128,128]{2,1,0:T(8,128)(2,1)} %bitcast.15), calls=%async_computation.2 | async-start | bytes 524288 | tf_op jit(solution)/shard_map/all_to_all | solution.py:295
  61.1 7.1 %collective-permute-start.8 = (bf16[272,128]{1,0:T(8,128)(2,1)}, bf16[272,128]{1,0:T(8,128)(2,1)S(1)}, u32[]{:S(2)}, u32[]{:S(2)}) collective-permute-start(bf16[272,128]{1,0:T(8,128)(2,1)} %get-tuple-element.33), channel_id=1, source_target_pairs={{0,4},{4,8},{8,12},{12,0},{1,5},{5,9},{9,13},{13,1},{2,6},{6,10},{... | collective-permute-start | bytes 208904 | tf_op jit(solution)/shard_map/ppermute | solution.py:303
  61.1 7.1 %collective-permute-start.9 = (bf16[272,128]{1,0:T(8,128)(2,1)}, bf16[272,128]{1,0:T(8,128)(2,1)S(1)}, u32[]{:S(2)}, u32[]{:S(2)}) collective-permute-start(bf16[272,128]{1,0:T(8,128)(2,1)} %get-tuple-element.34), channel_id=1, source_target_pairs={{0,8},{4,12},{8,0},{12,4},{1,9},{5,13},{9,1},{13,5},{2,10},{6,14},... | collective-permute-start | bytes 208904 | tf_op jit(solution)/shard_map/ppermute | solution.py:303
  64.7 4.3 %collective-permute-start.10 = (bf16[272,128]{1,0:T(8,128)(2,1)S(1)}, bf16[272,128]{1,0:T(8,128)(2,1)S(1)}, u32[]{:S(2)}, u32[]{:S(2)}) collective-permute-start(bf16[272,128]{1,0:T(8,128)(2,1)S(1)} %copy-done.5), channel_id=1, source_target_pairs={{0,12},{4,0},{8,4},{12,8},{1,13},{5,1},{9,5},{13,9},{2,14},{6,2},{... | collective-permute-start | bytes 208904 | tf_op jit(solution)/shard_map/ppermute | solution.py:303
  68.2 8.7 %copy-start.1 = (bf16[272,128]{1,0:T(8,128)(2,1)}, bf16[272,128]{1,0:T(8,128)(2,1)S(1)}, u32[]{:S(2)}) copy-start(bf16[272,128]{1,0:T(8,128)(2,1)S(1)} %collective-permute-done.8.g1) | copy-start | bytes 208900
  68.3 8.7 %copy-start.2 = (bf16[272,128]{1,0:T(8,128)(2,1)}, bf16[272,128]{1,0:T(8,128)(2,1)S(1)}, u32[]{:S(2)}) copy-start(bf16[272,128]{1,0:T(8,128)(2,1)S(1)} %collective-permute-done.9.g2) | copy-start | bytes 208900
  69.0 8.0 %copy-start.3 = (bf16[272,128]{1,0:T(8,128)(2,1)}, bf16[272,128]{1,0:T(8,128)(2,1)S(1)}, u32[]{:S(2)}) copy-start(bf16[272,128]{1,0:T(8,128)(2,1)S(1)} %collective-permute-done.10.g3) | copy-start | bytes 208900
  72.9 14.5 %all-to-all-start.3 = ((bf16[8,128,128]{2,1,0:T(8,128)(2,1)}), bf16[8,128,128]{2,1,0:T(8,128)(2,1)S(1)}, u32[]{:S(2)}, u32[]{:S(2)}) async-start(bf16[8,128,128]{2,1,0:T(8,128)(2,1)} %shard_map.168), calls=%async_computation.3 | async-start | bytes 524288 | tf_op jit(solution)/shard_map/all_to_all | solution.py:295
  87.4 6.4 %collective-permute-start.18 = (bf16[1024,128]{1,0:T(8,128)(2,1)S(1)}, bf16[1024,128]{1,0:T(8,128)(2,1)S(1)}, u32[]{:S(2)}, u32[]{:S(2)}) collective-permute-start(bf16[1024,128]{1,0:T(8,128)(2,1)S(1)} %bitcast.10), channel_id=1, source_target_pairs={{16,144},{48,176},{80,208},{112,240},{144,16},{176,48},{208,80},{2... | collective-permute-start | bytes 786440 | tf_op jit(solution)/shard_map/ppermute | solution.py:308
  88.1 8.4 %collective-permute-start.17 = (bf16[1024,128]{1,0:T(8,128)(2,1)S(1)}, bf16[1024,128]{1,0:T(8,128)(2,1)S(1)}, u32[]{:S(2)}, u32[]{:S(2)}) collective-permute-start(bf16[1024,128]{1,0:T(8,128)(2,1)S(1)} %bitcast.11), channel_id=1, source_target_pairs={{0,8},{4,12},{8,0},{12,4},{1,9},{5,13},{9,1},{13,5},{2,10},{6,14},... | collective-permute-start | bytes 786440 | tf_op jit(solution)/shard_map/ppermute | solution.py:303
  90.1 10.2 %collective-permute-start.11 = (bf16[3,512,128]{2,1,0:T(8,128)(2,1)}, bf16[3,512,128]{2,1,0:T(8,128)(2,1)S(1)}, u32[]{:S(2)}, u32[]{:S(2)}) collective-permute-start(bf16[3,512,128]{2,1,0:T(8,128)(2,1)} %get-tuple-element.43), channel_id=1, source_target_pairs={{0,16},{16,32},{32,48},{48,64},{64,80},{80,96},{96,112},{112,128},... | collective-permute-start | bytes 1179656 | tf_op jit(solution)/shard_map/ppermute | solution.py:316
  91.8 8.6 %collective-permute-start.12 = (bf16[1024,128]{1,0:T(8,128)(2,1)S(1)}, bf16[1024,128]{1,0:T(8,128)(2,1)S(1)}, u32[]{:S(2)}, u32[]{:S(2)}) collective-permute-start(bf16[1024,128]{1,0:T(8,128)(2,1)S(1)} %bitcast.12), channel_id=1, source_target_pairs={{0,12},{4,0},{8,4},{12,8},{1,13},{5,1},{9,5},{13,9},{2,14},{6,2},{... | collective-permute-start | bytes 786440 | tf_op jit(solution)/shard_map/ppermute | solution.py:303
  93.0 12.9 %collective-permute-start.16 = (bf16[1024,128]{1,0:T(8,128)(2,1)S(1)}, bf16[1024,128]{1,0:T(8,128)(2,1)S(1)}, u32[]{:S(2)}, u32[]{:S(2)}) collective-permute-start(bf16[1024,128]{1,0:T(8,128)(2,1)S(1)} %bitcast.13), channel_id=1, source_target_pairs={{0,4},{4,8},{8,12},{12,0},{1,5},{5,9},{9,13},{13,1},{2,6},{6,10},{... | collective-permute-start | bytes 786440 | tf_op jit(solution)/shard_map/ppermute | solution.py:303
  93.8 13.3 %collective-permute-start.19 = (bf16[1024,128]{1,0:T(8,128)(2,1)S(1)}, bf16[1024,128]{1,0:T(8,128)(2,1)S(1)}, u32[]{:S(2)}, u32[]{:S(2)}) collective-permute-start(bf16[1024,128]{1,0:T(8,128)(2,1)S(1)} %collective-permute-done.18.refs_8_), channel_id=1, source_target_pairs={{16,0},{48,32},{80,64},{112,96},{17,1},{49,33},{81,65},{113,97},{1... | collective-permute-start | bytes 786440 | tf_op jit(solution)/shard_map/ppermute | solution.py:312
  96.5 11.4 %collective-permute-start.21 = (bf16[1024,128]{1,0:T(8,128)(2,1)S(1)}, bf16[1024,128]{1,0:T(8,128)(2,1)S(1)}, u32[]{:S(2)}, u32[]{:S(2)}) collective-permute-start(bf16[1024,128]{1,0:T(8,128)(2,1)S(1)} %collective-permute-done.17.refs_6_), channel_id=1, source_target_pairs={{0,128},{16,144},{32,160},{48,176},{64,192},{80,208},{96,224},{112... | collective-permute-start | bytes 786440 | tf_op jit(solution)/shard_map/ppermute | solution.py:308
  102.9 13.4 %collective-permute-start.13 = (bf16[1040,128]{1,0:T(8,128)(2,1)}, bf16[1040,128]{1,0:T(8,128)(2,1)S(1)}, u32[]{:S(2)}, u32[]{:S(2)}) collective-permute-start(bf16[1040,128]{1,0:T(8,128)(2,1)} %get-tuple-element.48), channel_id=1, source_target_pairs={{0,4},{4,8},{8,12},{12,0},{1,5},{5,9},{9,13},{13,1},{2,6},{6,10},{... | collective-permute-start | bytes 798728 | tf_op jit(solution)/shard_map/ppermute | solution.py:303
  103.3 12.9 %collective-permute-start.14 = (bf16[1040,128]{1,0:T(8,128)(2,1)}, bf16[1040,128]{1,0:T(8,128)(2,1)S(1)}, u32[]{:S(2)}, u32[]{:S(2)}) collective-permute-start(bf16[1040,128]{1,0:T(8,128)(2,1)} %get-tuple-element.49), channel_id=1, source_target_pairs={{0,8},{4,12},{8,0},{12,4},{1,9},{5,13},{9,1},{13,5},{2,10},{6,14},... | collective-permute-start | bytes 798728 | tf_op jit(solution)/shard_map/ppermute | solution.py:303
  105.8 10.4 %collective-permute-start.15 = (bf16[1040,128]{1,0:T(8,128)(2,1)}, bf16[1040,128]{1,0:T(8,128)(2,1)S(1)}, u32[]{:S(2)}, u32[]{:S(2)}) collective-permute-start(bf16[1040,128]{1,0:T(8,128)(2,1)} %get-tuple-element.50), channel_id=1, source_target_pairs={{0,12},{4,0},{8,4},{12,8},{1,13},{5,1},{9,5},{13,9},{2,14},{6,2},{... | collective-permute-start | bytes 798728 | tf_op jit(solution)/shard_map/ppermute | solution.py:303
  107.1 6.4 %collective-permute-start.20 = (bf16[1024,128]{1,0:T(8,128)(2,1)S(1)}, bf16[1024,128]{1,0:T(8,128)(2,1)S(1)}, u32[]{:S(2)}, u32[]{:S(2)}) collective-permute-start(bf16[1024,128]{1,0:T(8,128)(2,1)S(1)} %collective-permute-done.16.refs_5_), channel_id=1, source_target_pairs={{0,128},{16,144},{32,160},{48,176},{64,192},{80,208},{96,224},{112... | collective-permute-start | bytes 786440 | tf_op jit(solution)/shard_map/ppermute | solution.py:308
  107.9 8.3 %collective-permute-start.22 = (bf16[1024,128]{1,0:T(8,128)(2,1)S(1)}, bf16[1024,128]{1,0:T(8,128)(2,1)S(1)}, u32[]{:S(2)}, u32[]{:S(2)}) collective-permute-start(bf16[1024,128]{1,0:T(8,128)(2,1)S(1)} %collective-permute-done.12.refs_7_), channel_id=1, source_target_pairs={{0,128},{16,144},{32,160},{48,176},{64,192},{80,208},{96,224},{112... | collective-permute-start | bytes 786440 | tf_op jit(solution)/shard_map/ppermute | solution.py:308

commit v5 on v4

--- a/solution.py
+++ b/solution.py
@@ -247,7 +247,9 @@
 def last_kernel(place, *refs):
     back, near_parts, far_parts = refs[:4], refs[4:8], refs[8:13]
     attended, log_total, grad_query, grad_keys, grad_values, out = refs[13:19]
-    held, held_attended, held_total, whole, sems = refs[19:]
+    held, held_attended, held_total, whole, own_back, sems = refs[19:]
+    load = pltpu.make_async_copy(back[0], own_back, sems.at[13])
+    load.start()
 
     def part_rows(far, distance, rows):
         if not far:
@@ -262,6 +264,20 @@
         copies.append(pltpu.make_async_copy(source, target, sems.at[len(copies)]))
         copies[-1].start()
 
+    strip = TOK // 4
+    for far in range(2):
+        y = place[2] + far - 2 * place[2] * far
+        for piece in range(4):
+            rows = pl.ds(pl.multiple_of(y * TOK + piece * strip, strip), strip)
+            for distance in range(4):
+                x = lax.rem(place[1] + 4 - distance, 4)
+                for j in range(4):
+                    lanes = pl.ds(pl.multiple_of((x * 4 + j) * HDIM, HDIM), HDIM)
+                    first = j * TOK + piece * strip
+                    whole[rows, lanes] = part_rows(far, distance, slice(first, first + strip))
+            send(whole.at[rows], out.at[rows])
+    load.wait()
+    back = (own_back, *back[1:])
     for i, target in enumerate((grad_keys, grad_values, grad_query)):
         for distance, ref in enumerate(back):
             head = lax.rem(place[1] + 4 - distance, 4)
@@ -275,18 +291,6 @@
         held_total[pl.ds(head, 1), :] = row_of(ref[4 * TOK :, :].astype(f32), 0, 3)
     send(held_attended, attended)
     send(held_total, log_total)
-    strip = TOK // 4
-    for far in range(2):
-        y = place[2] + far - 2 * place[2] * far
-        for piece in range(4):
-            rows = pl.ds(pl.multiple_of(y * TOK + piece * strip, strip), strip)
-            for distance in range(4):
-                x = lax.rem(place[1] + 4 - distance, 4)
-                for j in range(4):
-                    lanes = pl.ds(pl.multiple_of((x * 4 + j) * HDIM, HDIM), HDIM)
-                    first = j * TOK + piece * strip
-                    whole[rows, lanes] = part_rows(far, distance, slice(first, first + strip))
-            send(whole.at[rows], out.at[rows])
     for copy in copies:
         copy.wait()
 
@@ -435,8 +439,10 @@
                 pltpu.VMEM(block, bf16),
                 pltpu.VMEM((4, TOK), f32),
                 pltpu.VMEM((2 * TOK, 16 * HDIM), bf16),
-                pltpu.SemaphoreType.DMA((13,)),
+                pltpu.VMEM((BACK_ROWS, HDIM), bf16),
+                pltpu.SemaphoreType.DMA((14,)),
             ],
+            raw_in=(1,),
             raw_out=True,
         )
     )

time: 120 us -> 120 us (level)
  no operation moved by 1% of the time
where the time goes in v5:
time: 120 us
  starting transfers between devices  49.5 us (41%)
  waiting for transfers between devices  44.6 us (37%)
  Pallas kernels  23.4 us (20%)
    pallas_call x8, Pallas kernels, call(): pl.pallas_call(kernel, out_shape=out_shape, in_specs=[pl.BlockSpec(memory...  23.4 us
    all_to_all x4, starting transfers between devices, across(): return lax.all_to_all(value, axes, 0, 0, tiled=True)  23.2 us
    all_to_all x4, waiting for transfers between devices, across(): return lax.all_to_all(value, axes, 0, 0, tiled=True)  18.6 us
    ppermute x6, waiting for transfers between devices, other(): return lax.ppermute(value, axis, [(0, 1), (1, 0)])  13.6 us
    ppermute x9, starting transfers between devices, along_x(): return lax.ppermute(value, 'x', [(i, (i + distance) % 4) for i in range(4)])  12.4 us
    ppermute x4, waiting for transfers between devices, across_y(): return lax.ppermute(value, ('yl', 'z'), pairs)  7.16 us
    ppermute x6, starting transfers between devices, other(): return lax.ppermute(value, axis, [(0, 1), (1, 0)])  4.52 us
    ppermute x2, starting transfers between devices, next_row(): lax.ppermute(value, ('yl', 'z'), [(i, (i + 1) % 16) for i in range(16)])  3.56 us
  transfers between devices with their start and end apart: 27, of which 12 were waited for; matrix products, arithmetic and copies ran while one was open for 1% of the time, Pallas kernels for 14%

profile of v5, /device:TPU:2, one launch (start us, length us, event | category | flops | bytes accessed | tf_op | source)
XLA Modules:
  0.0 119.5 jit_solution(11426486863660334358)
XLA Ops:
  0.6 0.1 pad_add_fusion.1.place
  0.7 3.0 %shard_map.163 = (bf16[4,1552,128]{2,1,0:T(8,128)(2,1)}, bf16[256,768]{1,0:T(8,128)(2,1)}) custom-call(s32[4]{0:T(128)S(1)} %pad_add_fusion.1.place, bf16[256,512]{1,0:T(8,128)(2,1)} %qf.1, bf16[256,512]{1,0:T(8,128)(2,1)} %kf.1, bf16[256,512]{1,0:T(8,128)(2,1)} %vf.1, bf16[256,512]{1,0:T(8,128)(2,1)} %kb.1, bf16[256,512]{1,0:T(8,128)(2,1)} %vb.1, ...), custom_call_target="tpu_custom_call" | custom-call | tf_op jit(solution)/shard_map/pallas_call | solution.py:73
  3.7 0.0 copy-start.4
  3.7 5.9 %all-to-all-start = ((bf16[4,1552,128]{2,1,0:T(8,128)(2,1)}), bf16[4,1552,128]{2,1,0:T(8,128)(2,1)S(1)}, u32[]{:S(2)}, u32[]{:S(2)}) async-start(bf16[4,1552,128]{2,1,0:T(8,128)(2,1)} %get-tuple-element.29), calls=%async_computation | async-start | bytes 3178496 | tf_op jit(solution)/shard_map/all_to_all | solution.py:299
  9.7 0.6 collective-permute-start.2
  10.3 2.9 %collective-permute-start.4 = (bf16[256,512]{1,0:T(8,128)(2,1)S(1)}, bf16[256,512]{1,0:T(8,128)(2,1)S(1)}, u32[]{:S(2)}, u32[]{:S(2)}) collective-permute-start(bf16[256,512]{1,0:T(8,128)(2,1)S(1)} %copy-done), channel_id=1, source_target_pairs={{0,2},{2,0},{1,3},{3,1},{4,6},{6,4},{5,7},{7,5},{8,10},{10,8},{9,1... | collective-permute-start | bytes 786440 | tf_op jit(solution)/shard_map/ppermute | solution.py:324
  13.2 1.2 %collective-permute-start.6 = (bf16[256,512]{1,0:T(8,128)(2,1)S(1)}, bf16[256,512]{1,0:T(8,128)(2,1)S(1)}, u32[]{:S(2)}, u32[]{:S(2)}) collective-permute-start(bf16[256,512]{1,0:T(8,128)(2,1)S(1)} %copy-done), channel_id=1, source_target_pairs={{0,130},{2,128},{128,2},{130,0},{1,131},{3,129},{129,3},{131,1},{4... | collective-permute-start | bytes 786440 | tf_op jit(solution)/shard_map/ppermute | solution.py:303
  14.4 7.4 %collective-permute-done.2.c1 = bf16[256,768]{1,0:T(8,128)(2,1)S(1)} collective-permute-done((bf16[256,768]{1,0:T(8,128)(2,1)S(1)}, bf16[256,768]{1,0:T(8,128)(2,1)S(1)}, u32[]{:S(2)}, u32[]{:S(2)}) %collective-permute-start.2) | collective-permute-done | bytes 393248 | tf_op jit(solution)/shard_map/ppermute | solution.py:324
  21.7 0.5 collective-permute-start.1
  22.2 4.8 %collective-permute-done.4.c2 = bf16[256,512]{1,0:T(8,128)(2,1)S(1)} collective-permute-done((bf16[256,512]{1,0:T(8,128)(2,1)S(1)}, bf16[256,512]{1,0:T(8,128)(2,1)S(1)}, u32[]{:S(2)}, u32[]{:S(2)}) %collective-permute-start.4) | collective-permute-done | bytes 262176 | tf_op jit(solution)/shard_map/ppermute | solution.py:324
  27.0 0.5 collective-permute-start.7
  27.6 1.0 collective-permute-done.5.o2
  28.6 0.4 collective-permute-done.7.o3
  29.0 4.2 %shard_map.164 = (bf16[272,128]{1,0:T(8,128)(2,1)}, bf16[272,128]{1,0:T(8,128)(2,1)}, bf16[272,128]{1,0:T(8,128)(2,1)}, bf16[272,128]{1,0:T(8,128)(2,1)}, bf16[4,1024,128]{2,1,0:T(8,128)(2,1)}) custom-call(s32[4]{0:T(128)S(1)} %pad_add_fusion.1.place, bf16[256,512]{1,0:T(8,128)(2,1)} %c0.1, bf16[256,512]{1,0:T(8,128)(2,1)S(1)} %collective-permute-done.1.o0, ...), custom_call_target="tpu_custom_call" | custom-call | tf_op jit(solution)/shard_map/pallas_call | solution.py:73
  33.1 4.8 %all-to-all-start.1 = ((bf16[4,1024,128]{2,1,0:T(8,128)(2,1)}), bf16[4,1024,128]{2,1,0:T(8,128)(2,1)S(1)}, u32[]{:S(2)}, u32[]{:S(2)}) async-start(bf16[4,1024,128]{2,1,0:T(8,128)(2,1)} %get-tuple-element.31), calls=%async_computation.1 | async-start | bytes 2097152 | tf_op jit(solution)/shard_map/all_to_all | solution.py:299
  37.9 0.9 slice.4
  38.8 1.9 %collective-permute-start = (bf16[3,1024,128]{2,1,0:T(8,128)(2,1)}, bf16[3,1024,128]{2,1,0:T(8,128)(2,1)S(1)}, u32[]{:S(2)}, u32[]{:S(2)}) collective-permute-start(bf16[3,1024,128]{2,1,0:T(8,128)(2,1)} %slice.4), channel_id=1, source_target_pairs={{0,16},{16,32},{32,48},{48,64},{64,80},{80,96},{96,112},{112,128},... | collective-permute-start | bytes 2359304 | tf_op jit(solution)/shard_map/ppermute | solution.py:320
  40.7 11.1 %all-to-all-done.1.parts = bf16[4,1024,128]{2,1,0:T(8,128)(2,1)S(1)} async-done(((bf16[4,1024,128]{2,1,0:T(8,128)(2,1)}), bf16[4,1024,128]{2,1,0:T(8,128)(2,1)S(1)}, u32[]{:S(2)}, u32[]{:S(2)}) %all-to-all-start.1) | async-done | bytes 1048608 | tf_op jit(solution)/shard_map/all_to_all | solution.py:299
  51.8 0.8 shard_map.165
  52.7 8.5 %all-to-all-start.2 = ((bf16[8,128,128]{2,1,0:T(8,128)(2,1)}), bf16[8,128,128]{2,1,0:T(8,128)(2,1)S(1)}, u32[]{:S(2)}, u32[]{:S(2)}) async-start(bf16[8,128,128]{2,1,0:T(8,128)(2,1)} %bitcast.15), calls=%async_computation.2 | async-start | bytes 524288 | tf_op jit(solution)/shard_map/all_to_all | solution.py:299
  61.1 3.5 %collective-permute-start.9 = (bf16[272,128]{1,0:T(8,128)(2,1)}, bf16[272,128]{1,0:T(8,128)(2,1)S(1)}, u32[]{:S(2)}, u32[]{:S(2)}) collective-permute-start(bf16[272,128]{1,0:T(8,128)(2,1)} %get-tuple-element.34), channel_id=1, source_target_pairs={{0,8},{4,12},{8,0},{12,4},{1,9},{5,13},{9,1},{13,5},{2,10},{6,14},... | collective-permute-start | bytes 208904 | tf_op jit(solution)/shard_map/ppermute | solution.py:307
  64.7 0.6 collective-permute-start.10
  65.2 0.1 pad_add_fusion.place
  65.3 2.9 %shard_map.166.forward_out = bf16[4,272,128]{2,1,0:T(8,128)(2,1)S(1)} custom-call(s32[4]{0:T(128)S(1)} %pad_add_fusion.place, bf16[4,1552,128]{2,1,0:T(8,128)(2,1)S(1)} %all-to-all-done.own, bf16[3,1024,128]{2,1,0:T(8,128)(2,1)S(1)} %collective-permute-done.halo), custom_call_target="tpu_custom_call" | custom-call | tf_op jit(solution)/shard_map/pallas_call | solution.py:73
  68.3 0.7 collective-permute-done.10.g3
  69.0 3.2 %all-to-all-done.2.parts = bf16[8,128,128]{2,1,0:T(8,128)(2,1)S(1)} async-done(((bf16[8,128,128]{2,1,0:T(8,128)(2,1)}), bf16[8,128,128]{2,1,0:T(8,128)(2,1)S(1)}, u32[]{:S(2)}, u32[]{:S(2)}) %all-to-all-start.2) | async-done | bytes 262176 | tf_op jit(solution)/shard_map/all_to_all | solution.py:299
  72.2 0.7 shard_map.168
  72.9 4.0 %all-to-all-start.3 = ((bf16[8,128,128]{2,1,0:T(8,128)(2,1)}), bf16[8,128,128]{2,1,0:T(8,128)(2,1)S(1)}, u32[]{:S(2)}, u32[]{:S(2)}) async-start(bf16[8,128,128]{2,1,0:T(8,128)(2,1)} %shard_map.168), calls=%async_computation.3 | async-start | bytes 524288 | tf_op jit(solution)/shard_map/all_to_all | solution.py:299
  77.0 6.1 %shard_map.167 = (bf16[4,528,128]{2,1,0:T(8,128)(2,1)}, f32[4,512,128]{2,1,0:T(8,128)}, bf16[3,512,128]{2,1,0:T(8,128)(2,1)}) custom-call(s32[4]{0:T(128)S(1)} %pad_add_fusion.place, bf16[4,1552,128]{2,1,0:T(8,128)(2,1)S(1)} %all-to-all-done.own, bf16[3,1024,128]{2,1,0:T(8,128)(2,1)S(1)} %collective-permute-done.halo, ...), custom_call_target="tpu_custom_call" | custom-call | tf_op jit(solution)/shard_map/pallas_call | solution.py:73
  83.1 4.3 %all-to-all-done.3 = bf16[8,128,128]{2,1,0:T(8,128)(2,1)S(1)} async-done(((bf16[8,128,128]{2,1,0:T(8,128)(2,1)}), bf16[8,128,128]{2,1,0:T(8,128)(2,1)S(1)}, u32[]{:S(2)}, u32[]{:S(2)}) %all-to-all-start.3) | async-done | bytes 262176 | tf_op jit(solution)/shard_map/all_to_all | solution.py:299
  87.4 0.7 collective-permute-start.18
  88.1 2.0 %collective-permute-start.17 = (bf16[1024,128]{1,0:T(8,128)(2,1)S(1)}, bf16[1024,128]{1,0:T(8,128)(2,1)S(1)}, u32[]{:S(2)}, u32[]{:S(2)}) collective-permute-start(bf16[1024,128]{1,0:T(8,128)(2,1)S(1)} %bitcast.11), channel_id=1, source_target_pairs={{0,8},{4,12},{8,0},{12,4},{1,9},{5,13},{9,1},{13,5},{2,10},{6,14},... | collective-permute-start | bytes 786440 | tf_op jit(solution)/shard_map/ppermute | solution.py:307
  90.1 1.6 %collective-permute-start.11 = (bf16[3,512,128]{2,1,0:T(8,128)(2,1)}, bf16[3,512,128]{2,1,0:T(8,128)(2,1)S(1)}, u32[]{:S(2)}, u32[]{:S(2)}) collective-permute-start(bf16[3,512,128]{2,1,0:T(8,128)(2,1)} %get-tuple-element.43), channel_id=1, source_target_pairs={{0,16},{16,32},{32,48},{48,64},{64,80},{80,96},{96,112},{112,128},... | collective-permute-start | bytes 1179656 | tf_op jit(solution)/shard_map/ppermute | solution.py:320
  91.8 1.2 collective-permute-start.12
  93.0 0.8 collective-permute-start.16
  93.8 1.3 %collective-permute-start.19 = (bf16[1024,128]{1,0:T(8,128)(2,1)S(1)}, bf16[1024,128]{1,0:T(8,128)(2,1)S(1)}, u32[]{:S(2)}, u32[]{:S(2)}) collective-permute-start(bf16[1024,128]{1,0:T(8,128)(2,1)S(1)} %collective-permute-done.18.refs_8_), channel_id=1, source_target_pairs={{16,0},{48,32},{80,64},{112,96},{17,1},{49,33},{81,65},{113,97},{1... | collective-permute-start | bytes 786440 | tf_op jit(solution)/shard_map/ppermute | solution.py:316
  95.1 1.4 %collective-permute-done.17.refs_6_ = bf16[1024,128]{1,0:T(8,128)(2,1)S(1)} collective-permute-done((bf16[1024,128]{1,0:T(8,128)(2,1)S(1)}, bf16[1024,128]{1,0:T(8,128)(2,1)S(1)}, u32[]{:S(2)}, u32[]{:S(2)}) %collective-permute-start.17) | collective-permute-done | bytes 262176 | tf_op jit(solution)/shard_map/ppermute | solution.py:307
  96.5 0.7 collective-permute-start.21
  97.2 3.1 %collective-permute-done.11.behind = bf16[3,512,128]{2,1,0:T(8,128)(2,1)S(1)} collective-permute-done((bf16[3,512,128]{2,1,0:T(8,128)(2,1)}, bf16[3,512,128]{2,1,0:T(8,128)(2,1)S(1)}, u32[]{:S(2)}, u32[]{:S(2)}) %collective-permute-start.11) | collective-permute-done | bytes 393248 | tf_op jit(solution)/shard_map/ppermute | solution.py:320
  100.3 2.5 %shard_map.169 = (bf16[1040,128]{1,0:T(8,128)(2,1)}, bf16[1040,128]{1,0:T(8,128)(2,1)}, bf16[1040,128]{1,0:T(8,128)(2,1)}, bf16[1040,128]{1,0:T(8,128)(2,1)}) custom-call(s32[4]{0:T(128)S(1)} %pad_add_fusion.place, bf16[4,528,128]{2,1,0:T(8,128)(2,1)} %get-tuple-element.41.rest, f32[4,512,128]{2,1,0:T(8,128)} %get-tuple-element.42.grad_kv, ...), custom_call_target="tpu_custom_call" | custom-call | tf_op jit(solution)/shard_map/pallas_call | solution.py:73
  102.9 0.5 collective-permute-start.13
  103.3 2.5 %collective-permute-start.14 = (bf16[1040,128]{1,0:T(8,128)(2,1)}, bf16[1040,128]{1,0:T(8,128)(2,1)S(1)}, u32[]{:S(2)}, u32[]{:S(2)}) collective-permute-start(bf16[1040,128]{1,0:T(8,128)(2,1)} %get-tuple-element.49), channel_id=1, source_target_pairs={{0,8},{4,12},{8,0},{12,4},{1,9},{5,13},{9,1},{13,5},{2,10},{6,14},... | collective-permute-start | bytes 798728 | tf_op jit(solution)/shard_map/ppermute | solution.py:307
  105.8 1.2 %collective-permute-start.15 = (bf16[1040,128]{1,0:T(8,128)(2,1)}, bf16[1040,128]{1,0:T(8,128)(2,1)S(1)}, u32[]{:S(2)}, u32[]{:S(2)}) collective-permute-start(bf16[1040,128]{1,0:T(8,128)(2,1)} %get-tuple-element.50), channel_id=1, source_target_pairs={{0,12},{4,0},{8,4},{12,8},{1,13},{5,1},{9,5},{13,9},{2,14},{6,2},{... | collective-permute-start | bytes 798728 | tf_op jit(solution)/shard_map/ppermute | solution.py:307
  107.1 0.8 collective-permute-start.20
  107.9 1.2 collective-permute-start.22
  109.1 4.3 %collective-permute-done.20.refs_10_ = bf16[1024,128]{1,0:T(8,128)(2,1)S(1)} collective-permute-done((bf16[1024,128]{1,0:T(8,128)(2,1)S(1)}, bf16[1024,128]{1,0:T(8,128)(2,1)S(1)}, u32[]{:S(2)}, u32[]{:S(2)}) %collective-permute-start.20) | collective-permute-done | bytes 262176 | tf_op jit(solution)/shard_map/ppermute | solution.py:312
  113.4 2.8 %collective-permute-done.22.refs_12_ = bf16[1024,128]{1,0:T(8,128)(2,1)S(1)} collective-permute-done((bf16[1024,128]{1,0:T(8,128)(2,1)S(1)}, bf16[1024,128]{1,0:T(8,128)(2,1)S(1)}, u32[]{:S(2)}, u32[]{:S(2)}) %collective-permute-start.22) | collective-permute-done | bytes 262176 | tf_op jit(solution)/shard_map/ppermute | solution.py:312
  116.3 3.1 %shard_map.170 = (bf16[256,512]{1,0:T(8,128)(2,1)}, f32[4,256]{1,0:T(4,128)}, f32[256,512]{1,0:T(8,128)}, f32[256,512]{1,0:T(8,128)}, f32[256,512]{1,0:T(8,128)}, /*index=5*/bf16[512,2048]{1,0:T(8,128)(2,1)}) custom-call(s32[4]{0:T(128)S(1)} %pad_add_fusion.place, bf16[1040,128]{1,0:T(8,128)(2,1)} %get-tuple-element.47.refs_0_, ...), custom_call_target="tpu_custom_call" | custom-call | tf_op jit(solution)/shard_map/pallas_call | solution.py:73
  (29 shorter events, 0.1 us)
Async XLA Ops:
  3.7 6.0 %copy-start.4 = (bf16[256,768]{1,0:T(8,128)(2,1)S(1)}, bf16[256,768]{1,0:T(8,128)(2,1)}, u32[]{:S(2)}) copy-start(bf16[256,768]{1,0:T(8,128)(2,1)} %get-tuple-element.30) | copy-start | bytes 1179652
  3.7 6.6 %copy-start = (bf16[256,512]{1,0:T(8,128)(2,1)S(1)}, bf16[256,512]{1,0:T(8,128)(2,1)}, u32[]{:S(2)}) copy-start(bf16[256,512]{1,0:T(8,128)(2,1)} %c0.1) | copy-start | bytes 786436
  3.7 29.4 %all-to-all-start = ((bf16[4,1552,128]{2,1,0:T(8,128)(2,1)}), bf16[4,1552,128]{2,1,0:T(8,128)(2,1)S(1)}, u32[]{:S(2)}, u32[]{:S(2)}) async-start(bf16[4,1552,128]{2,1,0:T(8,128)(2,1)} %get-tuple-element.29), calls=%async_computation | async-start | bytes 3178496 | tf_op jit(solution)/shard_map/all_to_all | solution.py:299
  9.7 12.1 %collective-permute-start.2 = (bf16[256,768]{1,0:T(8,128)(2,1)S(1)}, bf16[256,768]{1,0:T(8,128)(2,1)S(1)}, u32[]{:S(2)}, u32[]{:S(2)}) collective-permute-start(bf16[256,768]{1,0:T(8,128)(2,1)S(1)} %copy-done.4), channel_id=1, source_target_pairs={{0,128},{128,0},{1,129},{129,1},{2,130},{130,2},{3,131},{131,3},{4... | collective-permute-start | bytes 1179656 | tf_op jit(solution)/shard_map/ppermute | solution.py:324
  10.3 16.8 %collective-permute-start.4 = (bf16[256,512]{1,0:T(8,128)(2,1)S(1)}, bf16[256,512]{1,0:T(8,128)(2,1)S(1)}, u32[]{:S(2)}, u32[]{:S(2)}) collective-permute-start(bf16[256,512]{1,0:T(8,128)(2,1)S(1)} %copy-done), channel_id=1, source_target_pairs={{0,2},{2,0},{1,3},{3,1},{4,6},{6,4},{5,7},{7,5},{8,10},{10,8},{9,1... | collective-permute-start | bytes 786440 | tf_op jit(solution)/shard_map/ppermute | solution.py:324
  13.2 13.9 %collective-permute-start.6 = (bf16[256,512]{1,0:T(8,128)(2,1)S(1)}, bf16[256,512]{1,0:T(8,128)(2,1)S(1)}, u32[]{:S(2)}, u32[]{:S(2)}) collective-permute-start(bf16[256,512]{1,0:T(8,128)(2,1)S(1)} %copy-done), channel_id=1, source_target_pairs={{0,130},{2,128},{128,2},{130,0},{1,131},{3,129},{129,3},{131,1},{4... | collective-permute-start | bytes 786440 | tf_op jit(solution)/shard_map/ppermute | solution.py:303
  21.7 7.2 %collective-permute-start.3 = (bf16[256,768]{1,0:T(8,128)(2,1)S(1)}, bf16[256,768]{1,0:T(8,128)(2,1)S(1)}, u32[]{:S(2)}, u32[]{:S(2)}) collective-permute-start(bf16[256,768]{1,0:T(8,128)(2,1)S(1)} %collective-permute-done.2.c1), channel_id=1, source_target_pairs={{0,1},{1,0},{2,3},{3,2},{4,5},{5,4},{6,7},{7,6},{8,9},{9,8},{10,11... | collective-permute-start | bytes 1179656 | tf_op jit(solution)/shard_map/ppermute | solution.py:324
  21.7 5.8 %collective-permute-start.1 = (bf16[256,512]{1,0:T(8,128)(2,1)S(1)}, bf16[256,512]{1,0:T(8,128)(2,1)S(1)}, u32[]{:S(2)}, u32[]{:S(2)}) collective-permute-start(bf16[256,512]{1,0:T(8,128)(2,1)S(1)} %copy-done), channel_id=1, source_target_pairs={{0,1},{1,0},{2,3},{3,2},{4,5},{5,4},{6,7},{7,6},{8,9},{9,8},{10,11... | collective-permute-start | bytes 786440 | tf_op jit(solution)/shard_map/ppermute | solution.py:324
  27.0 1.5 %collective-permute-start.5 = (bf16[256,512]{1,0:T(8,128)(2,1)S(1)}, bf16[256,512]{1,0:T(8,128)(2,1)S(1)}, u32[]{:S(2)}, u32[]{:S(2)}) collective-permute-start(bf16[256,512]{1,0:T(8,128)(2,1)S(1)} %collective-permute-done.4.c2), channel_id=1, source_target_pairs={{0,1},{1,0},{2,3},{3,2},{4,5},{5,4},{6,7},{7,6},{8,9},{9,8},{10,11... | collective-permute-start | bytes 786440 | tf_op jit(solution)/shard_map/ppermute | solution.py:324
  27.0 1.9 %collective-permute-start.7 = (bf16[256,512]{1,0:T(8,128)(2,1)S(1)}, bf16[256,512]{1,0:T(8,128)(2,1)S(1)}, u32[]{:S(2)}, u32[]{:S(2)}) collective-permute-start(bf16[256,512]{1,0:T(8,128)(2,1)S(1)} %collective-permute-done.6.c3), channel_id=1, source_target_pairs={{0,1},{1,0},{2,3},{3,2},{4,5},{5,4},{6,7},{7,6},{8,9},{9,8},{10,11... | collective-permute-start | bytes 786440 | tf_op jit(solution)/shard_map/ppermute | solution.py:324
  33.1 18.7 %all-to-all-start.1 = ((bf16[4,1024,128]{2,1,0:T(8,128)(2,1)}), bf16[4,1024,128]{2,1,0:T(8,128)(2,1)S(1)}, u32[]{:S(2)}, u32[]{:S(2)}) async-start(bf16[4,1024,128]{2,1,0:T(8,128)(2,1)} %get-tuple-element.31), calls=%async_computation.1 | async-start | bytes 2097152 | tf_op jit(solution)/shard_map/all_to_all | solution.py:299
  37.9 26.8 %copy-start.5 = (bf16[272,128]{1,0:T(8,128)(2,1)S(1)}, bf16[272,128]{1,0:T(8,128)(2,1)}, u32[]{:S(2)}) copy-start(bf16[272,128]{1,0:T(8,128)(2,1)} %get-tuple-element.35) | copy-start | bytes 208900
  38.8 26.5 %collective-permute-start = (bf16[3,1024,128]{2,1,0:T(8,128)(2,1)}, bf16[3,1024,128]{2,1,0:T(8,128)(2,1)S(1)}, u32[]{:S(2)}, u32[]{:S(2)}) collective-permute-start(bf16[3,1024,128]{2,1,0:T(8,128)(2,1)} %slice.4), channel_id=1, source_target_pairs={{0,16},{16,32},{32,48},{48,64},{64,80},{80,96},{96,112},{112,128},... | collective-permute-start | bytes 2359304 | tf_op jit(solution)/shard_map/ppermute | solution.py:320
  52.7 19.5 %all-to-all-start.2 = ((bf16[8,128,128]{2,1,0:T(8,128)(2,1)}), bf16[8,128,128]{2,1,0:T(8,128)(2,1)S(1)}, u32[]{:S(2)}, u32[]{:S(2)}) async-start(bf16[8,128,128]{2,1,0:T(8,128)(2,1)} %bitcast.15), calls=%async_computation.2 | async-start | bytes 524288 | tf_op jit(solution)/shard_map/all_to_all | solution.py:299
  61.1 7.1 %collective-permute-start.8 = (bf16[272,128]{1,0:T(8,128)(2,1)}, bf16[272,128]{1,0:T(8,128)(2,1)S(1)}, u32[]{:S(2)}, u32[]{:S(2)}) collective-permute-start(bf16[272,128]{1,0:T(8,128)(2,1)} %get-tuple-element.33), channel_id=1, source_target_pairs={{0,4},{4,8},{8,12},{12,0},{1,5},{5,9},{9,13},{13,1},{2,6},{6,10},{... | collective-permute-start | bytes 208904 | tf_op jit(solution)/shard_map/ppermute | solution.py:307
  61.1 7.1 %collective-permute-start.9 = (bf16[272,128]{1,0:T(8,128)(2,1)}, bf16[272,128]{1,0:T(8,128)(2,1)S(1)}, u32[]{:S(2)}, u32[]{:S(2)}) collective-permute-start(bf16[272,128]{1,0:T(8,128)(2,1)} %get-tuple-element.34), channel_id=1, source_target_pairs={{0,8},{4,12},{8,0},{12,4},{1,9},{5,13},{9,1},{13,5},{2,10},{6,14},... | collective-permute-start | bytes 208904 | tf_op jit(solution)/shard_map/ppermute | solution.py:307
  64.7 4.3 %collective-permute-start.10 = (bf16[272,128]{1,0:T(8,128)(2,1)S(1)}, bf16[272,128]{1,0:T(8,128)(2,1)S(1)}, u32[]{:S(2)}, u32[]{:S(2)}) collective-permute-start(bf16[272,128]{1,0:T(8,128)(2,1)S(1)} %copy-done.5), channel_id=1, source_target_pairs={{0,12},{4,0},{8,4},{12,8},{1,13},{5,1},{9,5},{13,9},{2,14},{6,2},{... | collective-permute-start | bytes 208904 | tf_op jit(solution)/shard_map/ppermute | solution.py:307
  68.2 8.7 %copy-start.1 = (bf16[272,128]{1,0:T(8,128)(2,1)}, bf16[272,128]{1,0:T(8,128)(2,1)S(1)}, u32[]{:S(2)}) copy-start(bf16[272,128]{1,0:T(8,128)(2,1)S(1)} %collective-permute-done.8.g1) | copy-start | bytes 208900
  68.3 8.7 %copy-start.2 = (bf16[272,128]{1,0:T(8,128)(2,1)}, bf16[272,128]{1,0:T(8,128)(2,1)S(1)}, u32[]{:S(2)}) copy-start(bf16[272,128]{1,0:T(8,128)(2,1)S(1)} %collective-permute-done.9.g2) | copy-start | bytes 208900
  69.0 8.0 %copy-start.3 = (bf16[272,128]{1,0:T(8,128)(2,1)}, bf16[272,128]{1,0:T(8,128)(2,1)S(1)}, u32[]{:S(2)}) copy-start(bf16[272,128]{1,0:T(8,128)(2,1)S(1)} %collective-permute-done.10.g3) | copy-start | bytes 208900
  72.9 14.5 %all-to-all-start.3 = ((bf16[8,128,128]{2,1,0:T(8,128)(2,1)}), bf16[8,128,128]{2,1,0:T(8,128)(2,1)S(1)}, u32[]{:S(2)}, u32[]{:S(2)}) async-start(bf16[8,128,128]{2,1,0:T(8,128)(2,1)} %shard_map.168), calls=%async_computation.3 | async-start | bytes 524288 | tf_op jit(solution)/shard_map/all_to_all | solution.py:299
  87.4 6.4 %collective-permute-start.18 = (bf16[1024,128]{1,0:T(8,128)(2,1)S(1)}, bf16[1024,128]{1,0:T(8,128)(2,1)S(1)}, u32[]{:S(2)}, u32[]{:S(2)}) collective-permute-start(bf16[1024,128]{1,0:T(8,128)(2,1)S(1)} %bitcast.10), channel_id=1, source_target_pairs={{16,144},{48,176},{80,208},{112,240},{144,16},{176,48},{208,80},{2... | collective-permute-start | bytes 786440 | tf_op jit(solution)/shard_map/ppermute | solution.py:312
  88.1 8.4 %collective-permute-start.17 = (bf16[1024,128]{1,0:T(8,128)(2,1)S(1)}, bf16[1024,128]{1,0:T(8,128)(2,1)S(1)}, u32[]{:S(2)}, u32[]{:S(2)}) collective-permute-start(bf16[1024,128]{1,0:T(8,128)(2,1)S(1)} %bitcast.11), channel_id=1, source_target_pairs={{0,8},{4,12},{8,0},{12,4},{1,9},{5,13},{9,1},{13,5},{2,10},{6,14},... | collective-permute-start | bytes 786440 | tf_op jit(solution)/shard_map/ppermute | solution.py:307
  90.1 10.2 %collective-permute-start.11 = (bf16[3,512,128]{2,1,0:T(8,128)(2,1)}, bf16[3,512,128]{2,1,0:T(8,128)(2,1)S(1)}, u32[]{:S(2)}, u32[]{:S(2)}) collective-permute-start(bf16[3,512,128]{2,1,0:T(8,128)(2,1)} %get-tuple-element.43), channel_id=1, source_target_pairs={{0,16},{16,32},{32,48},{48,64},{64,80},{80,96},{96,112},{112,128},... | collective-permute-start | bytes 1179656 | tf_op jit(solution)/shard_map/ppermute | solution.py:320
  91.8 8.6 %collective-permute-start.12 = (bf16[1024,128]{1,0:T(8,128)(2,1)S(1)}, bf16[1024,128]{1,0:T(8,128)(2,1)S(1)}, u32[]{:S(2)}, u32[]{:S(2)}) collective-permute-start(bf16[1024,128]{1,0:T(8,128)(2,1)S(1)} %bitcast.12), channel_id=1, source_target_pairs={{0,12},{4,0},{8,4},{12,8},{1,13},{5,1},{9,5},{13,9},{2,14},{6,2},{... | collective-permute-start | bytes 786440 | tf_op jit(solution)/shard_map/ppermute | solution.py:307
  93.0 12.9 %collective-permute-start.16 = (bf16[1024,128]{1,0:T(8,128)(2,1)S(1)}, bf16[1024,128]{1,0:T(8,128)(2,1)S(1)}, u32[]{:S(2)}, u32[]{:S(2)}) collective-permute-start(bf16[1024,128]{1,0:T(8,128)(2,1)S(1)} %bitcast.13), channel_id=1, source_target_pairs={{0,4},{4,8},{8,12},{12,0},{1,5},{5,9},{9,13},{13,1},{2,6},{6,10},{... | collective-permute-start | bytes 786440 | tf_op jit(solution)/shard_map/ppermute | solution.py:307
  93.8 13.3 %collective-permute-start.19 = (bf16[1024,128]{1,0:T(8,128)(2,1)S(1)}, bf16[1024,128]{1,0:T(8,128)(2,1)S(1)}, u32[]{:S(2)}, u32[]{:S(2)}) collective-permute-start(bf16[1024,128]{1,0:T(8,128)(2,1)S(1)} %collective-permute-done.18.refs_8_), channel_id=1, source_target_pairs={{16,0},{48,32},{80,64},{112,96},{17,1},{49,33},{81,65},{113,97},{1... | collective-permute-start | bytes 786440 | tf_op jit(solution)/shard_map/ppermute | solution.py:316
  96.5 11.4 %collective-permute-start.21 = (bf16[1024,128]{1,0:T(8,128)(2,1)S(1)}, bf16[1024,128]{1,0:T(8,128)(2,1)S(1)}, u32[]{:S(2)}, u32[]{:S(2)}) collective-permute-start(bf16[1024,128]{1,0:T(8,128)(2,1)S(1)} %collective-permute-done.17.refs_6_), channel_id=1, source_target_pairs={{0,128},{16,144},{32,160},{48,176},{64,192},{80,208},{96,224},{112... | collective-permute-start | bytes 786440 | tf_op jit(solution)/shard_map/ppermute | solution.py:312
  102.9 13.4 %collective-permute-start.13 = (bf16[1040,128]{1,0:T(8,128)(2,1)}, bf16[1040,128]{1,0:T(8,128)(2,1)S(1)}, u32[]{:S(2)}, u32[]{:S(2)}) collective-permute-start(bf16[1040,128]{1,0:T(8,128)(2,1)} %get-tuple-element.48), channel_id=1, source_target_pairs={{0,4},{4,8},{8,12},{12,0},{1,5},{5,9},{9,13},{13,1},{2,6},{6,10},{... | collective-permute-start | bytes 798728 | tf_op jit(solution)/shard_map/ppermute | solution.py:307
  103.3 12.9 %collective-permute-start.14 = (bf16[1040,128]{1,0:T(8,128)(2,1)}, bf16[1040,128]{1,0:T(8,128)(2,1)S(1)}, u32[]{:S(2)}, u32[]{:S(2)}) collective-permute-start(bf16[1040,128]{1,0:T(8,128)(2,1)} %get-tuple-element.49), channel_id=1, source_target_pairs={{0,8},{4,12},{8,0},{12,4},{1,9},{5,13},{9,1},{13,5},{2,10},{6,14},... | collective-permute-start | bytes 798728 | tf_op jit(solution)/shard_map/ppermute | solution.py:307
  105.8 10.4 %collective-permute-start.15 = (bf16[1040,128]{1,0:T(8,128)(2,1)}, bf16[1040,128]{1,0:T(8,128)(2,1)S(1)}, u32[]{:S(2)}, u32[]{:S(2)}) collective-permute-start(bf16[1040,128]{1,0:T(8,128)(2,1)} %get-tuple-element.50), channel_id=1, source_target_pairs={{0,12},{4,0},{8,4},{12,8},{1,13},{5,1},{9,5},{13,9},{2,14},{6,2},{... | collective-permute-start | bytes 798728 | tf_op jit(solution)/shard_map/ppermute | solution.py:307
  107.1 6.4 %collective-permute-start.20 = (bf16[1024,128]{1,0:T(8,128)(2,1)S(1)}, bf16[1024,128]{1,0:T(8,128)(2,1)S(1)}, u32[]{:S(2)}, u32[]{:S(2)}) collective-permute-start(bf16[1024,128]{1,0:T(8,128)(2,1)S(1)} %collective-permute-done.16.refs_5_), channel_id=1, source_target_pairs={{0,128},{16,144},{32,160},{48,176},{64,192},{80,208},{96,224},{112... | collective-permute-start | bytes 786440 | tf_op jit(solution)/shard_map/ppermute | solution.py:312
  107.9 8.3 %collective-permute-start.22 = (bf16[1024,128]{1,0:T(8,128)(2,1)S(1)}, bf16[1024,128]{1,0:T(8,128)(2,1)S(1)}, u32[]{:S(2)}, u32[]{:S(2)}) collective-permute-start(bf16[1024,128]{1,0:T(8,128)(2,1)S(1)} %collective-permute-done.12.refs_7_), channel_id=1, source_target_pairs={{0,128},{16,144},{32,160},{48,176},{64,192},{80,208},{96,224},{112... | collective-permute-start | bytes 786440 | tf_op jit(solution)/shard_map/ppermute | solution.py:312
